TPU v7x, 32 devices: a whole 2x2x4 slice. The times are simulated.
32 devices in a mesh: dp: 4 (over y, core), ctx: 4 (over z), tp: 2 (over x).
Axes of the slice: x: 2, y: 2, z: 4, core: 2. Of those that a mesh axis runs over, the one named last changes fastest.
Arguments:
- tokens: bfloat16 [8, 1536, 2048], P('dp', ('ctx', 'tp')), may hold values from -6 to 6
- cotangent: bfloat16 [8, 1536, 2048], P('dp', ('ctx', 'tp')), may hold values from -6 to 6
- lengths: int32 [8, 3], P('dp'), may hold values from 129 to 1024, as said below
- head_counts: int32 [2], replicated, may hold values from 8 to 12, as said below
- norm1_gain: float32 [2048], replicated, may hold values from 0.25 to 1.75
- norm2_gain: float32 [2048], replicated, may hold values from 0.25 to 1.75
- q_gain: float32 [64], replicated, may hold values from 0.25 to 1.75
- k_gain: float32 [64], replicated, may hold values from 0.25 to 1.75
- w_query: bfloat16 [2048, 1536], P(('dp', 'ctx'), 'tp'), may hold values from -0.125 to 0.125
- w_key: bfloat16 [2048, 320], replicated, may hold values from -0.125 to 0.125
- w_value: bfloat16 [2048, 320], replicated, may hold values from -0.125 to 0.125
- w_out: bfloat16 [1536, 2048], P('tp', ('dp', 'ctx')), may hold values from -1.25 to 1.25
- w_gate: bfloat16 [2048, 8192], P(('dp', 'ctx'), 'tp'), may hold values from -0.125 to 0.125
- w_up: bfloat16 [2048, 8192], P(('dp', 'ctx'), 'tp'), may hold values from -0.125 to 0.125
- w_down: bfloat16 [8192, 2048], P('tp', ('dp', 'ctx')), may hold values from -0.0625 to 0.0625
Outputs:
- output: bfloat16 [8, 1536, 2048], P('dp', ('ctx', 'tp'))
- d_input: float32 [8, 1536, 2048], P('dp', ('ctx', 'tp'))
- d_norm1: float32 [2048], replicated
- d_norm2: float32 [2048], replicated
- d_qgain: float32 [64], replicated
- d_kgain: float32 [64], replicated
- d_query: float32 [2048, 1536], P(('dp', 'ctx'), 'tp')
- d_key: float32 [2048, 320], replicated
- d_value: float32 [2048, 320], replicated
- d_out: float32 [1536, 2048], P('tp', ('dp', 'ctx'))
- d_gate: float32 [2048, 8192], P(('dp', 'ctx'), 'tp')
- d_up: float32 [2048, 8192], P(('dp', 'ctx'), 'tp')
- d_down: float32 [8192, 2048], P('tp', ('dp', 'ctx'))
Inputs may be any that keep to these rules, and one draw needn't show every extreme that they name: `lengths`: each packed row of 1536 tokens holds three documents: the middle one has 1024 tokens, starts before token 384 and ends after token 1152; the first and the last sum to 512. The counts sum to 20; index t of tp holds the query heads offset_t to offset_t + head_counts[t] - 1, offset_t being the sum over lower indices; some index holds 12.
All inputs are finite; a program needn't handle non-finite values.
Results may differ from a plain program's by a relative error of at most 0.019.
Values may be sent and summed in bfloat16 or wider, within the bound.
No kernel may reach another device: no remote copies, remote signals or barrier semaphores. Data moves between devices by JAX's collectives and lax.ppermute only.
A program may use at most 640 MiB of HBM per device.

v0:
```python
import math

import jax
import jax.numpy as jnp
from jax import lax
from jax.sharding import PartitionSpec as P

HEADS = 20
KVH = 5
HEAD_DIM = 64


EPSILON = 1e-05
THETA = 10000.0
MASKED = -1e30


def rms_norm(value_tensor, gain):
    return (
        value_tensor
        * lax.rsqrt(jnp.mean(value_tensor * value_tensor, axis=-1, keepdims=True) + EPSILON)
        * gain
    )


def rotary(value_tensor, positions):
    half_width = value_tensor.shape[-1] // 2
    indices = jnp.arange(half_width).astype(jnp.float32)
    frequency = jnp.exp(indices * (-2.0 * math.log(THETA) / value_tensor.shape[-1]))
    angles = positions.astype(jnp.float32)[:, None] * frequency[None, :]
    cosine = jnp.cos(angles)[:, None, :]
    sine_of = jnp.sin(angles)[:, None, :]
    first_half = value_tensor[..., :half_width]
    second_half = value_tensor[..., half_width:]
    return jnp.concatenate(
        [first_half * cosine - second_half * sine_of, first_half * sine_of + second_half * cosine],
        axis=-1,
    )


def head_path(projected, gain, positions):
    shaped = projected.reshape(projected.shape[0], projected.shape[1] // HEAD_DIM, HEAD_DIM)
    return rotary(rms_norm(shaped, gain), positions)


def plain_dot(left, right):
    return jnp.dot(left, right, preferred_element_type=jnp.float32)


def dot_last(left, right):
    return lax.dot_general(
        left, right, (((1,), (1,)), ((), ())), preferred_element_type=jnp.float32
    )


def dot_first(left, right):
    return lax.dot_general(
        left, right, (((0,), (0,)), ((), ())), preferred_element_type=jnp.float32
    )


def gather_rows(value_tensor):
    gathered = lax.all_gather(value_tensor, "tp", axis=1, tiled=True)
    return gathered.reshape(gathered.shape[0] * gathered.shape[1], gathered.shape[2])


def sum_rows(term_fn, row_count):
    return lax.psum_scatter(
        term_fn(jnp.int32(0), row_count * lax.axis_size("tp")),
        "tp",
        scatter_dimension=0,
        tiled=True,
    )


def tp_block(value_tensor, count, seq_rows):
    row_total = value_tensor.shape[0]
    width = value_tensor.shape[2]
    span = count // row_total
    block = value_tensor
    block = block.reshape(row_total, span // seq_rows, seq_rows, width)
    return jnp.swapaxes(block, 0, 1).reshape(count, width)


def slot_table(head_counts, slot_count):
    tp_index = lax.axis_index("tp")
    ranks = jnp.arange(head_counts.shape[0])
    offset = jnp.sum(jnp.where(ranks < tp_index, head_counts, 0))
    held = jnp.sum(jnp.where(ranks == tp_index, head_counts, 0))
    slot_ids = jnp.arange(slot_count)
    valid = (slot_ids < held).astype(jnp.float32)
    kv_head = jnp.minimum((offset + slot_ids) // (HEADS // KVH), KVH - 1)
    select = (jnp.arange(KVH)[:, None] == kv_head[None, :]).astype(jnp.bfloat16)
    return (valid, select)


def doc_table(lengths, row_length):
    doc_ends = jnp.cumsum(lengths, axis=1)
    doc_starts = doc_ends - lengths
    token_places = jnp.arange(row_length)[None, :]
    doc_ids = (token_places >= doc_ends[:, 0:1]).astype(jnp.int32) + (
        token_places >= doc_ends[:, 1:2]
    ).astype(jnp.int32)
    begins = jnp.where(
        doc_ids == 0,
        doc_starts[:, 0:1],
        jnp.where(doc_ids == 1, doc_starts[:, 1:2], doc_starts[:, 2:3]),
    )
    return (doc_ids, token_places - begins)


def body(
    tokens,
    cotangent,
    lengths,
    head_counts,
    norm1_gain,
    norm2_gain,
    q_gain,
    k_gain,
    w_query,
    w_key,
    w_value,
    w_out,
    w_gate,
    w_up,
    w_down,
):
    row_total = tokens.shape[0]
    seq_rows = tokens.shape[1]
    stretch_rows = seq_rows * lax.axis_size("tp")
    row_length = stretch_rows * lax.axis_size("ctx")
    local_rows = row_total * seq_rows
    flat_rows = row_total * stretch_rows
    slot_count = w_query.shape[1] // HEAD_DIM
    model_width = w_key.shape[0]
    scale = HEAD_DIM ** (-0.5)
    valid, select = slot_table(head_counts, slot_count)
    doc_ids, positions = doc_table(lengths, row_length)
    own_start = lax.axis_index("ctx") * stretch_rows
    own_docs = lax.dynamic_slice_in_dim(doc_ids, own_start, stretch_rows, 1)
    own_positions = lax.dynamic_slice_in_dim(positions, own_start, stretch_rows, 1).reshape(
        flat_rows
    )
    own_places = own_start + jnp.arange(stretch_rows)
    allowed = (own_docs[:, :, None] == doc_ids[:, None, :]) & (
        own_places[None, :, None] >= jnp.arange(row_length)[None, None, :]
    )
    query_full, out_full, gate_full, up_full, down_full = (
        lax.all_gather(w_query, ("dp", "ctx"), axis=0, tiled=True),
        lax.all_gather(w_out, ("dp", "ctx"), axis=1, tiled=True),
        lax.all_gather(w_gate, ("dp", "ctx"), axis=0, tiled=True),
        lax.all_gather(w_up, ("dp", "ctx"), axis=0, tiled=True),
        lax.all_gather(w_down, ("dp", "ctx"), axis=1, tiled=True),
    )
    key_slots = (
        jnp.einsum(
            "dkh,ks->dsh",
            w_key.reshape(model_width, KVH, HEAD_DIM),
            select,
            preferred_element_type=jnp.float32,
        )
        .astype(jnp.bfloat16)
        .reshape(model_width, slot_count * HEAD_DIM)
    )
    value_slots = (
        jnp.einsum(
            "dkh,ks->dsh",
            w_value.reshape(model_width, KVH, HEAD_DIM),
            select,
            preferred_element_type=jnp.float32,
        )
        .astype(jnp.bfloat16)
        .reshape(model_width, slot_count * HEAD_DIM)
    )

    def by_slot(value_tensor, length):
        return jnp.moveaxis(value_tensor.reshape(row_total, length, slot_count, HEAD_DIM), 2, 1)

    def by_rows(value_tensor, length):
        return jnp.moveaxis(value_tensor, 1, 2).reshape(row_total, length, slot_count * HEAD_DIM)

    def as_rows(value_tensor):
        return value_tensor.reshape(row_total, stretch_rows, value_tensor.shape[-1])

    inputs = tokens.astype(jnp.float32)
    normed_one = gather_rows(rms_norm(inputs, norm1_gain).astype(jnp.bfloat16))
    query_proj = plain_dot(normed_one, query_full)
    key_proj = plain_dot(normed_one, key_slots)
    value_low = plain_dot(normed_one, value_slots).astype(jnp.bfloat16)
    query_low = head_path(query_proj, q_gain, own_positions).astype(jnp.bfloat16)
    key_low = (
        head_path(key_proj, k_gain, own_positions)
        .astype(jnp.bfloat16)
        .reshape(flat_rows, slot_count * HEAD_DIM)
    )
    key_all, value_all = (
        lax.all_gather(as_rows(key_low), "ctx", axis=1, tiled=True),
        lax.all_gather(as_rows(value_low), "ctx", axis=1, tiled=True),
    )
    query_slots = by_slot(query_low, stretch_rows)

    def forward_row(row_pieces):
        row_query, row_keys, row_values, row_allowed = row_pieces

        def forward_slot(pieces):
            query, keys, values = pieces
            scores = jnp.where(row_allowed, dot_last(query, keys) * scale, MASKED)
            peak = jnp.max(scores, axis=1, keepdims=True)
            exp_scores = jnp.exp(scores - peak)
            exp_total = jnp.sum(exp_scores, axis=1, keepdims=True)
            probs_low = (exp_scores / exp_total).astype(jnp.bfloat16)
            return (plain_dot(probs_low, values), (peak + jnp.log(exp_total))[:, 0])

        return lax.map(forward_slot, (row_query, row_keys, row_values))

    attended, log_sums = lax.map(
        forward_row,
        (query_slots, by_slot(key_all, row_length), by_slot(value_all, row_length), allowed),
    )
    out_low = by_rows(attended * valid[None, :, None, None], stretch_rows).astype(jnp.bfloat16)

    def out_term(start, count):
        return plain_dot(tp_block(out_low, count, seq_rows), out_full)

    residual = inputs + sum_rows(out_term, local_rows).reshape(row_total, seq_rows, model_width)
    normed_two = gather_rows(rms_norm(residual, norm2_gain).astype(jnp.bfloat16))
    gate = plain_dot(normed_two, gate_full)
    up_proj = plain_dot(normed_two, up_full)
    sigmoid_gate = jax.nn.sigmoid(gate)
    silu_gate = gate * sigmoid_gate
    hidden = (silu_gate * up_proj).astype(jnp.bfloat16)
    hidden_rows = as_rows(hidden)

    def down_term(start, count):
        return plain_dot(tp_block(hidden_rows, count, seq_rows), down_full)

    output = (
        residual + sum_rows(down_term, local_rows).reshape(row_total, seq_rows, model_width)
    ).astype(jnp.bfloat16)
    grad_out_all = gather_rows(cotangent)
    grad_down = dot_first(hidden, grad_out_all)
    grad_hidden = dot_last(grad_out_all, down_full)
    grad_gate_low = (
        grad_hidden * up_proj * sigmoid_gate * (1.0 + gate * (1.0 - sigmoid_gate))
    ).astype(jnp.bfloat16)
    grad_up_low = (grad_hidden * silu_gate).astype(jnp.bfloat16)
    grad_gate_w = dot_first(normed_two, grad_gate_low)
    grad_up_w = dot_first(normed_two, grad_up_low)
    gate_rows = as_rows(grad_gate_low)
    up_rows = as_rows(grad_up_low)

    def ffn_input_term(start, count):
        return dot_last(tp_block(gate_rows, count, seq_rows), gate_full) + dot_last(
            tp_block(up_rows, count, seq_rows), up_full
        )

    grad_normed_two = sum_rows(ffn_input_term, local_rows).reshape(row_total, seq_rows, model_width)
    _, pull_two = jax.vjp(rms_norm, residual, norm2_gain)
    grad_residual_norm, grad_norm_two = pull_two(grad_normed_two)
    grad_residual = cotangent.astype(jnp.float32) + grad_residual_norm
    grad_attn_all = gather_rows(grad_residual.astype(jnp.bfloat16))
    out_flat = out_low.reshape(flat_rows, slot_count * HEAD_DIM)
    grad_out_w = dot_first(out_flat, grad_attn_all)
    grad_out_low = (
        dot_last(grad_attn_all, out_full) * jnp.repeat(valid, HEAD_DIM)[None, :]
    ).astype(jnp.bfloat16)
    key_back, value_back = (
        lax.all_gather(as_rows(key_low), "ctx", axis=1, tiled=True),
        lax.all_gather(as_rows(value_low), "ctx", axis=1, tiled=True),
    )

    def backward_row(row_pieces):
        row_query, row_keys, row_values, row_sums, row_grads, row_allowed = row_pieces

        def backward_slot(pieces):
            query, keys, values, log_sum, grad_slot = pieces
            scores = jnp.where(row_allowed, dot_last(query, keys) * scale, MASKED)
            probs = jnp.exp(scores - log_sum[:, None])
            grad_probs = dot_last(grad_slot, values)
            inner = jnp.sum(grad_probs * probs, axis=1, keepdims=True)
            grad_scores = (probs * (grad_probs - inner)).astype(jnp.bfloat16)
            grad_query = plain_dot(grad_scores, keys) * scale
            grad_keys = dot_first(grad_scores, query) * scale
            grad_values = dot_first(probs.astype(jnp.bfloat16), grad_slot)
            return (grad_query, grad_keys, grad_values)

        return lax.map(backward_slot, (row_query, row_keys, row_values, row_sums, row_grads))

    grad_query, grad_keys, grad_values = lax.map(
        backward_row,
        (
            query_slots,
            by_slot(key_back, row_length),
            by_slot(value_back, row_length),
            log_sums,
            by_slot(grad_out_low, stretch_rows),
            allowed,
        ),
    )
    grad_key_own, grad_value_own = (
        lax.psum_scatter(
            by_rows(grad_keys, row_length).astype(jnp.bfloat16),
            "ctx",
            scatter_dimension=1,
            tiled=True,
        ).astype(jnp.float32),
        lax.psum_scatter(
            by_rows(grad_values, row_length).astype(jnp.bfloat16),
            "ctx",
            scatter_dimension=1,
            tiled=True,
        ).astype(jnp.float32),
    )
    _, pull_query = jax.vjp(
        lambda projected, gain: head_path(projected, gain, own_positions), query_proj, q_gain
    )
    grad_query_proj, grad_q_gain = pull_query(
        jnp.moveaxis(grad_query, 1, 2).reshape(flat_rows, slot_count, HEAD_DIM)
    )
    _, pull_key = jax.vjp(
        lambda projected, gain: head_path(projected, gain, own_positions), key_proj, k_gain
    )
    grad_key_proj, grad_k_gain = pull_key(grad_key_own.reshape(flat_rows, slot_count, HEAD_DIM))
    grad_query_low = grad_query_proj.astype(jnp.bfloat16)
    grad_key_low = grad_key_proj.astype(jnp.bfloat16)
    grad_value_low = grad_value_own.reshape(flat_rows, slot_count * HEAD_DIM).astype(jnp.bfloat16)
    grad_query_w = dot_first(normed_one, grad_query_low)
    select_float = select.astype(jnp.float32)
    grad_key_w = jnp.einsum(
        "dsh,ks->dkh",
        dot_first(normed_one, grad_key_low).reshape(model_width, slot_count, HEAD_DIM),
        select_float,
        precision=lax.Precision.HIGHEST,
    ).reshape(model_width, KVH * HEAD_DIM)
    grad_value_w = jnp.einsum(
        "dsh,ks->dkh",
        dot_first(normed_one, grad_value_low).reshape(model_width, slot_count, HEAD_DIM),
        select_float,
        precision=lax.Precision.HIGHEST,
    ).reshape(model_width, KVH * HEAD_DIM)
    query_rows = as_rows(grad_query_low)
    key_rows = as_rows(grad_key_low)
    value_rows = as_rows(grad_value_low)

    def attn_input_term(start, count):
        return (
            dot_last(tp_block(query_rows, count, seq_rows), query_full)
            + dot_last(tp_block(key_rows, count, seq_rows), key_slots)
            + dot_last(tp_block(value_rows, count, seq_rows), value_slots)
        )

    grad_normed_one = sum_rows(attn_input_term, local_rows).reshape(
        row_total, seq_rows, model_width
    )
    _, pull_one = jax.vjp(rms_norm, inputs, norm1_gain)
    grad_inputs_norm, grad_norm_one = pull_one(grad_normed_one)
    grad_inputs = grad_residual + grad_inputs_norm
    grad_query_w, grad_out_w, grad_gate_w, grad_up_w, grad_down = (
        lax.psum_scatter(
            grad_query_w.astype(jnp.bfloat16), ("dp", "ctx"), scatter_dimension=0, tiled=True
        ).astype(jnp.float32),
        lax.psum_scatter(
            grad_out_w.astype(jnp.bfloat16), ("dp", "ctx"), scatter_dimension=1, tiled=True
        ).astype(jnp.float32),
        lax.psum_scatter(
            grad_gate_w.astype(jnp.bfloat16), ("dp", "ctx"), scatter_dimension=0, tiled=True
        ).astype(jnp.float32),
        lax.psum_scatter(
            grad_up_w.astype(jnp.bfloat16), ("dp", "ctx"), scatter_dimension=0, tiled=True
        ).astype(jnp.float32),
        lax.psum_scatter(
            grad_down.astype(jnp.bfloat16), ("dp", "ctx"), scatter_dimension=1, tiled=True
        ).astype(jnp.float32),
    )
    grad_key_w, grad_value_w, grad_norm_one, grad_norm_two, grad_q_gain, grad_k_gain = lax.psum(
        (grad_key_w, grad_value_w, grad_norm_one, grad_norm_two, grad_q_gain, grad_k_gain),
        ("dp", "ctx", "tp"),
    )
    return (
        output,
        grad_inputs,
        grad_norm_one,
        grad_norm_two,
        grad_q_gain,
        grad_k_gain,
        grad_query_w,
        grad_key_w,
        grad_value_w,
        grad_out_w,
        grad_gate_w,
        grad_up_w,
        grad_down,
    )


def solution(mesh):
    return jax.shard_map(
        body,
        mesh=mesh,
        in_specs=(
            P("dp", ("ctx", "tp"), None),
            P("dp", ("ctx", "tp"), None),
            P("dp", None),
            P(),
            P(),
            P(),
            P(),
            P(),
            P(("dp", "ctx"), "tp"),
            P(),
            P(),
            P("tp", ("dp", "ctx")),
            P(("dp", "ctx"), "tp"),
            P(("dp", "ctx"), "tp"),
            P("tp", ("dp", "ctx")),
        ),
        out_specs=(
            P("dp", ("ctx", "tp"), None),
            P("dp", ("ctx", "tp"), None),
            P(),
            P(),
            P(),
            P(),
            P(("dp", "ctx"), "tp"),
            P(),
            P(),
            P("tp", ("dp", "ctx")),
            P(("dp", "ctx"), "tp"),
            P(("dp", "ctx"), "tp"),
            P("tp", ("dp", "ctx")),
        ),
        check_vma=False,
    )
```

profile of v0, /device:TPU:0, one launch (start us, length us, event | category | flops | bytes accessed | tf_op | source)
XLA Modules:
  0.0 3366.9 jit_solution(612909178825626275)
XLA Ops:
  137.0 61.5 %all-gather.18.cloned.1.call-done = bf16[2,1536,768]{1,2,0:T(8,128)(2,1)} async-done(((bf16[2,384,768]{1,2,0:T(8,128)(2,1)}), bf16[2,1536,768]{1,2,0:T(8,128)(2,1)}) %all-gather.18.cloned.1.call-update) | async-done | bytes 4718608 | tf_op jit(solution)/shard_map/all_gather | solution.py:199
  208.1 80.3 %all-gather.16.cloned.1.call-done = bf16[2,1536,768]{1,2,0:T(8,128)(2,1)} async-done(((bf16[2,384,768]{1,2,0:T(8,128)(2,1)}), bf16[2,1536,768]{1,2,0:T(8,128)(2,1)}) %all-gather.16.cloned.1.call-update) | async-done | bytes 4718608 | tf_op jit(solution)/shard_map/all_gather | solution.py:198
  299.8 134.2 %while.53 = (s32[]{:T(128)}, f32[2,12,384,64]{2,3,1,0:T(8,128)}, f32[2,12,384]{2,1,0:T(8,128)S(1)}, bf16[2,12,384,64]{3,2,1,0:T(8,128)(2,1)}, bf16[2,12,1536,64]...) while((s32[]{:T(128)}, f32[2,12,384,64]{2,3,1,0:T(8,128)}, ...), condition=%wide.region_10.11_spmd, body=%wide.region_5.10_spmd.sunk | while | flops 155713152 | bytes 32313720 | solution.py:217
  310.6 53.8 %while.56 = (s32[]{:T(128)}, f32[12,384,64]{1,2,0:T(8,128)}, f32[12,384]{1,0:T(8,128)S(1)}, bf16[12,384,64]{2,1,0:T(8,128)(2,1)S(1)}, bf16[12,1536,64]{2,1,0:T(8...) while((s32[]{:T(128)}, f32[12,384,64]{1,2,0:T(8,128)}, ...), condition=%wide.region_9.9_spmd, body=%wide.region_6.8_spmd.sunk | while | flops 155713152 | bytes 8671337 | solution.py:215
  377.7 53.7 %while.56 = (s32[]{:T(128)}, f32[12,384,64]{1,2,0:T(8,128)}, f32[12,384]{1,0:T(8,128)S(1)}, bf16[12,384,64]{2,1,0:T(8,128)(2,1)S(1)}, bf16[12,1536,64]{2,1,0:T(8...) while((s32[]{:T(128)}, f32[12,384,64]{1,2,0:T(8,128)}, ...), condition=%wide.region_9.9_spmd, body=%wide.region_6.8_spmd.sunk | while | flops 155713152 | bytes 8671337 | solution.py:215
  448.2 75.6 %reduce-scatter.20.cloned.1.call-done = f32[384,2048]{1,0:T(8,128)} async-done(((f32[768,2048]{1,0:T(8,128)}), f32[384,2048]{1,0:T(8,128)}) %reduce-scatter.20.cloned.1.call-update) | async-done | bytes 3145744 | tf_op jit(solution)/shard_map/reduce_scatter | solution.py:68
  532.7 41.8 %all-gather.22.cloned.1.call-done = bf16[2,384,2048]{2,1,0:T(8,128)(2,1)} async-done(((bf16[2,192,2048]{2,1,0:T(8,128)(2,1)}), bf16[2,384,2048]{2,1,0:T(8,128)(2,1)}) %all-gather.22.cloned.1.call-update) | async-done | bytes 3145744 | tf_op jit(solution)/shard_map/all_gather | solution.py:63
  574.5 129.4 %all-gather.26.cloned.1.call-done = bf16[2048,4096]{1,0:T(8,128)(2,1)} async-done(((bf16[128,4096]{1,0:T(8,128)(2,1)}), bf16[2048,4096]{1,0:T(8,128)(2,1)}) %all-gather.26.cloned.1.call-update) | async-done | bytes 16777232 | tf_op jit(solution)/shard_map/all_gather | solution.py:153
  724.1 107.3 %all-gather.24.cloned.1.call-done = bf16[2048,4096]{1,0:T(8,128)(2,1)} async-done(((bf16[128,4096]{1,0:T(8,128)(2,1)}), bf16[2048,4096]{1,0:T(8,128)(2,1)}) %all-gather.24.cloned.1.call-update) | async-done | bytes 16777232 | tf_op jit(solution)/shard_map/all_gather | solution.py:152
  876.0 132.7 %all-gather.28.cloned.1.call-done = bf16[4096,2048]{1,0:T(8,128)(2,1)} async-done(((bf16[4096,128]{1,0:T(8,128)(2,1)}), bf16[4096,2048]{1,0:T(8,128)(2,1)}) %all-gather.28.cloned.1.call-update) | async-done | bytes 16777232 | tf_op jit(solution)/shard_map/all_gather | solution.py:154
  1084.9 75.3 %reduce-scatter.24.cloned.1.call-done = f32[384,2048]{1,0:T(8,128)} async-done(((f32[768,2048]{1,0:T(8,128)}), f32[384,2048]{1,0:T(8,128)}) %reduce-scatter.24.cloned.1.call-update) | async-done | bytes 3145744 | tf_op jit(solution)/shard_map/reduce_scatter | solution.py:68
  1167.4 44.9 %all-gather.32.cloned.1.call-done = bf16[2,384,2048]{2,1,0:T(8,128)(2,1)} async-done(((bf16[2,192,2048]{2,1,0:T(8,128)(2,1)}), bf16[2,384,2048]{2,1,0:T(8,128)(2,1)}) %all-gather.32.cloned.1.call-update) | async-done | bytes 3145744 | tf_op jit(solution)/shard_map/all_gather | solution.py:63
  1221.6 258.5 %while.55 = (s32[]{:T(128)}, f32[2,12,384,64]{2,3,1,0:T(8,128)}, bf16[2,12,1536,64]{2,3,1,0:T(8,128)(2,1)}, bf16[2,12,1536,64]{2,3,1,0:T(8,128)(2,1)}, bf16[2,12...) while((s32[]{:T(128)}, f32[2,12,384,64]{2,3,1,0:T(8,128)}, ...), condition=%wide.region_21.22_spmd, body=%wide.region_17.21_spmd.sunk | while | flops 382918272 | bytes 75056560 | solution.py:290
  1238.4 105.7 %while.57 = (s32[]{:T(128)}, f32[12,384,64]{1,2,0:T(8,128)}, bf16[12,1536,64]{1,2,0:T(8,128)(2,1)}, bf16[12,1536,64]{1,2,0:T(8,128)(2,1)}, bf16[12,384,64]{2,1,0...) while((s32[]{:T(128)}, f32[12,384,64]{1,2,0:T(8,128)}, ...), condition=%wide.region_20.20_spmd, body=%wide.region_18.19_spmd.sunk | while | flops 382918272 | bytes 20755576 | solution.py:288
  1367.7 105.7 %while.57 = (s32[]{:T(128)}, f32[12,384,64]{1,2,0:T(8,128)}, bf16[12,1536,64]{1,2,0:T(8,128)(2,1)}, bf16[12,1536,64]{1,2,0:T(8,128)(2,1)}, bf16[12,384,64]{2,1,0...) while((s32[]{:T(128)}, f32[12,384,64]{1,2,0:T(8,128)}, ...), condition=%wide.region_20.20_spmd, body=%wide.region_18.19_spmd.sunk | while | flops 382918272 | bytes 20755576 | solution.py:288
  1489.5 210.1 %copy.126 = bf16[2,1536,768]{0,2,1:T(8,128)(2,1)} copy(bf16[2,1536,768]{1,0,2:T(2,128)(2,1)} %bitcast.319) | data formatting | bytes 9437184
  1699.5 484.5 %reshape.444 = bf16[1536,1536]{1,0:T(8,128)(2,1)} reshape(bf16[1536,768,2]{2,1,0:T(8,128)(2,1)} %bitcast.94) | data formatting | bytes 9437184
  2299.1 164.4 %reshape.445 = bf16[384,768,2]{2,1,0:T(8,128)(2,1)} reshape(bf16[384,1536]{1,0:T(8,128)(2,1)} %reduce-scatter.34.cloned.1.call-done) | data formatting | bytes 2359296
  2463.5 68.5 %copy.127 = bf16[2,384,768]{1,0,2:T(2,128)(2,1)S(1)} copy(bf16[2,384,768]{0,2,1:T(8,128)(2,1)} %bitcast.95) | data formatting | bytes 2359296
  2641.4 149.5 %reduce-scatter.32.cloned.1.call-done = bf16[128,4096]{1,0:T(8,128)(2,1)} async-done(((bf16[2048,4096]{1,0:T(8,128)(2,1)}), bf16[128,4096]{1,0:T(8,128)(2,1)}) %reduce-scatter.32.cloned.1.call-update) | async-done | bytes 1048592 | tf_op jit(solution)/shard_map/reduce_scatter | solution.py:369
  2793.6 178.9 %reduce-scatter.30.cloned.1.call-done = bf16[128,4096]{1,0:T(8,128)(2,1)} async-done(((bf16[2048,4096]{1,0:T(8,128)(2,1)}), bf16[128,4096]{1,0:T(8,128)(2,1)}) %reduce-scatter.30.cloned.1.call-update) | async-done | bytes 1048592 | tf_op jit(solution)/shard_map/reduce_scatter | solution.py:366
  2975.3 66.1 %reduce-scatter.28.cloned.1.call-done = bf16[128,768]{1,0:T(8,128)(2,1)} async-done(((bf16[2048,768]{1,0:T(8,128)(2,1)}), bf16[128,768]{1,0:T(8,128)(2,1)}) %reduce-scatter.28.cloned.1.call-update) | async-done | bytes 196624 | tf_op jit(solution)/shard_map/reduce_scatter | solution.py:360
  3043.1 76.6 %reduce-scatter.26.cloned.1.call-done = f32[384,2048]{1,0:T(8,128)} async-done(((f32[768,2048]{1,0:T(8,128)}), f32[384,2048]{1,0:T(8,128)}) %reduce-scatter.26.cloned.1.call-update) | async-done | bytes 3145744 | tf_op jit(solution)/shard_map/reduce_scatter | solution.py:68
  3208.1 146.9 %all-reduce.8.cloned.1.call-done = (f32[2048,320]{0,1:T(8,128)}, f32[2048,320]{0,1:T(8,128)}) async-done(((f32[2048,320]{0,1:T(8,128)}, f32[2048,320]{0,1:T(8,128)}), (f32[2048,320]{0,1:T(8,128)}, f32[2048,320]{0,1:T(8,128)})) %all-reduce.8.cloned.1.call-update) | async-done | bytes 5242896 | tf_op jit(solution)/shard_map/psum | solution.py:376
  (688 shorter events, 1056.3 us)
Async XLA Ops:
  7.2 53.3 %all-gather.12.cloned.1.call-start = ((), (), s32[]{:S(2)}) async-start(), calls=%async_computation.11 | async-start | bytes 4718592 | tf_op jit(solution)/shard_map/all_gather | solution.py:63
  12.7 95.3 %all-gather.14.cloned.1.call-start = ((), (), s32[]{:S(2)}) async-start(), calls=%async_computation.12 | async-start | bytes 3342336 | tf_op jit(solution)/shard_map/all_gather | solution.py:150
  13.5 185.0 %all-gather.18.cloned.1.call-start = ((), (), s32[]{:S(2)}) async-start(), calls=%async_computation.14 | async-start | bytes 5898240 | tf_op jit(solution)/shard_map/all_gather | solution.py:199
  67.5 220.9 %all-gather.16.cloned.1.call-start = ((), (), s32[]{:S(2)}) async-start(), calls=%async_computation.13 | async-start | bytes 5898240 | tf_op jit(solution)/shard_map/all_gather | solution.py:198
  123.1 318.7 %all-gather.20.cloned.1.call-start = ((), (), s32[]{:S(2)}) async-start(), calls=%async_computation.15 | async-start | bytes 3342336 | tf_op jit(solution)/shard_map/all_gather | solution.py:151
  123.6 400.2 %reduce-scatter.20.cloned.1.call-start = ((), (), s32[]{:S(2)}) async-start(), calls=%async_computation.16 | async-start | bytes 9437184 | tf_op jit(solution)/shard_map/reduce_scatter | solution.py:68
  448.2 126.3 %all-gather.22.cloned.1.call-start = ((), (), s32[]{:S(2)}) async-start(), calls=%async_computation.17 | async-start | bytes 4718592 | tf_op jit(solution)/shard_map/all_gather | solution.py:63
  529.4 174.5 %all-gather.26.cloned.1.call-start = ((), (), s32[]{:S(2)}) async-start(), calls=%async_computation.19 | async-start | bytes 17825792 | tf_op jit(solution)/shard_map/all_gather | solution.py:153
  530.1 301.2 %all-gather.24.cloned.1.call-start = ((), (), s32[]{:S(2)}) async-start(), calls=%async_computation.18 | async-start | bytes 17825792 | tf_op jit(solution)/shard_map/all_gather | solution.py:152
  530.9 345.1 %all-gather.30.cloned.1.call-start = ((), (), s32[]{:S(2)}) async-start(), calls=%async_computation.22 | async-start | bytes 4718592 | tf_op jit(solution)/shard_map/all_gather | solution.py:63
  531.5 477.2 %all-gather.28.cloned.1.call-start = ((), (), s32[]{:S(2)}) async-start(), calls=%async_computation.20 | async-start | bytes 17825792 | tf_op jit(solution)/shard_map/all_gather | solution.py:154
  532.2 628.0 %reduce-scatter.24.cloned.1.call-start = ((), (), s32[]{:S(2)}) async-start(), calls=%async_computation.23 | async-start | bytes 9437184 | tf_op jit(solution)/shard_map/reduce_scatter | solution.py:68
  1084.9 127.4 %all-gather.32.cloned.1.call-start = ((), (), s32[]{:S(2)}) async-start(), calls=%async_computation.24 | async-start | bytes 4718592 | tf_op jit(solution)/shard_map/all_gather | solution.py:63
  1167.2 1131.9 %reduce-scatter.34.cloned.1.call-start = ((), (), s32[]{:S(2)}) async-start(), calls=%async_computation.29 | async-start | bytes 5898240
  2184.1 366.1 %reduce-scatter.36.cloned.1.call-start = ((), (), s32[]{:S(2)}) async-start(), calls=%async_computation.30 | async-start | bytes 5898240
  2202.2 433.9 %reduce-scatter.38.cloned.1.call-start = ((), (), s32[]{:S(2)}) async-start(), calls=%async_computation.31 | async-start | bytes 3342336
  2214.2 423.8 %reduce-scatter.40.cloned.1.call-start = ((), (), s32[]{:S(2)}) async-start(), calls=%async_computation.32 | async-start | bytes 17825792
  2255.4 535.5 %reduce-scatter.32.cloned.1.call-start = ((), (), s32[]{:S(2)}) async-start(), calls=%async_computation.28 | async-start | bytes 17825792 | tf_op jit(solution)/shard_map/reduce_scatter | solution.py:369
  2275.3 697.2 %reduce-scatter.30.cloned.1.call-start = ((), (), s32[]{:S(2)}) async-start(), calls=%async_computation.27 | async-start | bytes 17825792 | tf_op jit(solution)/shard_map/reduce_scatter | solution.py:366
  2295.6 745.8 %reduce-scatter.28.cloned.1.call-start = ((), (), s32[]{:S(2)}) async-start(), calls=%async_computation.26 | async-start | bytes 3342336 | tf_op jit(solution)/shard_map/reduce_scatter | solution.py:360
  2544.5 575.1 %reduce-scatter.26.cloned.1.call-start = ((), (), s32[]{:S(2)}) async-start(), calls=%async_computation.25 | async-start | bytes 9437184 | tf_op jit(solution)/shard_map/reduce_scatter | solution.py:68
  2584.5 615.9 %reduce-scatter.22.cloned.1.call-start = ((), (), s32[]{:S(2)}) async-start(), calls=%async_computation.21 | async-start | bytes 9437184 | tf_op jit(solution)/shard_map/reduce_scatter | solution.py:68
  2606.7 748.2 %all-reduce.8.cloned.1.call-start = ((), (), s32[]{:S(2)}) async-start(), calls=%async_computation.33 | async-start | bytes 10485760 | tf_op jit(solution)/shard_map/psum | solution.py:376
  2793.6 326.1 %copy-start.53 = (f32[2,192]{1,0:T(2,128)S(1)}, f32[2,192]{1,0:T(2,128)}, u32[]{:S(2)}) copy-start(f32[2,192]{1,0:T(2,128)} %copy-done.52) | copy-start | bytes 4612
  (80 other events, 1818.2 us)
Sparse Core Ops, SparseCore 0:
  12.8 47.6 all-gather.11
  62.8 45.1 all-gather.13
  110.2 88.1 all-gather.17
  200.5 87.8 all-gather.15
  290.3 46.6 all-gather.19
  448.3 75.4 reduce-scatter.19
  529.5 44.9 all-gather.21
  577.0 126.8 all-gather.25
  706.3 124.9 all-gather.23
  832.8 43.0 all-gather.29
  878.3 130.3 all-gather.27
  1085.0 75.2 reduce-scatter.23
  1167.3 44.9 all-gather.31
  2184.2 85.2 reduce-scatter.33
  2271.7 85.7 reduce-scatter.35
  2361.1 66.7 reduce-scatter.37
  2431.8 177.5 reduce-scatter.39
  2613.3 177.4 reduce-scatter.31
  2795.0 177.5 reduce-scatter.29
  2976.2 65.1 reduce-scatter.27
  3043.7 75.9 reduce-scatter.25
  3122.1 78.2 reduce-scatter.21
  3207.3 147.5 all-reduce.7
where the time goes:
time: 3390 us; the launch traced here: 3370 us
  waiting for transfers between devices  1500 us (44%)
  local copies, waits for them, and re-layouts  1170 us (35%)
  matrix products  558 us (16%)
  other arithmetic  78.3 us (2%)
  blocking collectives  40.2 us (1%)
    unnamed x159, local copies, waits for them, and re-layouts  995 us
    reduce_scatter x4, waiting for transfers between devices, sum_rows(): lax.psum_scatter(term_fn(jnp.int32(0), row_count * lax.axis_size('tp')),...  265 us
    dot_general x79, matrix products, dot_last(): lax.dot_general(left, right, (((1,), (1,)), ((), ())), preferred_element_...  204 us
    dot_general x55, matrix products, plain_dot(): return jnp.dot(left, right, preferred_element_type=jnp.float32)  189 us
    reduce_scatter x1, waiting for transfers between devices, body(): lax.psum_scatter(grad_gate_w.astype(jnp.bfloat16), ('dp', 'ctx'), scatter...  179 us
    all_gather x4, waiting for transfers between devices, gather_rows(): gathered = lax.all_gather(value_tensor, 'tp', axis=1, tiled=True)  151 us
    reduce_scatter x1, waiting for transfers between devices, body(): lax.psum_scatter(grad_up_w.astype(jnp.bfloat16), ('dp', 'ctx'), scatter_d...  149 us
    dot_general x55, matrix products, dot_first(): lax.dot_general(left, right, (((0,), (0,)), ((), ())), preferred_element_...  148 us
  transfers between devices with their start and end apart: 23, of which 18 were waited for; matrix products, arithmetic and copies ran while one was open for 21% of the time, Pallas kernels for 0%

commit v1 on v0

v1 whole, which is shorter than its diff:
```python
import math

import jax
import jax.numpy as jnp
from jax import lax
from jax.experimental import pallas as pl
from jax.experimental.pallas import tpu as pltpu
from jax.sharding import Mesh
from jax.sharding import PartitionSpec as P

HEADS = 20
KVH = 5
HEAD_DIM = 64
GROUP = HEADS // KVH

EPSILON = 1e-05
THETA = 10000.0
SCALE = HEAD_DIM ** (-0.5)
EXP2_SCALE = SCALE / math.log(2.0)

BF16 = jnp.bfloat16
F32 = jnp.float32


def dot(left, right, contract):
    return lax.dot_general(left, right, ((contract[:1], contract[1:]), ((), ())), preferred_element_type=F32)


def swap(value, axis, bit=1):
    size = lax.axis_size(axis)
    return lax.ppermute(value, axis, [(i, i ^ bit) for i in range(size)])


def join(value, axis, dimension, bit=1):
    return jnp.concatenate([value, swap(value, axis, bit)], axis=dimension)


def fold(value, axis, dimension, bit=1):
    size = value.shape[dimension] // 2
    got = swap(lax.slice_in_dim(value, size, 2 * size, axis=dimension), axis, bit)
    return sum32(lax.slice_in_dim(value, 0, size, axis=dimension), got)


def sum32(left, right):
    return (left.astype(F32) + right.astype(F32)).astype(BF16)


def stacked(ref, slots, head, begin, span):
    return jnp.concatenate(
        [ref[slots[head * GROUP + i], :, begin : begin + span] for i in range(GROUP)], axis=1
    )


def attend_kernel(
    order, counts, starts, slots, q_ref, k_ref, v_ref, first_ref, place_ref, o_ref, total_ref
):
    head = pl.program_id(0)
    pack, _, wide = first_ref.shape
    span = wide // GROUP

    @pl.when(head == 0)
    def _():
        o_ref[...] = jnp.zeros_like(o_ref)

    place = place_ref[...]
    for row in range(pack):
        begin = row * span
        query = stacked(q_ref, slots, head, begin, span)
        first = first_ref[row]

        def step(i, carry):
            acc, total = carry
            block = order[row, i]
            scores = dot(k_ref[block, :, begin : begin + span].T, query, (1, 0))
            keys = starts[block] + lax.broadcasted_iota(jnp.int32, scores.shape, 0)
            weight = jnp.where((keys >= first) & (keys <= place), jnp.exp2(scores * EXP2_SCALE), 0.0)
            total = total + jnp.sum(weight, axis=0, keepdims=True)
            acc = acc + dot(v_ref[block, :, begin : begin + span], weight.astype(BF16), (1, 0))
            return acc, total

        acc, total = lax.fori_loop(
            0, counts[row], step, (jnp.zeros((HEAD_DIM, wide), F32), jnp.zeros((1, wide), F32))
        )
        total_ref[0, row] = total
        acc = (acc / total).astype(o_ref.dtype)
        for i in range(GROUP):
            o_ref[slots[head * GROUP + i], :, begin : begin + span] = acc[:, i * span : (i + 1) * span]


def attention_specs(query, keyvalue, first):
    slot_count, _, lanes = query.shape
    pack, _, wide = first.shape
    blocks = keyvalue.shape[0]
    whole = pl.BlockSpec((slot_count, HEAD_DIM, lanes), lambda g, *_: (0, 0, 0))
    keys = pl.BlockSpec((blocks, HEAD_DIM, lanes), lambda g, *_: (0, g, 0))
    values = pl.BlockSpec((blocks, HEAD_DIM, lanes), lambda g, *_: (0, KVH + g, 0))
    totals = pl.BlockSpec((1, pack, 1, wide), lambda g, *_: (g, 0, 0, 0))
    bounds = [
        pl.BlockSpec((pack, 1, wide), lambda g, *_: (0, 0, 0)),
        pl.BlockSpec((1, wide), lambda g, *_: (0, 0)),
    ]
    work = HEADS * lanes * blocks * (wide // GROUP)
    return whole, keys, values, totals, bounds, work


def attend(query, keyvalue, tables):
    order, counts, starts, slots, first, place = tables
    pack, _, wide = first.shape
    whole, keys, values, totals, bounds, work = attention_specs(query, keyvalue, first)
    spec = pltpu.PrefetchScalarGridSpec(
        num_scalar_prefetch=4,
        grid=(KVH,),
        in_specs=[whole, keys, values, *bounds],
        out_specs=[whole, totals],
    )
    return pl.pallas_call(
        attend_kernel,
        grid_spec=spec,
        out_shape=[jax.ShapeDtypeStruct(query.shape, BF16), jax.ShapeDtypeStruct((KVH, pack, 1, wide), F32)],
        compiler_params=pltpu.CompilerParams(dimension_semantics=("arbitrary",), vmem_limit_bytes=40 * 2**20),
        cost_estimate=pl.CostEstimate(flops=work * 1024, bytes_accessed=8 * 2**20, transcendentals=work),
        name="attend",
    )(order, counts, starts, slots, query, keyvalue, keyvalue, first, place)


def attend_back_kernel(
    order, counts, starts, slots, q_ref, g_ref, o_ref, k_ref, v_ref, total_ref, first_ref, place_ref,
    dq_ref, dkv_ref,
):
    head = pl.program_id(0)
    pack, _, wide = first_ref.shape
    span = wide // GROUP

    @pl.when(head == 0)
    def _():
        dq_ref[...] = jnp.zeros_like(dq_ref)

    dkv_ref[...] = jnp.zeros_like(dkv_ref)
    place = place_ref[...]
    for row in range(pack):
        begin = row * span
        query, grad, out = (stacked(ref, slots, head, begin, span) for ref in (q_ref, g_ref, o_ref))
        inner = jnp.sum(grad.astype(F32) * out.astype(F32), axis=0, keepdims=True)
        lift = jnp.log2(total_ref[0, row])
        first = first_ref[row]

        def step(i, acc):
            block = order[row, i]
            key, value = (ref[block, :, begin : begin + span] for ref in (k_ref, v_ref))
            scores = dot(key.T, query, (1, 0))
            keys = starts[block] + lax.broadcasted_iota(jnp.int32, scores.shape, 0)
            probs = jnp.where((keys >= first) & (keys <= place), jnp.exp2(scores * EXP2_SCALE - lift), 0.0)
            grad_probs = dot(value.T, grad, (1, 0))
            grad_scores = (probs * (grad_probs - inner)).astype(BF16)
            dkv_ref[block, 0, :, begin : begin + span] = (
                (dot(grad_scores, query, (1, 1)) * SCALE).T.astype(dkv_ref.dtype)
            )
            dkv_ref[block, 1, :, begin : begin + span] = (
                dot(probs.astype(BF16), grad, (1, 1)).T.astype(dkv_ref.dtype)
            )
            return acc + dot(key, grad_scores, (1, 0))

        acc = lax.fori_loop(0, counts[row], step, jnp.zeros((HEAD_DIM, wide), F32)) * SCALE
        for i in range(GROUP):
            dq_ref[slots[head * GROUP + i], :, begin : begin + span] = acc[:, i * span : (i + 1) * span]


def attend_back(query, grad, out, keyvalue, totals_in, tables):
    order, counts, starts, slots, first, place = tables
    whole, keys, values, totals, bounds, work = attention_specs(query, keyvalue, first)
    blocks, _, lanes = keyvalue.shape
    spec = pltpu.PrefetchScalarGridSpec(
        num_scalar_prefetch=4,
        grid=(KVH,),
        in_specs=[whole, whole, whole, keys, values, totals, *bounds],
        out_specs=[whole, pl.BlockSpec((blocks, 2, HEAD_DIM, lanes), lambda g, *_: (0, 0, g, 0))],
    )
    return pl.pallas_call(
        attend_back_kernel,
        grid_spec=spec,
        out_shape=[
            jax.ShapeDtypeStruct(query.shape, F32),
            jax.ShapeDtypeStruct((blocks, 2, KVH * HEAD_DIM, lanes), BF16),
        ],
        compiler_params=pltpu.CompilerParams(dimension_semantics=("arbitrary",), vmem_limit_bytes=48 * 2**20),
        cost_estimate=pl.CostEstimate(flops=work * 2560, bytes_accessed=16 * 2**20, transcendentals=work),
        name="attend_back",
    )(order, counts, starts, slots, query, grad, out, keyvalue, keyvalue, totals_in, first, place)


def strip_of(ref, index, strip):
    return ref[:, pl.ds(pl.multiple_of(index * strip, strip), strip)]


def rate_of(value):
    return lax.rsqrt(jnp.mean(value * value, axis=-1, keepdims=True) + EPSILON)


def norm_one_kernel(near, tokens_ref, gain_ref, normed_ref, near_ref):
    value = tokens_ref[...].astype(F32)
    normed_ref[...] = (value * rate_of(value) * gain_ref[...]).astype(BF16)
    strip = value.shape[1] // near.shape[0]
    for j in range(near.shape[0]):
        near_ref[:, j * strip : (j + 1) * strip] = strip_of(normed_ref, near[j], strip)


def norm_two_kernel(place, tokens_ref, attended_ref, gain_ref, residual_ref, normed_ref):
    strip = tokens_ref.shape[1] // place.shape[0]
    for i in range(place.shape[0]):
        columns = slice(i * strip, (i + 1) * strip)
        residual_ref[:, columns] = tokens_ref[:, columns].astype(F32) + strip_of(attended_ref, place[i], strip)
    value = residual_ref[...]
    normed_ref[...] = (value * rate_of(value) * gain_ref[...]).astype(BF16)


def norm_back(value, gain, grad):
    rate = rate_of(value)
    normed = value * rate
    scaled = grad * gain
    back = rate * (scaled - normed * jnp.mean(scaled * normed, axis=-1, keepdims=True))
    return back, jnp.sum(grad * normed, axis=0, keepdims=True)


def add_up(ref, value):
    @pl.when(pl.program_id(0) == 0)
    def _():
        ref[...] = jnp.zeros_like(ref)

    ref[...] += value


def back_two_kernel(near, grad_ref, residual_ref, cotangent_ref, gain_ref, out_ref, near_ref, gain_grad_ref):
    back, gain_grad = norm_back(residual_ref[...], gain_ref[...], grad_ref[...])
    out_ref[...] = cotangent_ref[...].astype(F32) + back
    add_up(gain_grad_ref, gain_grad)
    strip = grad_ref.shape[1] // near.shape[0]
    for j in range(near.shape[0]):
        near_ref[:, j * strip : (j + 1) * strip] = strip_of(out_ref, near[j], strip).astype(BF16)


def back_one_kernel(place, grad_ref, near_ref, tokens_ref, above_ref, gain_ref, out_ref, gain_grad_ref):
    strip = tokens_ref.shape[1] // place.shape[0]
    for i in range(place.shape[0]):
        columns = slice(i * strip, (i + 1) * strip)
        out_ref[:, columns] = grad_ref[:, columns] + strip_of(near_ref, place[i], strip)
    back, gain_grad = norm_back(tokens_ref[...].astype(F32), gain_ref[...], out_ref[...])
    out_ref[...] = above_ref[...] + back
    add_up(gain_grad_ref, gain_grad)


def by_tokens(kernel, table, arrays, gain, outs, gain_grad=False):
    tokens, width = arrays[0].shape
    block = tokens // 3
    tile = pl.BlockSpec((block, width), lambda i, *_: (i, 0))
    line = pl.BlockSpec((1, width), lambda i, *_: (0, 0))
    spec = pltpu.PrefetchScalarGridSpec(
        num_scalar_prefetch=1,
        grid=(3,),
        in_specs=[tile] * len(arrays) + [line],
        out_specs=[tile] * len(outs) + [line] * gain_grad,
    )
    shapes = [jax.ShapeDtypeStruct((tokens, width), t) for t in outs]
    shapes += [jax.ShapeDtypeStruct((1, width), F32)] * gain_grad
    return pl.pallas_call(
        kernel,
        grid_spec=spec,
        out_shape=shapes,
        compiler_params=pltpu.CompilerParams(dimension_semantics=("arbitrary",), vmem_limit_bytes=40 * 2**20),
        cost_estimate=pl.CostEstimate(flops=16 * tokens * width, bytes_accessed=16 * tokens * width, transcendentals=0),
    )(table, *arrays, gain[None, :])


def unfold_kernel(place, total_ref, key_ref, value_ref, small_ref):
    width = key_ref.shape[0]
    strip = total_ref.shape[1] // place.shape[0]
    for i in range(place.shape[0]):
        columns = slice(i * strip, (i + 1) * strip)
        block = strip_of(total_ref, place[i], strip).astype(F32)
        key_ref[:, columns] = block[:width]
        value_ref[:, columns] = block[width : 2 * width]
        small_ref[:, columns] = block[2 * width : 2 * width + 16]


def unfold(place, total, width):
    model = total.shape[1]
    spec = pltpu.PrefetchScalarGridSpec(
        num_scalar_prefetch=1,
        grid=(1,),
        in_specs=[pl.BlockSpec(total.shape, lambda i, *_: (0, 0))],
        out_specs=[
            pl.BlockSpec((width, model), lambda i, *_: (0, 0)),
            pl.BlockSpec((width, model), lambda i, *_: (0, 0)),
            pl.BlockSpec((16, model), lambda i, *_: (0, 0)),
        ],
    )
    return pl.pallas_call(
        unfold_kernel,
        grid_spec=spec,
        out_shape=[
            jax.ShapeDtypeStruct((width, model), F32),
            jax.ShapeDtypeStruct((width, model), F32),
            jax.ShapeDtypeStruct((16, model), F32),
        ],
        compiler_params=pltpu.CompilerParams(dimension_semantics=("arbitrary",), vmem_limit_bytes=40 * 2**20),
    )(place, total)


def head_forward(projected, gain, turn):
    cosine, sine = turn
    half = HEAD_DIM // 2
    rate = lax.rsqrt(jnp.mean(projected * projected, axis=1, keepdims=True) + EPSILON)
    value = projected * rate * gain[:, None]
    low, high = value[:, :half], value[:, half:]
    return jnp.concatenate([low * cosine - high * sine, low * sine + high * cosine], axis=1)


def head_back(projected, gain, turn, grad):
    cosine, sine = turn
    half = HEAD_DIM // 2
    low, high = grad[:, :half], grad[:, half:]
    grad = jnp.concatenate([low * cosine + high * sine, high * cosine - low * sine], axis=1)
    rate = lax.rsqrt(jnp.mean(projected * projected, axis=1, keepdims=True) + EPSILON)
    normed = projected * rate
    scaled = grad * gain[:, None]
    back = rate * (scaled - normed * jnp.mean(scaled * normed, axis=1, keepdims=True))
    return back, jnp.sum(grad * normed, axis=(0, 2))


def paired():
    return lax.axis_size("tp") == 2 and lax.axis_size("row") == 2


def plane_sum(value):
    return lax.psum_scatter(value, ("row", "core", "tp"), scatter_dimension=0, tiled=True)


def both_cores(chunk):
    return jnp.concatenate([chunk, swap(chunk, "core")])


def other_half(part):
    return part[part.shape[0] // 2 :]


def own_half(part, got):
    return part[: part.shape[0] // 2].astype(F32) + got.astype(F32)


def far_hops(far):
    middle = far.shape[0] // 2
    return swap(far[:middle], "row"), swap(far[middle:], "tp")


def near_sends(near, hop_y, hop_x):
    half = near.shape[0] // 2
    return (
        (near[:half] + hop_y[half:].astype(F32)).astype(BF16),
        (near[half:] + hop_x[half:].astype(F32)).astype(BF16),
    )


def plane_total(own, hop_y, hop_x, top_x, bottom_y):
    half = own.shape[0] // 2
    return own + jnp.concatenate(
        [hop_y[:half].astype(F32) + top_x.astype(F32), hop_x[:half].astype(F32) + bottom_y.astype(F32)]
    )


def stage(*values):
    return lax.optimization_barrier(values)


def body(
    tokens, cotangent, lengths, head_counts, norm1_gain, norm2_gain, q_gain, k_gain,
    w_query, w_key, w_value, w_out, w_gate, w_up, w_down,
):
    pack, span, width = tokens.shape
    rows, cores, ctx, tp = (lax.axis_size(a) for a in ("row", "core", "ctx", "tp"))
    own_tokens = pack * span
    slot_count = w_query.shape[1] // HEAD_DIM
    all_slots = slot_count * tp
    devices = rows * cores * ctx
    strip = width // devices
    row_index, core_index, ctx_index, tp_index = (lax.axis_index(a) for a in ("row", "core", "ctx", "tp"))

    plane = rows * cores

    def ordered(mine, other, index):
        first = index == 0
        return jnp.where(first, mine, other), jnp.where(first, other, mine)

    part = w_gate.shape[1] // plane
    down_turned = w_down.T

    def first_hop(pick):
        mine = jnp.stack([pick(r, core_index) for r in range(rows)])
        return mine, swap(jnp.stack([pick(r, 1 - core_index) for r in range(rows)]), "core")

    def second_hop(mine, got):
        both = ordered(mine, got, core_index)
        mine = jnp.stack([lax.dynamic_index_in_dim(x, row_index, 0, False) for x in both])
        got = swap(jnp.stack([lax.dynamic_index_in_dim(x, 1 - row_index, 0, False) for x in both]), "row")
        low, high = ordered(mine, got, row_index)
        return jnp.concatenate([low, high])

    def pick_columns(r, c):
        return jnp.concatenate(
            [lax.dynamic_slice_in_dim(w, (r * cores + c) * part, part, 1) for w in (w_gate, w_up, down_turned)]
        )

    def by_weight(blocks, first, last):
        return jnp.concatenate([blocks[:, i * strip : (i + 1) * strip] for i in range(first, last)])

    def row_out(grad):
        view = grad.reshape(rows, cores, *grad.shape[1:])
        mine = lax.dynamic_index_in_dim(view, row_index, 0, False)
        got = swap(lax.dynamic_index_in_dim(view, 1 - row_index, 0, False), "row")
        return jnp.stack(ordered(mine, got, row_index))

    def core_out(both):
        mine = lax.dynamic_index_in_dim(both, core_index, 1, False)
        got = swap(lax.dynamic_index_in_dim(both, 1 - core_index, 1, False), "core")
        low, high = ordered(mine, got, core_index)
        return [x for r in range(rows) for x in (low[r], high[r])]

    def from_tp(value, axis):
        if tp == 2:
            return join(value, "tp", axis)
        return lax.all_gather(value, "tp", axis=axis, tiled=True)

    def up(value):
        return lax.ppermute(value, "ctx", [(i, i + 1) for i in range(ctx - 1)])

    def beside(value):
        if tp == 2:
            return jnp.stack([value, swap(value, "tp")])
        return lax.all_gather(value, "tp", axis=0)

    length = span * tp * ctx
    first_end = lengths[:, 0:1]
    second_end = first_end + lengths[:, 1:2]
    own_start = (ctx_index * tp + tp_index) * span
    places = own_start + jnp.arange(span, dtype=jnp.int32)[None, :]
    begins = jnp.where(places >= second_end, second_end, jnp.where(places >= first_end, first_end, 0))
    angles_of = (places - begins).astype(F32)
    frequency = jnp.exp(jnp.arange(HEAD_DIM // 2).astype(F32) * (-2.0 * math.log(THETA) / HEAD_DIM))
    angles = frequency[:, None] * angles_of.reshape(1, own_tokens)
    turn = (jnp.cos(angles), jnp.sin(angles))
    offsets = [jnp.int32(0)]
    for i in range(tp):
        offsets.append(offsets[-1] + head_counts[i])
    heads = jnp.arange(HEADS, dtype=jnp.int32)
    slots = jnp.zeros((HEADS,), jnp.int32)
    for i in range(tp):
        inside = (heads >= offsets[i]) & (heads < offsets[i + 1])
        holder = jnp.bitwise_xor(i, tp_index) if tp == 2 else i
        slots = jnp.where(inside, holder * slot_count + heads - offsets[i], slots)
    ranks = jnp.arange(devices, dtype=jnp.int32)
    near_strips = (
        (jnp.bitwise_xor(ranks // ctx % rows, row_index) * cores + jnp.bitwise_xor(ranks // (ctx * rows), core_index))
        * ctx + jnp.bitwise_xor(ranks % ctx, ctx_index)
    )
    strip_places = (
        (jnp.bitwise_xor(ranks // ctx % cores, core_index) * rows + jnp.bitwise_xor(ranks // (ctx * cores), row_index))
        * ctx + jnp.bitwise_xor(ranks % ctx, ctx_index)
    )
    blocks = ctx * tp
    steps = jnp.arange(blocks, dtype=jnp.int32) // tp
    partner = jnp.arange(blocks, dtype=jnp.int32) % tp
    if tp == 2:
        partner = jnp.bitwise_xor(partner, tp_index)
    starts = ((ctx_index - steps) * tp + partner) * span
    seen = (starts[None, :] >= 0) & (starts[None, :] <= own_start) & (starts[None, :] + span > begins[:, :1])
    counts = jnp.sum(seen.astype(jnp.int32), axis=1)
    turns = jnp.sum(
        (seen[:, None, :] & (jnp.arange(blocks)[None, None, :] < jnp.arange(blocks)[None, :, None])).astype(jnp.int32),
        axis=2,
    )
    order = jnp.sum(
        jnp.where(
            seen[:, None, :] & (turns[:, None, :] == jnp.arange(blocks)[None, :, None]),
            jnp.arange(blocks, dtype=jnp.int32)[None, None, :],
            0,
        ),
        axis=2,
    )
    tables = (
        order,
        counts,
        starts,
        slots,
        jnp.concatenate([begins] * GROUP, axis=1)[:, None, :],
        jnp.concatenate([places] * GROUP, axis=1),
    )

    half = own_tokens // 2
    two = paired()
    key_value = jnp.concatenate([w_key, w_value], axis=1)
    flat = tokens.reshape(own_tokens, width)
    grad_low = cotangent.reshape(own_tokens, width)
    normed_one, normed_near = by_tokens(norm_one_kernel, near_strips, [flat], norm1_gain, [BF16, BF16])
    kv_width = KVH * HEAD_DIM
    projected = dot(key_value, normed_one, (0, 1))
    key_proj = projected[:kv_width].reshape(KVH, HEAD_DIM, own_tokens)
    key_low = head_forward(key_proj, k_gain, turn).astype(BF16).reshape(kv_width, own_tokens)
    own_kv = jnp.concatenate([key_low, projected[kv_width:].astype(BF16)])

    mine, got = first_hop(pick_columns)
    query_part = join(w_query, "ctx", 0)
    out_part = join(w_out, "ctx", 1)
    got, query_part, out_part, own_kv = stage(got, query_part, out_part, own_kv)

    packed = second_hop(mine, got)
    going, arrived = up(own_kv), [beside(own_kv)]
    query_part = join(query_part, "ctx", 0, 2)
    packed, going, arrived[0], query_part = stage(packed, going, arrived[0], query_part)
    gate_up = lax.all_gather(by_weight(packed, 0, 2), "ctx", axis=1, tiled=True)

    arrived.append(beside(going))
    going = up(going)
    query_part = join(query_part, "row", 0)
    going, arrived[1], query_part, packed = stage(going, arrived[1], query_part, packed)

    arrived.append(beside(going))
    going = up(going)
    query_part = from_tp(query_part, 1)
    out_part = join(out_part, "ctx", 1, 2)
    going, arrived[2], query_part, out_part, packed = stage(going, arrived[2], query_part, out_part, packed)

    arrived.append(beside(going))
    query_full = join(query_part, "core", 0)
    out_part = join(out_part, "row", 1)
    arrived[3], query_full, out_part, packed = stage(arrived[3], query_full, out_part, packed)
    keyvalue = jnp.concatenate(arrived)

    query_proj = dot(query_full, normed_near, (0, 1)).reshape(all_slots, HEAD_DIM, own_tokens)
    query_low = head_forward(query_proj, q_gain, turn).astype(BF16)
    out_low, totals = attend(query_low, keyvalue, tables)
    out_part = from_tp(out_part, 0)
    top, bottom = grad_low[:half], grad_low[half:]
    grad_near = (swap(top, "tp"), swap(bottom, "row")) if two else (top, bottom)
    out_low, totals, out_part, grad_near, packed = stage(out_low, totals, out_part, grad_near, packed)
    down_full = lax.all_gather(by_weight(packed, 2, 3), "ctx", axis=1, tiled=True)
    out_full = join(out_part, "core", 1)
    out_flat = out_low.reshape(all_slots * HEAD_DIM, own_tokens)
    attended = dot(out_flat, out_full, (0, 0))
    residual, normed_two = by_tokens(norm_two_kernel, strip_places, [flat, attended], norm2_gain, [F32, BF16])
    normed_two, residual, out_full = stage(normed_two, residual, out_full)

    def forward(chunk):
        gate, up_proj = dot(chunk, gate_full, (1, 0)), dot(chunk, up_full, (1, 0))
        return gate, up_proj, (gate * jax.nn.sigmoid(gate) * up_proj).astype(BF16)

    if two:
        top, bottom = normed_two[:half], normed_two[half:]
        near = swap(top, "tp"), swap(bottom, "row")
        normed_all = [both_cores(normed_two)]
        near, normed_all[0] = stage(near, normed_all[0])
        far = swap(jnp.concatenate([top, near[0]]), "row"), swap(jnp.concatenate([bottom, near[1]]), "tp")
        normed_all.append(both_cores(jnp.concatenate(near)))
        far, normed_all, gate_up = stage(far, normed_all, gate_up)
    gate_full, up_full = (gate_up[i * plane : (i + 1) * plane].reshape(width, part) for i in range(2))
    if two:
        top, bottom = grad_low[:half], grad_low[half:]
        normed_all.append(both_cores(jnp.concatenate(far)))
        ready = [forward(x) for x in normed_all]
        grad_far = (
            swap(jnp.concatenate([top, grad_near[0]]), "row"), swap(jnp.concatenate([bottom, grad_near[1]]), "tp")
        )
        grad_all = [both_cores(grad_low), both_cores(jnp.concatenate(grad_near))]
        ready, grad_far, grad_all, normed_all = stage(ready, grad_far, grad_all, normed_all)
        grad_all.append(both_cores(jnp.concatenate(grad_far)))
    else:
        normed_all = [lax.all_gather(normed_two, ("row", "core", "tp"), axis=0, tiled=True)]
        grad_all = [lax.all_gather(grad_low, ("row", "core", "tp"), axis=0, tiled=True)]
        ready = [forward(normed_all[0])]
    chunks = range(len(normed_all))
    hidden = [x[2] for x in ready]

    def column_gradient(values, grads):
        summed = sum(dot(values[i], grads[i], (0, 0)) for i in chunks)
        return summed.astype(BF16).reshape(plane, strip * ctx, part)

    grad_down = column_gradient(grad_all, hidden)
    grad_down, gate_full, up_full, down_full, ready, grad_all = stage(
        grad_down, gate_full, up_full, down_full, ready, grad_all
    )
    down_full = down_full.reshape(width, part)
    grad_down = lax.psum_scatter(grad_down, "ctx", scatter_dimension=1, tiled=True)
    hidden = [x[2] for x in ready]

    def hidden_grads(i):
        gate, up_proj, _ = ready[i]
        sigmoid_gate = jax.nn.sigmoid(gate)
        grad_hidden = dot(grad_all[i], down_full, (1, 0))
        return (
            (grad_hidden * up_proj * sigmoid_gate * (1.0 + gate * (1.0 - sigmoid_gate))).astype(BF16),
            (grad_hidden * gate * sigmoid_gate).astype(BF16),
        )

    def input_part(grads):
        return (dot(grads[0], gate_full, (1, 1)) + dot(grads[1], up_full, (1, 1))).astype(BF16)

    def column_part(kind, values, pairs):
        return sum(dot(values[i], pairs[i][kind], (0, 0)) for i in chunks[:-1]) if two else 0.0

    def column_rest(kind, values, pairs, summed):
        summed = summed + dot(values[-1], pairs[-1][kind], (0, 0))
        return summed.astype(BF16).reshape(plane, strip * ctx, part)

    def output_part(i):
        return dot(hidden[i], down_full, (1, 1)).astype(BF16)

    grads = [None] * len(chunks)
    if two:
        grads[2] = hidden_grads(2)
        far_part = input_part(grads[2])
        grads[2], far_part, far_send, grad_all = stage(grads[2], far_part, other_half(far_part), grad_all)
        far = own_half(far_part, swap(far_send, "core")).astype(BF16)
        grads[1] = hidden_grads(1)
        far, grads[1], grad_all = stage(far, grads[1], grad_all)
        hops = far_hops(far)
        near_part = input_part(grads[1])
        grads[0] = hidden_grads(0)
        own_part = input_part(grads[0])
        hops, near_part, own_part, grads, hidden = stage(hops, near_part, own_part, grads, hidden)
        near = own_half(near_part, swap(other_half(near_part), "core"))
        own = own_half(own_part, swap(other_half(own_part), "core"))
        sends = near_sends(near, *hops)
        far_part = output_part(2)
        sends, own, far_part, normed_all = stage(sends, own, far_part, normed_all)
        top_x, bottom_y = swap(sends[0], "tp"), swap(sends[1], "row")
        output_far = own_half(far_part, swap(other_half(far_part), "core")).astype(BF16)
        gate_parts = column_part(0, normed_all, grads)
        top_x, bottom_y, output_far, grads, normed_all, gate_parts = stage(
            top_x, bottom_y, output_far, grads, normed_all, gate_parts
        )
        output_hops = far_hops(output_far)
        grad_normed_two = plane_total(own, *hops, top_x, bottom_y)
    else:
        grads[0] = hidden_grads(0)
        gate_parts = column_part(0, normed_all, grads)
        grad_normed_two = plane_sum(input_part(grads[0])).astype(F32)
        output_hops = grad_normed_two
    grad_residual, grad_attn, grad_norm_two = by_tokens(
        back_two_kernel, near_strips, [grad_normed_two, residual, grad_low], norm2_gain, [F32, BF16], True
    )

    grad_out = dot(out_full, grad_attn, (1, 1)).astype(BF16).reshape(all_slots, HEAD_DIM, own_tokens)
    grad_query, grad_kv = attend_back(query_low, grad_out, out_low, keyvalue, totals, tables)
    grad_out_w = dot(out_flat, grad_attn, (1, 0)).astype(BF16)
    grad_out_w = fold(grad_out_w, "core", 1)
    output_hops, grad_query, grad_kv, grads, grad_out_w, grad_down = stage(
        output_hops, grad_query, grad_kv, grads, grad_out_w, grad_down
    )
    grad_kv = grad_kv.reshape(ctx, tp, 2 * kv_width, own_tokens)

    def to_tp(value, axis):
        if tp == 2:
            return fold(value, "tp", axis)
        return lax.psum_scatter(value, "tp", scatter_dimension=axis, tiled=True)

    def to_owner(value):
        if tp == 2:
            return value[0].astype(F32) + swap(value[1], "tp").astype(F32)
        return lax.psum_scatter(value, "tp", scatter_dimension=0, tiled=False).astype(F32)

    def down(value):
        return lax.ppermute(value.astype(BF16), "ctx", [(j, j - 1) for j in range(1, ctx)]).astype(F32)

    summed = to_owner(grad_kv[ctx - 1])
    grad_gate_w = column_rest(0, normed_all, grads, gate_parts)
    out_w_low, out_w_high = grad_out_w[: all_slots * 32], grad_out_w[all_slots * 32 :]
    out_w_low = fold(out_w_low, "row", 1)
    summed, grad_gate_w, grad_kv, grad_query, out_w_low, out_w_high, normed_all, grads = stage(
        summed, grad_gate_w, grad_kv, grad_query, out_w_low, out_w_high, normed_all, grads
    )
    grad_gate_w = lax.psum_scatter(grad_gate_w, "ctx", scatter_dimension=1, tiled=True)

    summed = to_owner(grad_kv[2]) + down(summed)
    up_parts = column_part(1, normed_all, grads)
    out_w_high = fold(out_w_high, "row", 1)
    summed, grad_kv, grad_query, out_w_low, out_w_high, normed_all, grads, up_parts = stage(
        summed, grad_kv, grad_query, out_w_low, out_w_high, normed_all, grads, up_parts
    )

    summed = to_owner(grad_kv[1]) + down(summed)
    grad_up_w = column_rest(1, normed_all, grads, up_parts)
    grad_query_proj, grad_q_gain = head_back(query_proj, q_gain, turn, grad_query)
    grad_query_low = grad_query_proj.astype(BF16).reshape(all_slots * HEAD_DIM, own_tokens)
    grad_down = row_out(grad_down)
    summed, grad_query_low, grad_q_gain, grad_kv, grad_up_w, grad_gate_w, grad_down, out_w_low, out_w_high = stage(
        summed, grad_query_low, grad_q_gain, grad_kv, grad_up_w, grad_gate_w, grad_down, out_w_low, out_w_high
    )
    grad_up_w = lax.psum_scatter(grad_up_w, "ctx", scatter_dimension=1, tiled=True)

    summed = to_owner(grad_kv[0]) + down(summed)
    grad_query_w = dot(normed_near, grad_query_low, (0, 1)).astype(BF16)
    grad_query_w = fold(grad_query_w, "core", 0)
    grad_down = core_out(grad_down)
    grad_gate_w = row_out(grad_gate_w)
    summed, grad_query_w, grad_query_low, grad_down, grad_gate_w, out_w_low, out_w_high = stage(
        summed, grad_query_w, grad_query_low, grad_down, grad_gate_w, out_w_low, out_w_high
    )

    grad_normed_near = dot(grad_query_low, query_full, (0, 1))
    grad_gate_w = core_out(grad_gate_w)
    grad_key_proj, grad_k_gain = head_back(
        key_proj, k_gain, turn, summed[:kv_width].reshape(KVH, HEAD_DIM, own_tokens)
    )
    grad_kv_low = jnp.concatenate(
        [grad_key_proj.reshape(kv_width, own_tokens).astype(BF16), summed[kv_width:].astype(BF16)]
    )
    padded = jnp.pad(grad_kv_low, ((0, 32), (0, 0)))
    total = dot(padded, normed_near if two else normed_one, (1, 0))
    grad_normed_one = dot(grad_kv_low, key_value, (0, 1))
    grad_inputs, grad_norm_one = by_tokens(
        back_one_kernel, strip_places, [grad_normed_one, grad_normed_near, flat, grad_residual], norm1_gain, [F32], True
    )
    gains = jnp.concatenate([grad_q_gain, grad_k_gain, jnp.zeros((width - 2 * HEAD_DIM,), F32)])
    small = jnp.concatenate([grad_norm_one, grad_norm_two, gains[None]])
    moved = (near_strips if two else ranks)[:, None] == ranks[None, :]
    small = jnp.sum(
        jnp.where(moved[None, :, :, None], small.reshape(3, 1, devices, strip), 0.0), axis=2
    ).reshape(3, width)
    total = lax.dynamic_update_slice(total, small, (2 * kv_width, 0)).astype(BF16)
    query_w_low, query_w_high = grad_query_w[:, : all_slots * 32], grad_query_w[:, all_slots * 32 :]
    query_w_low = fold(query_w_low, "row", 0)
    grad_out_w = to_tp(jnp.concatenate([out_w_low, out_w_high]), 0)
    total, query_w_low, query_w_high, grad_out_w, grad_gate_w, hidden = stage(
        total, query_w_low, query_w_high, grad_out_w, grad_gate_w, hidden
    )

    if not two:
        total = lax.psum(total, ("row", "core", "ctx", "tp"))
        output = residual + plane_sum(output_part(0)).astype(F32)
        grad_query_w = jnp.concatenate([query_w_low, fold(query_w_high, "row", 0)], axis=1)
        grad_query_w = to_tp(grad_query_w, 1)
        grad_query_w = fold(fold(grad_query_w, "ctx", 0, 2), "ctx", 0)
        grad_out_w = fold(fold(grad_out_w, "ctx", 1, 2), "ctx", 1)
        grad_up_w = core_out(row_out(grad_up_w))
    else:
        total = fold(total, "core", 1)
        near_part = output_part(1)
        query_w_high = fold(query_w_high, "row", 0)
        total, near_part, query_w_low, query_w_high, grad_out_w = stage(
            total, near_part, query_w_low, query_w_high, grad_out_w
        )
        size = total.shape[0] // 2
        got = swap(lax.dynamic_slice_in_dim(total, (1 - tp_index) * size, size, 0), "tp")
        total = sum32(lax.dynamic_slice_in_dim(total, tp_index * size, size, 0), got)
        own_part = output_part(0)
        near = own_half(near_part, swap(other_half(near_part), "core"))
        grad_out_w = fold(grad_out_w, "ctx", 1, 2)
        total, grad_out_w, query_w_low, query_w_high, own_part, near = stage(
            total, grad_out_w, query_w_low, query_w_high, own_part, near
        )
        total = fold(total, "row", 1)
        grad_query_w = fold(jnp.concatenate([query_w_low, query_w_high], axis=1), "tp", 1)
        own = own_half(own_part, swap(other_half(own_part), "core"))
        total, grad_query_w, own, grad_out_w = stage(total, grad_query_w, own, grad_out_w)
        total = fold(total, "ctx", 1, 2)
        sends = near_sends(near, *output_hops)
        top_x, bottom_y = swap(sends[0], "tp"), swap(sends[1], "row")
        grad_out_w = fold(grad_out_w, "ctx", 1)
        total, top_x, bottom_y, grad_query_w, grad_out_w = stage(total, top_x, bottom_y, grad_query_w, grad_out_w)
        total = fold(total, "ctx", 1)
        grad_query_w = fold(grad_query_w, "ctx", 0, 2)
        total, grad_query_w, grad_up_w = stage(total, grad_query_w, grad_up_w)
        total = join(total, "ctx", 1)
        output = residual + plane_total(own, *output_hops, top_x, bottom_y)
        grad_up_w = row_out(grad_up_w)
        total, grad_query_w, grad_up_w, output = stage(total, grad_query_w, grad_up_w, output)
        total = join(total, "ctx", 1, 2)
        total, grad_query_w, grad_up_w = stage(total, grad_query_w, grad_up_w)
        total = join(total, "row", 1)
        grad_query_w = fold(grad_query_w, "ctx", 0)
        grad_up_w = core_out(grad_up_w)
        total, grad_query_w, grad_up_w = stage(total, grad_query_w, grad_up_w)
        other = swap(total, "tp")
        first = tp_index == 0
        total = jnp.concatenate([jnp.where(first, total, other), jnp.where(first, other, total)])
        (total,) = stage(total)
        total = join(total, "core", 1)
    grad_key_w, grad_value_w, small = unfold(strip_places if two else ranks, total, kv_width)

    return (
        output.astype(BF16).reshape(pack, span, width),
        grad_inputs.reshape(pack, span, width),
        small[0],
        small[1],
        small[2, :HEAD_DIM],
        small[2, HEAD_DIM : 2 * HEAD_DIM],
        grad_query_w.astype(F32),
        grad_key_w.T,
        grad_value_w.T,
        grad_out_w.astype(F32),
        jnp.concatenate(grad_gate_w, axis=1).astype(F32),
        jnp.concatenate(grad_up_w, axis=1).astype(F32),
        jnp.concatenate([x.T for x in grad_down]).astype(F32),
    )


def solution(mesh):
    dp, ctx, tp = (mesh.shape[a] for a in ("dp", "ctx", "tp"))
    split = Mesh(mesh.devices.reshape(dp // 2, 2, ctx, tp), ("row", "core", "ctx", "tp"))
    dp = ("row", "core")
    every = ("row", "core", "ctx")
    token = P(dp, ("ctx", "tp"), None)
    by_row, by_column = P(every, "tp"), P("tp", every)
    return jax.shard_map(
        body,
        mesh=split,
        in_specs=(
            token, token, P(dp, None), P(), P(), P(), P(), P(),
            by_row, P(), P(), by_column, by_row, by_row, by_column,
        ),
        out_specs=(
            token, token, P(), P(), P(), P(),
            by_row, P(), P(), by_column, by_row, by_row, by_column,
        ),
        check_vma=False,
    )
```

time: 3390 us -> 1010 us (0.30)
  waiting for transfers between devices: 1500 us -> 364 us
  local copies, waits for them, and re-layouts: 1170 us -> 111 us
  matrix products: 558 us -> 229 us
  starting transfers between devices: 1.87 us -> 85 us
  other arithmetic: 78.3 us -> 161 us
  blocking collectives: 40.2 us -> 0 us
  Pallas kernels: 0 us -> 34.8 us
    unnamed x159 -> x318, local copies, waits for them, and re-layouts: 995 us -> 48.5 us
    all_gather x11 -> x2, waiting for transfers between devices: 694 us -> 28.1 us  [the longest x1 28.1 us: body(): gate_up = lax.all_gather(by_weight(packed, 0, 2), 'ctx', axis=1, tiled=True)]
    reduce_scatter x7 -> x3, waiting for transfers between devices: 660 us -> 30.8 us  [the longest x1 17.7 us: body(): lax.psum_scatter(grad_down, 'ctx', scatter_dimension=1, tiled=True)]
    dot_general x193 -> x36, matrix products: 558 us -> 229 us  [dot(): lax.dot_general(left, right, ((contract[:1], contract[1:]), ((), ())), pr...]
    ppermute x0 -> x82, waiting for transfers between devices: none -> 305 us  [the longest x76 262 us: swap(): return lax.ppermute(value, axis, [(i, i ^ bit) for i in range(size)])]
    psum x1 -> x0, waiting for transfers between devices: 147 us -> none  [body(): lax.psum((grad_key_w, grad_value_w, grad_norm_one, grad_norm_two, grad_q_...]
    ppermute x0 -> x82, starting transfers between devices: none -> 84.6 us  [the longest x76 69.1 us: swap(): return lax.ppermute(value, axis, [(i, i ^ bit) for i in range(size)])]
    concatenate x1 -> x31, other arithmetic: 0.08 us -> 48.3 us  [the longest x13 18 us: join(): return jnp.concatenate([value, swap(value, axis, bit)], axis=dimension)]
  transfers between devices with their start and end apart: 23 -> 87, of which waited for: 18 -> 39; matrix products, arithmetic and copies ran while one was open for 21% -> 38% of each run, Pallas kernels for 0% -> 3%
where the time goes in v1:
time: 1010 us; the launch traced here: 1000 us
  waiting for transfers between devices  364 us (36%)
  matrix products  229 us (23%)
  other arithmetic  161 us (16%)
  local copies, waits for them, and re-layouts  111 us (11%)
  starting transfers between devices  85 us (8%)
  Pallas kernels  34.8 us (3%)
  between operations  18 us (2%)
    ppermute x76, waiting for transfers between devices, swap(): return lax.ppermute(value, axis, [(i, i ^ bit) for i in range(size)])  262 us
    dot_general x36, matrix products, dot(): lax.dot_general(left, right, ((contract[:1], contract[1:]), ((), ())), pr...  229 us
    ppermute x76, starting transfers between devices, swap(): return lax.ppermute(value, axis, [(i, i ^ bit) for i in range(size)])  69.1 us
    unnamed x318, local copies, waits for them, and re-layouts  48.5 us
    ppermute x3, waiting for transfers between devices, down(): lax.ppermute(value.astype(BF16), 'ctx', [(j, j - 1) for j in range(1, ctx)])  43 us
    all_gather x1, waiting for transfers between devices, body(): gate_up = lax.all_gather(by_weight(packed, 0, 2), 'ctx', axis=1, tiled=True)  28.1 us
    convert_element_type x17, other arithmetic, sum32(): return (left.astype(F32) + right.astype(F32)).astype(BF16)  22 us
  transfers between devices with their start and end apart: 87, of which 39 were waited for; matrix products, arithmetic and copies ran while one was open for 38% of the time, Pallas kernels for 3%

profile of v1, /device:TPU:0, one launch (start us, length us, event | category | flops | bytes accessed | tf_op | source)
XLA Modules:
  0.0 1002.4 jit_solution(17715198131802383982)
XLA Ops:
  44.7 12.8 %collective-permute-done.6 = bf16[256,768]{1,0:T(8,128)(2,1)} collective-permute-done((bf16[256,768]{1,0:T(8,128)(2,1)}, bf16[256,768]{1,0:T(8,128)(2,1)}, u32[]{:S(2)}, u32[]{:S(2)}) %collective-permute-start.6) | collective-permute-done | bytes 393248 | tf_op jit(solution)/shard_map/ppermute | solution.py:31
  60.9 11.1 %collective-permute-done.3 = bf16[2,384,1024]{2,1,0:T(8,128)(2,1)} collective-permute-done((bf16[2,384,1024]{2,1,0:T(8,128)(2,1)}, bf16[2,384,1024]{2,1,0:T(8,128)(2,1)}, u32[]{:S(2)}, u32[]{:S(2)}) %collective-permute-start.3) | collective-permute-done | bytes 1572896 | tf_op jit(solution)/shard_map/ppermute | solution.py:31
  103.4 10.8 %collective-permute-done.13 = bf16[768,256]{1,0:T(8,128)(2,1)S(1)} collective-permute-done((bf16[768,256]{1,0:T(8,128)(2,1)S(1)}, bf16[768,256]{1,0:T(8,128)(2,1)S(1)}, u32[]{:S(2)}, u32[]{:S(2)}) %collective-permute-start.13) | collective-permute-done | bytes 393248 | tf_op jit(solution)/shard_map/ppermute | solution.py:31
  115.2 24.6 %collective-permute-done.11 = bf16[640,384]{1,0:T(8,128)(2,1)S(1)} collective-permute-done((bf16[640,384]{1,0:T(8,128)(2,1)S(1)}, bf16[640,384]{1,0:T(8,128)(2,1)S(1)}, u32[]{:S(2)}, u32[]{:S(2)}) %collective-permute-start.11) | collective-permute-done | bytes 491552 | tf_op jit(solution)/shard_map/ppermute | solution.py:31
  158.1 16.6 %collective-permute-done.14 = bf16[640,384]{1,0:T(8,128)(2,1)S(1)} collective-permute-done((bf16[640,384]{1,0:T(8,128)(2,1)}, bf16[640,384]{1,0:T(8,128)(2,1)S(1)}, u32[]{:S(2)}, u32[]{:S(2)}) %collective-permute-start.14) | collective-permute-done | bytes 491552 | tf_op jit(solution)/shard_map/ppermute | solution.py:31
  206.8 18.8 %collective-permute-done.17 = bf16[768,1024]{1,0:T(8,128)(2,1)S(1)} collective-permute-done((bf16[768,1024]{1,0:T(8,128)(2,1)S(1)}, bf16[768,1024]{1,0:T(8,128)(2,1)S(1)}, u32[]{:S(2)}, u32[]{:S(2)}) %collective-permute-start.17) | collective-permute-done | bytes 1572896 | tf_op jit(solution)/shard_map/ppermute | solution.py:31
  246.2 10.7 %collective-permute-done.21 = bf16[192,2048]{1,0:T(8,128)(2,1)S(1)} collective-permute-done((bf16[192,2048]{1,0:T(8,128)(2,1)S(1)}, bf16[192,2048]{1,0:T(8,128)(2,1)S(1)}, u32[]{:S(2)}, u32[]{:S(2)}) %collective-permute-start.21) | collective-permute-done | bytes 786464 | tf_op jit(solution)/shard_map/ppermute | solution.py:31
  275.5 28.1 %all-gather.3.cloned.1.call-done = bf16[8,512,1024]{2,1,0:T(8,128)(2,1)} async-done(((bf16[8,128,1024]{2,1,0:T(8,128)(2,1)}), bf16[8,512,1024]{2,1,0:T(8,128)(2,1)}) %all-gather.3.cloned.1.call-update) | async-done | bytes 8388624 | tf_op jit(solution)/shard_map/all_gather | solution.py:517
  343.3 13.8 %multiply_convert_fusion.2 = (bf16[1536,1024]{1,0:T(8,128)(2,1)}, f32[1536,1024]{1,0:T(8,128)}) fusion(f32[1536,1024]{1,0:T(8,128)S(1)} %fusion.45, bf16[1536,2048]{1,0:T(8,128)(2,1)} %copy-done.127, bf16[2048,1024]{1,0:T(8,128)(2,1)S(1)} %bitcast.309), kind=kOutput, calls=%fused_computation.17 | convolution fusion | flops 6451888128 | bytes 26214400 | tf_op jit(solution)/shard_map/dot_general | solution.py:26
  375.0 12.2 %add_convert_fusion.3 = bf16[2048,1024]{1,0:T(8,128)(2,1)} fusion(f32[2048,1024]{1,0:T(8,128)} %fusion.46, f32[2048,1024]{1,0:T(8,128)S(1)} %fusion.47, bf16[1536,2048]{1,0:T(8,128)(2,1)S(1)} %constant_dynamic-update-slice_fusion.11, bf16[1536,1024]{1,0:T(8,128)(2,1)} %get-tuple-element.318), kind=kOutput, calls=%fused_computation.3 | convolution fusion | flops 6448742400 | bytes 30408704 | tf_op jit(solution)/shard_map/dot_general | solution.py:26
  387.2 15.6 %multiply_convert_fusion = (bf16[1536,1024]{1,0:T(8,128)(2,1)S(1)}, bf16[1536,1024]{1,0:T(8,128)(2,1)}) fusion(f32[1536,1024]{1,0:T(8,128)} %copy-done.142, f32[1536,1024]{1,0:T(8,128)} %get-tuple-element.291, bf16[1536,2048]{1,0:T(8,128)(2,1)} %copy-done.128, bf16[2048,1024]{1,0:T(8,128)(2,1)} %bitcast.349), kind=kOutput, calls=%fused_computation.14 | convolution fusion | flops 6462898176 | bytes 29360128 | tf_op jit(solution)/shard_map/dot_general | solution.py:26
  411.8 10.9 %add_convert_fusion = bf16[1536,2048]{1,0:T(8,128)(2,1)S(1)} fusion(f32[1536,2048]{1,0:T(8,128)} %fusion.48, bf16[1536,1024]{1,0:T(8,128)(2,1)} %get-tuple-element.352, bf16[2048,1024]{1,0:T(8,128)(2,1)S(1)} %bitcast.304), kind=kOutput, calls=%fused_computation | convolution fusion | flops 6448742400 | bytes 26214400 | tf_op jit(solution)/shard_map/dot_general | solution.py:26
  469.5 17.2 %collective-permute-done.34 = bf16[384,2048]{1,0:T(8,128)(2,1)S(1)} collective-permute-done((bf16[384,2048]{1,0:T(8,128)(2,1)}, bf16[384,2048]{1,0:T(8,128)(2,1)S(1)}, u32[]{:S(2)}, u32[]{:S(2)}) %collective-permute-start.34) | collective-permute-done | bytes 1572896 | tf_op jit(solution)/shard_map/ppermute | solution.py:31
  548.4 12.4 %attend_back.1 = (f32[24,64,384]{2,1,0:T(8,128)S(1)}, bf16[8,2,320,384]{3,2,1,0:T(8,128)(2,1)}) custom-call(s32[2,8]{1,0:T(2,128)S(1)} %copy-done.29, s32[2]{0:T(128)S(1)} %copy-done.31, s32[8]{0:T(128)S(1)} %get-tuple-element.501.starts, s32[20]{0:T(128)S(1)} %copy-done.33, bf16[24,64,384]{2,1,0:T(8,128)(2,1)S(1)} %copy-done.14, ...), custom_call_target="tpu_custom_call" | custom-call | flops 30198988800 | bytes 16777216 | tf_op jit(solution)/shard_map/attend_back/pallas_call | solution.py:178
  568.2 17.7 %reduce-scatter.4.cloned.1.call-done = bf16[4,128,1024]{2,1,0:T(8,128)(2,1)} async-done(((bf16[4,512,1024]{2,1,0:T(8,128)(2,1)}), bf16[4,128,1024]{2,1,0:T(8,128)(2,1)}) %reduce-scatter.4.cloned.1.call-update) | async-done | bytes 1048592 | tf_op jit(solution)/shard_map/reduce_scatter | solution.py:589
  593.1 11.0 %fusion.54 = f32[2048,1024]{1,0:T(8,128)} fusion(bf16[1536,2048]{1,0:T(8,128)(2,1)} %copy-done.127, bf16[1536,1024]{1,0:T(8,128)(2,1)S(1)} %copy-done.144), kind=kOutput, calls=%fused_computation.320 | convolution fusion | flops 6442450944 | bytes 17825792 | tf_op jit(solution)/shard_map/dot_general | solution.py:26
  623.7 10.8 %collective-permute-done.51 = bf16[2,128,1024]{1,2,0:T(8,128)(2,1)} collective-permute-done((bf16[2,128,1024]{1,2,0:T(8,128)(2,1)}, bf16[2,128,1024]{1,2,0:T(8,128)(2,1)}, u32[]{:S(2)}, u32[]{:S(2)}) %collective-permute-start.51) | collective-permute-done | bytes 524320 | tf_op jit(solution)/shard_map/ppermute | solution.py:31
  650.7 17.0 %collective-permute-done.47 = bf16[640,384]{1,0:T(8,128)(2,1)S(1)} collective-permute-done((bf16[640,384]{1,0:T(8,128)(2,1)S(1)}, bf16[640,384]{1,0:T(8,128)(2,1)S(1)}, u32[]{:S(2)}, u32[]{:S(2)}) %collective-permute-start.47) | collective-permute-done | bytes 491552 | tf_op jit(solution)/shard_map/ppermute | solution.py:669
  678.4 11.8 %fusion.56 = f32[2048,1024]{1,0:T(8,128)} fusion(bf16[1536,2048]{1,0:T(8,128)(2,1)} %copy-done.127, bf16[1536,1024]{1,0:T(8,128)(2,1)} %copy-done.143), kind=kOutput, calls=%fused_computation.322 | convolution fusion | flops 6442450944 | bytes 17825792 | tf_op jit(solution)/shard_map/dot_general | solution.py:26
  699.7 22.8 %collective-permute-done.50 = bf16[640,384]{1,0:T(8,128)(2,1)} collective-permute-done((bf16[640,384]{1,0:T(8,128)(2,1)}, bf16[640,384]{1,0:T(8,128)(2,1)}, u32[]{:S(2)}, u32[]{:S(2)}) %collective-permute-start.50) | collective-permute-done | bytes 491552 | tf_op jit(solution)/shard_map/ppermute | solution.py:669
  724.8 13.1 %reduce-scatter.6.cloned.1.call-done = bf16[4,128,1024]{2,1,0:T(8,128)(2,1)} async-done(((bf16[4,512,1024]{2,1,0:T(8,128)(2,1)}), bf16[4,128,1024]{2,1,0:T(8,128)(2,1)}) %reduce-scatter.6.cloned.1.call-update) | async-done | bytes 1048592 | tf_op jit(solution)/shard_map/reduce_scatter | solution.py:678
  821.4 15.5 %collective-permute-done.61 = bf16[512,768]{1,0:T(8,128)(2,1)S(1)} collective-permute-done((bf16[512,768]{1,0:T(8,128)(2,1)S(1)}, bf16[512,768]{1,0:T(8,128)(2,1)S(1)}, u32[]{:S(2)}, u32[]{:S(2)}) %collective-permute-start.61) | collective-permute-done | bytes 786464 | tf_op jit(solution)/shard_map/ppermute | solution.py:31
  852.5 10.5 %collective-permute-done.63 = bf16[768,256]{1,0:T(8,128)(2,1)S(1)} collective-permute-done((bf16[768,256]{1,0:T(8,128)(2,1)S(1)}, bf16[768,256]{1,0:T(8,128)(2,1)S(1)}, u32[]{:S(2)}, u32[]{:S(2)}) %collective-permute-start.63) | collective-permute-done | bytes 393248 | tf_op jit(solution)/shard_map/ppermute | solution.py:31
  963.5 15.7 %collective-permute-done.80 = bf16[336,1024]{1,0:T(8,128)(2,1)} collective-permute-done((bf16[336,1024]{1,0:T(8,128)(2,1)S(1)}, bf16[336,1024]{1,0:T(8,128)(2,1)}, u32[]{:S(2)}, u32[]{:S(2)}) %collective-permute-start.80) | collective-permute-done | bytes 688160 | tf_op jit(solution)/shard_map/ppermute | solution.py:31
  (738 shorter events, 623.3 us)
Async XLA Ops:
  7.2 296.3 %all-gather.3.cloned.1.call-start = ((), (), s32[]{:S(2)}) async-start(), calls=%async_computation.3 | async-start | bytes 10485760 | tf_op jit(solution)/shard_map/all_gather | solution.py:517
  35.3 36.7 %collective-permute-start.3 = (bf16[2,384,1024]{2,1,0:T(8,128)(2,1)}, bf16[2,384,1024]{2,1,0:T(8,128)(2,1)}, u32[]{:S(2)}, u32[]{:S(2)}) collective-permute-start(bf16[2,384,1024]{2,1,0:T(8,128)(2,1)} %pad_maximum_fusion.20), channel_id=1, source_target_pairs={{0,16},{16,0},{1,17},{17,1},{2,18},{18,2},{3,19},{19,3},{4,20},{20... | collective-permute-start | bytes 4718600 | tf_op jit(solution)/shard_map/ppermute | solution.py:31
  41.2 34.5 %collective-permute-start.4 = (bf16[640,384]{1,0:T(8,128)(2,1)}, bf16[640,384]{1,0:T(8,128)(2,1)S(1)}, u32[]{:S(2)}, u32[]{:S(2)}) collective-permute-start(bf16[640,384]{1,0:T(8,128)(2,1)} %pad_maximum_fusion.37), channel_id=1, source_target_pairs={{0,2},{2,4},{4,6},{1,3},{3,5},{5,7},{8,10},{10,12},{12,14},{9,11},... | collective-permute-start | bytes 1474568 | tf_op jit(solution)/shard_map/ppermute | solution.py:432
  94.5 46.3 %collective-permute-start.12 = (bf16[1024,768]{1,0:T(8,128)(2,1)S(1)}, bf16[1024,768]{1,0:T(8,128)(2,1)S(1)}, u32[]{:S(2)}, u32[]{:S(2)}) collective-permute-start(bf16[1024,768]{1,0:T(8,128)(2,1)S(1)} %pad_maximum_fusion.21), channel_id=1, source_target_pairs={{0,1},{1,0},{2,3},{3,2},{4,5},{5,4},{6,7},{7,6},{8,9},{9,8},{10,11... | collective-permute-start | bytes 4718600 | tf_op jit(solution)/shard_map/ppermute | solution.py:31
  98.6 41.2 %collective-permute-start.11 = (bf16[640,384]{1,0:T(8,128)(2,1)S(1)}, bf16[640,384]{1,0:T(8,128)(2,1)S(1)}, u32[]{:S(2)}, u32[]{:S(2)}) collective-permute-start(bf16[640,384]{1,0:T(8,128)(2,1)S(1)} %collective-permute-done.7), channel_id=1, source_target_pairs={{0,1},{1,0},{2,3},{3,2},{4,5},{5,4},{6,7},{7,6},{8,9},{9,8},{10,11... | collective-permute-start | bytes 1474568 | tf_op jit(solution)/shard_map/ppermute | solution.py:31
  99.1 43.6 %collective-permute-start.10 = (bf16[640,384]{1,0:T(8,128)(2,1)S(1)}, bf16[640,384]{1,0:T(8,128)(2,1)}, u32[]{:S(2)}, u32[]{:S(2)}) collective-permute-start(bf16[640,384]{1,0:T(8,128)(2,1)S(1)} %collective-permute-done.7), channel_id=1, source_target_pairs={{0,2},{2,4},{4,6},{1,3},{3,5},{5,7},{8,10},{10,12},{12,14},{9,11},... | collective-permute-start | bytes 1474568 | tf_op jit(solution)/shard_map/ppermute | solution.py:432
  142.7 40.9 %collective-permute-start.15 = (bf16[1024,1536]{1,0:T(8,128)(2,1)}, bf16[1024,1536]{1,0:T(8,128)(2,1)}, u32[]{:S(2)}, u32[]{:S(2)}) collective-permute-start(bf16[1024,1536]{1,0:T(8,128)(2,1)} %pad_maximum_fusion.2), channel_id=1, source_target_pairs={{0,8},{8,0},{1,9},{9,1},{2,10},{10,2},{3,11},{11,3},{4,12},{12,4},... | collective-permute-start | bytes 9437192 | tf_op jit(solution)/shard_map/ppermute | solution.py:31
  144.0 81.9 %collective-permute-start.18 = (bf16[192,2048]{1,0:T(8,128)(2,1)}, bf16[192,2048]{1,0:T(8,128)(2,1)}, u32[]{:S(2)}, u32[]{:S(2)}) collective-permute-start(bf16[192,2048]{1,0:T(8,128)(2,1)} %get-tuple-element.543), channel_id=1, source_target_pairs={{0,1},{1,0},{2,3},{3,2},{4,5},{5,4},{6,7},{7,6},{8,9},{9,8},{10,11... | collective-permute-start | bytes 2359304 | tf_op jit(solution)/shard_map/ppermute | solution.py:31
  145.1 80.8 %collective-permute-start.19 = (bf16[192,2048]{1,0:T(8,128)(2,1)}, bf16[192,2048]{1,0:T(8,128)(2,1)}, u32[]{:S(2)}, u32[]{:S(2)}) collective-permute-start(bf16[192,2048]{1,0:T(8,128)(2,1)} %get-tuple-element.542), channel_id=1, source_target_pairs={{0,16},{16,0},{1,17},{17,1},{2,18},{18,2},{3,19},{19,3},{4,20},{20... | collective-permute-start | bytes 2359304 | tf_op jit(solution)/shard_map/ppermute | solution.py:31
  153.3 233.9 %all-gather.5.cloned.1.call-start = ((), (), s32[]{:S(2)}) async-start(), calls=%async_computation.4 | async-start | bytes 5242880 | tf_op jit(solution)/shard_map/all_gather | solution.py:543
  189.8 35.9 %collective-permute-start.17 = (bf16[768,1024]{1,0:T(8,128)(2,1)S(1)}, bf16[768,1024]{1,0:T(8,128)(2,1)S(1)}, u32[]{:S(2)}, u32[]{:S(2)}) collective-permute-start(bf16[768,1024]{1,0:T(8,128)(2,1)S(1)} %pad_maximum_fusion.22), channel_id=1, source_target_pairs={{0,1},{1,0},{2,3},{3,2},{4,5},{5,4},{6,7},{7,6},{8,9},{9,8},{10,11... | collective-permute-start | bytes 4718600 | tf_op jit(solution)/shard_map/ppermute | solution.py:31
  259.6 43.9 %collective-permute-start.24 = (bf16[384,2048]{1,0:T(8,128)(2,1)}, bf16[384,2048]{1,0:T(8,128)(2,1)}, u32[]{:S(2)}, u32[]{:S(2)}) collective-permute-start(bf16[384,2048]{1,0:T(8,128)(2,1)} %get-tuple-element.580), channel_id=1, source_target_pairs={{0,16},{16,0},{1,17},{17,1},{2,18},{18,2},{3,19},{19,3},{4,20},{20... | collective-permute-start | bytes 4718600 | tf_op jit(solution)/shard_map/ppermute | solution.py:31
  261.2 42.3 %collective-permute-start.25 = (bf16[384,2048]{1,0:T(8,128)(2,1)}, bf16[384,2048]{1,0:T(8,128)(2,1)}, u32[]{:S(2)}, u32[]{:S(2)}) collective-permute-start(bf16[384,2048]{1,0:T(8,128)(2,1)} %get-tuple-element.581), channel_id=1, source_target_pairs={{0,1},{1,0},{2,3},{3,2},{4,5},{5,4},{6,7},{7,6},{8,9},{9,8},{10,11... | collective-permute-start | bytes 4718600 | tf_op jit(solution)/shard_map/ppermute | solution.py:31
  264.6 92.4 %collective-permute-start.28 = (bf16[384,2048]{1,0:T(8,128)(2,1)}, bf16[384,2048]{1,0:T(8,128)(2,1)}, u32[]{:S(2)}, u32[]{:S(2)}) collective-permute-start(bf16[384,2048]{1,0:T(8,128)(2,1)} %get-tuple-element.577), channel_id=1, source_target_pairs={{0,16},{16,0},{1,17},{17,1},{2,18},{18,2},{3,19},{19,3},{4,20},{20... | collective-permute-start | bytes 4718600 | tf_op jit(solution)/shard_map/ppermute | solution.py:31
  267.4 318.5 %reduce-scatter.4.cloned.1.call-start = ((), (), s32[]{:S(2)}) async-start(), calls=%async_computation.5 | async-start | bytes 5242880 | tf_op jit(solution)/shard_map/reduce_scatter | solution.py:589
  267.5 89.6 %collective-permute-start.29 = (bf16[384,2048]{1,0:T(8,128)(2,1)}, bf16[384,2048]{1,0:T(8,128)(2,1)}, u32[]{:S(2)}, u32[]{:S(2)}) collective-permute-start(bf16[384,2048]{1,0:T(8,128)(2,1)} %get-tuple-element.578), channel_id=1, source_target_pairs={{0,1},{1,0},{2,3},{3,2},{4,5},{5,4},{6,7},{7,6},{8,9},{9,8},{10,11... | collective-permute-start | bytes 4718600 | tf_op jit(solution)/shard_map/ppermute | solution.py:31
  449.6 37.1 %collective-permute-start.34 = (bf16[384,2048]{1,0:T(8,128)(2,1)}, bf16[384,2048]{1,0:T(8,128)(2,1)S(1)}, u32[]{:S(2)}, u32[]{:S(2)}) collective-permute-start(bf16[384,2048]{1,0:T(8,128)(2,1)} %get-tuple-element.521), channel_id=1, source_target_pairs={{0,16},{16,0},{1,17},{17,1},{2,18},{18,2},{3,19},{19,3},{4,20},{20... | collective-permute-start | bytes 4718600 | tf_op jit(solution)/shard_map/ppermute | solution.py:31
  451.1 36.6 %collective-permute-start.35 = (bf16[384,2048]{1,0:T(8,128)(2,1)S(1)}, bf16[384,2048]{1,0:T(8,128)(2,1)S(1)}, u32[]{:S(2)}, u32[]{:S(2)}) collective-permute-start(bf16[384,2048]{1,0:T(8,128)(2,1)S(1)} %get-tuple-element.520), channel_id=1, source_target_pairs={{0,1},{1,0},{2,3},{3,2},{4,5},{5,4},{6,7},{7,6},{8,9},{9,8},{10,11... | collective-permute-start | bytes 4718600 | tf_op jit(solution)/shard_map/ppermute | solution.py:31
  505.5 232.4 %reduce-scatter.6.cloned.1.call-start = ((), (), s32[]{:S(2)}) async-start(), calls=%async_computation.6 | async-start | bytes 5242880 | tf_op jit(solution)/shard_map/reduce_scatter | solution.py:678
  547.2 38.7 %collective-permute-start.41 = (bf16[384,2048]{1,0:T(8,128)(2,1)}, bf16[384,2048]{1,0:T(8,128)(2,1)}, u32[]{:S(2)}, u32[]{:S(2)}) collective-permute-start(bf16[384,2048]{1,0:T(8,128)(2,1)} %get-tuple-element.517), channel_id=1, source_target_pairs={{0,16},{16,0},{1,17},{17,1},{2,18},{18,2},{3,19},{19,3},{4,20},{20... | collective-permute-start | bytes 4718600 | tf_op jit(solution)/shard_map/ppermute | solution.py:31
  547.7 38.1 %collective-permute-start.42 = (bf16[384,2048]{1,0:T(8,128)(2,1)}, bf16[384,2048]{1,0:T(8,128)(2,1)}, u32[]{:S(2)}, u32[]{:S(2)}) collective-permute-start(bf16[384,2048]{1,0:T(8,128)(2,1)} %get-tuple-element.516), channel_id=1, source_target_pairs={{0,1},{1,0},{2,3},{3,2},{4,5},{5,4},{6,7},{7,6},{8,9},{9,8},{10,11... | collective-permute-start | bytes 4718600 | tf_op jit(solution)/shard_map/ppermute | solution.py:31
  616.7 305.7 %reduce-scatter.8.cloned.1.call-start = ((), (), s32[]{:S(2)}) async-start(), calls=%async_computation.7 | async-start | bytes 5242880 | tf_op jit(solution)/shard_map/reduce_scatter | solution.py:695
  636.9 32.8 %collective-permute-start.48 = (bf16[768,512]{1,0:T(8,128)(2,1)S(1)}, bf16[768,512]{1,0:T(8,128)(2,1)S(1)}, u32[]{:S(2)}, u32[]{:S(2)}) collective-permute-start(bf16[768,512]{1,0:T(8,128)(2,1)S(1)} %slice.411), channel_id=1, source_target_pairs={{0,16},{16,0},{1,17},{17,1},{2,18},{18,2},{3,19},{19,3},{4,20},{20... | collective-permute-start | bytes 2359304 | tf_op jit(solution)/shard_map/ppermute | solution.py:31
  677.1 45.4 %collective-permute-start.50 = (bf16[640,384]{1,0:T(8,128)(2,1)}, bf16[640,384]{1,0:T(8,128)(2,1)}, u32[]{:S(2)}, u32[]{:S(2)}) collective-permute-start(bf16[640,384]{1,0:T(8,128)(2,1)} %fusion.8), channel_id=1, source_target_pairs={{2,0},{4,2},{6,4},{3,1},{5,3},{7,5},{10,8},{12,10},{14,12},{11,9},... | collective-permute-start | bytes 1474568 | tf_op jit(solution)/shard_map/ppermute | solution.py:669
  (214 other events, 2408.3 us)
Sparse Core Ops, SparseCore 0:
  153.4 150.0 all-gather.2
  305.1 78.9 all-gather.4
  505.6 80.1 reduce-scatter.3
  616.8 121.0 reduce-scatter.5
  758.4 78.6 reduce-scatter.7

commit v2 on v1

--- a/solution.py
+++ b/solution.py
@@ -324,6 +324,130 @@
     scaled = grad * gain[:, None]
     back = rate * (scaled - normed * jnp.mean(scaled * normed, axis=1, keepdims=True))
     return back, jnp.sum(grad * normed, axis=(0, 2))
+
+
+def weight_grad_kernel(*refs):
+    out_ref = refs[-1]
+    count = len(refs) // 2
+    total = sum(dot(refs[i][...], refs[count + i][...], (0, 0)) for i in range(count))
+    out_ref[0] = total.astype(out_ref.dtype)
+
+
+def weight_grad(values, grads, blocks):
+    width, hidden = values[0].shape[1], grads[0].shape[1]
+    block = width // blocks
+    tokens = sum(v.shape[0] for v in values)
+    return pl.pallas_call(
+        weight_grad_kernel,
+        grid=(blocks,),
+        in_specs=[pl.BlockSpec((v.shape[0], block), lambda i: (0, i)) for v in values]
+        + [pl.BlockSpec(g.shape, lambda i: (0, 0), pipeline_mode=pl.Buffered(1)) for g in grads],
+        out_specs=pl.BlockSpec((1, block, hidden), lambda i: (i, 0, 0)),
+        out_shape=jax.ShapeDtypeStruct((blocks, block, hidden), BF16),
+        compiler_params=pltpu.CompilerParams(dimension_semantics=("arbitrary",), vmem_limit_bytes=56 * 2**20),
+        cost_estimate=pl.CostEstimate(
+            flops=2 * tokens * width * hidden, bytes_accessed=2 * tokens * (width + hidden), transcendentals=0
+        ),
+        name="weight_grad",
+    )(*values, *grads)
+
+
+def tall(tile, columns):
+    return pl.BlockSpec((tile, columns), lambda i: (i, 0))
+
+
+def held(weights, which=None):
+    blocks = weights.shape[0] if which is None else weights.shape[0] // 2
+    return pl.BlockSpec((blocks, *weights.shape[1:]), lambda i: (which or 0, 0, 0), pipeline_mode=pl.Buffered(1))
+
+
+FFN_PARAMS = pltpu.CompilerParams(dimension_semantics=("arbitrary",), vmem_limit_bytes=56 * 2**20)
+
+
+def matrix(ref):
+    return ref[...].reshape(ref.shape[0] * ref.shape[1], ref.shape[2])
+
+
+def forward_kernel(tokens_ref, gate_w, up_w, gate_ref, up_ref, hidden_ref):
+    tokens = tokens_ref[...]
+    gate, up = dot(tokens, matrix(gate_w), (1, 0)), dot(tokens, matrix(up_w), (1, 0))
+    gate_ref[...] = gate
+    up_ref[...] = up
+    hidden_ref[...] = (gate / (1.0 + jnp.exp(-gate)) * up).astype(BF16)
+
+
+def forward(tokens, gate_up, tile=256):
+    count, width = tokens.shape
+    hidden = gate_up.shape[2]
+    return pl.pallas_call(
+        forward_kernel,
+        grid=(count // tile,),
+        in_specs=[tall(tile, width), held(gate_up, 0), held(gate_up, 1)],
+        out_specs=[tall(tile, hidden)] * 3,
+        out_shape=[jax.ShapeDtypeStruct((count, hidden), t) for t in (F32, F32, BF16)],
+        compiler_params=FFN_PARAMS,
+        cost_estimate=pl.CostEstimate(
+            flops=4 * count * width * hidden,
+            bytes_accessed=4 * width * hidden + 2 * count * width + 10 * count * hidden,
+            transcendentals=count * hidden,
+        ),
+        name="forward",
+    )(tokens, gate_up, gate_up)
+
+
+def hidden_back_kernel(grad_ref, gate_ref, up_ref, down_w, gate_w, up_w, gate_grad_ref, up_grad_ref, part_ref):
+    grad = dot(grad_ref[...], matrix(down_w), (1, 0))
+    gate = gate_ref[...]
+    sigmoid = 1.0 / (1.0 + jnp.exp(-gate))
+    gate_grad = (grad * up_ref[...] * sigmoid * (1.0 + gate * (1.0 - sigmoid))).astype(BF16)
+    up_grad = (grad * gate * sigmoid).astype(BF16)
+    gate_grad_ref[...] = gate_grad
+    up_grad_ref[...] = up_grad
+    part_ref[...] = (dot(gate_grad, matrix(gate_w), (1, 1)) + dot(up_grad, matrix(up_w), (1, 1))).astype(BF16)
+
+
+def hidden_back(grad, gate, up, down_w, gate_up, tile=256):
+    count, width = grad.shape
+    hidden = gate.shape[1]
+    return pl.pallas_call(
+        hidden_back_kernel,
+        grid=(count // tile,),
+        in_specs=[
+            tall(tile, width), tall(tile, hidden), tall(tile, hidden), held(down_w), held(gate_up, 0), held(gate_up, 1)
+        ],
+        out_specs=[tall(tile, hidden), tall(tile, hidden), tall(tile, width)],
+        out_shape=[jax.ShapeDtypeStruct((count, n), BF16) for n in (hidden, hidden, width)],
+        compiler_params=FFN_PARAMS,
+        cost_estimate=pl.CostEstimate(
+            flops=6 * count * width * hidden,
+            bytes_accessed=6 * width * hidden + 16 * count * hidden,
+            transcendentals=count * hidden,
+        ),
+        name="hidden_back",
+    )(grad, gate, up, down_w, gate_up, gate_up)
+
+
+def down_kernel(hidden_ref, down_w, out_ref):
+    out_ref[...] = dot(hidden_ref[...], matrix(down_w), (1, 1)).astype(BF16)
+
+
+def down_product(hidden, down_w, tile=256):
+    count, size = hidden.shape
+    width = down_w.shape[0] * down_w.shape[1]
+    return pl.pallas_call(
+        down_kernel,
+        grid=(count // tile,),
+        in_specs=[tall(tile, size), held(down_w)],
+        out_specs=tall(tile, width),
+        out_shape=jax.ShapeDtypeStruct((count, width), BF16),
+        compiler_params=FFN_PARAMS,
+        cost_estimate=pl.CostEstimate(
+            flops=2 * count * width * size,
+            bytes_accessed=2 * width * size + 2 * count * (width + size),
+            transcendentals=0,
+        ),
+        name="down_product",
+    )(hidden, down_w)
 
 
 def paired():
@@ -511,10 +635,11 @@
     got, query_part, out_part, own_kv = stage(got, query_part, out_part, own_kv)
 
     packed = second_hop(mine, got)
+    gate_up, packed = by_weight(packed, 0, 2), by_weight(packed, 2, 3)
     going, arrived = up(own_kv), [beside(own_kv)]
     query_part = join(query_part, "ctx", 0, 2)
-    packed, going, arrived[0], query_part = stage(packed, going, arrived[0], query_part)
-    gate_up = lax.all_gather(by_weight(packed, 0, 2), "ctx", axis=1, tiled=True)
+    packed, gate_up, going, arrived[0], query_part = stage(packed, gate_up, going, arrived[0], query_part)
+    gate_up = lax.all_gather(gate_up, "ctx", axis=1, tiled=True)
 
     arrived.append(beside(going))
     going = up(going)
@@ -539,109 +664,81 @@
     out_part = from_tp(out_part, 0)
     top, bottom = grad_low[:half], grad_low[half:]
     grad_near = (swap(top, "tp"), swap(bottom, "row")) if two else (top, bottom)
-    out_low, totals, out_part, grad_near, packed = stage(out_low, totals, out_part, grad_near, packed)
-    down_full = lax.all_gather(by_weight(packed, 2, 3), "ctx", axis=1, tiled=True)
+    out_low, totals, out_part, grad_near, packed, gate_up = stage(
+        out_low, totals, out_part, grad_near, packed, gate_up
+    )
+    down_full = lax.all_gather(packed, "ctx", axis=1, tiled=True)
     out_full = join(out_part, "core", 1)
     out_flat = out_low.reshape(all_slots * HEAD_DIM, own_tokens)
     attended = dot(out_flat, out_full, (0, 0))
     residual, normed_two = by_tokens(norm_two_kernel, strip_places, [flat, attended], norm2_gain, [F32, BF16])
     normed_two, residual, out_full = stage(normed_two, residual, out_full)
 
-    def forward(chunk):
-        gate, up_proj = dot(chunk, gate_full, (1, 0)), dot(chunk, up_full, (1, 0))
-        return gate, up_proj, (gate * jax.nn.sigmoid(gate) * up_proj).astype(BF16)
-
     if two:
         top, bottom = normed_two[:half], normed_two[half:]
         near = swap(top, "tp"), swap(bottom, "row")
-        normed_all = [both_cores(normed_two)]
-        near, normed_all[0] = stage(near, normed_all[0])
+        other = swap(normed_two, "core")
+        near, other = stage(near, other)
         far = swap(jnp.concatenate([top, near[0]]), "row"), swap(jnp.concatenate([bottom, near[1]]), "tp")
-        normed_all.append(both_cores(jnp.concatenate(near)))
-        far, normed_all, gate_up = stage(far, normed_all, gate_up)
-    gate_full, up_full = (gate_up[i * plane : (i + 1) * plane].reshape(width, part) for i in range(2))
-    if two:
+        near = jnp.concatenate(near)
+        normed_all = [jnp.concatenate([normed_two, other, near, swap(near, "core")])]
+        near = jnp.concatenate(grad_near)
+        grad_all = [jnp.concatenate([grad_low, swap(grad_low, "core"), near, swap(near, "core")])]
+        ready = [forward(normed_all[0], gate_up)]
+        far, normed_all, grad_all, ready, down_full = stage(far, normed_all, grad_all, ready, down_full)
         top, bottom = grad_low[:half], grad_low[half:]
         normed_all.append(both_cores(jnp.concatenate(far)))
-        ready = [forward(x) for x in normed_all]
+        ready.append(forward(normed_all[1], gate_up))
         grad_far = (
             swap(jnp.concatenate([top, grad_near[0]]), "row"), swap(jnp.concatenate([bottom, grad_near[1]]), "tp")
         )
-        grad_all = [both_cores(grad_low), both_cores(jnp.concatenate(grad_near))]
         ready, grad_far, grad_all, normed_all = stage(ready, grad_far, grad_all, normed_all)
         grad_all.append(both_cores(jnp.concatenate(grad_far)))
     else:
         normed_all = [lax.all_gather(normed_two, ("row", "core", "tp"), axis=0, tiled=True)]
         grad_all = [lax.all_gather(grad_low, ("row", "core", "tp"), axis=0, tiled=True)]
-        ready = [forward(normed_all[0])]
+        ready = [forward(normed_all[0], gate_up)]
     chunks = range(len(normed_all))
     hidden = [x[2] for x in ready]
 
-    def column_gradient(values, grads):
-        summed = sum(dot(values[i], grads[i], (0, 0)) for i in chunks)
-        return summed.astype(BF16).reshape(plane, strip * ctx, part)
-
-    grad_down = column_gradient(grad_all, hidden)
-    grad_down, gate_full, up_full, down_full, ready, grad_all = stage(
-        grad_down, gate_full, up_full, down_full, ready, grad_all
-    )
-    down_full = down_full.reshape(width, part)
-    grad_down = lax.psum_scatter(grad_down, "ctx", scatter_dimension=1, tiled=True)
-    hidden = [x[2] for x in ready]
-
-    def hidden_grads(i):
-        gate, up_proj, _ = ready[i]
-        sigmoid_gate = jax.nn.sigmoid(gate)
-        grad_hidden = dot(grad_all[i], down_full, (1, 0))
-        return (
-            (grad_hidden * up_proj * sigmoid_gate * (1.0 + gate * (1.0 - sigmoid_gate))).astype(BF16),
-            (grad_hidden * gate * sigmoid_gate).astype(BF16),
-        )
-
-    def input_part(grads):
-        return (dot(grads[0], gate_full, (1, 1)) + dot(grads[1], up_full, (1, 1))).astype(BF16)
-
-    def column_part(kind, values, pairs):
-        return sum(dot(values[i], pairs[i][kind], (0, 0)) for i in chunks[:-1]) if two else 0.0
-
-    def column_rest(kind, values, pairs, summed):
-        summed = summed + dot(values[-1], pairs[-1][kind], (0, 0))
-        return summed.astype(BF16).reshape(plane, strip * ctx, part)
+    def backward(i):
+        return hidden_back(grad_all[i], ready[i][0], ready[i][1], down_full, gate_up)
 
     def output_part(i):
-        return dot(hidden[i], down_full, (1, 1)).astype(BF16)
-
-    grads = [None] * len(chunks)
+        return down_product(hidden[i], down_full)
+
+    def scattered(gradient):
+        return lax.psum_scatter(gradient, "ctx", scatter_dimension=1, tiled=True)
+
     if two:
-        grads[2] = hidden_grads(2)
-        far_part = input_part(grads[2])
-        grads[2], far_part, far_send, grad_all = stage(grads[2], far_part, other_half(far_part), grad_all)
-        far = own_half(far_part, swap(far_send, "core")).astype(BF16)
-        grads[1] = hidden_grads(1)
-        far, grads[1], grad_all = stage(far, grads[1], grad_all)
+        far_grads = backward(1)
+        far_grads, far_send, grad_all = stage(far_grads, other_half(far_grads[2]), grad_all)
+        far = own_half(far_grads[2], swap(far_send, "core")).astype(BF16)
+        far_part = output_part(1)
+        far, grad_all, far_part = stage(far, grad_all, far_part)
         hops = far_hops(far)
-        near_part = input_part(grads[1])
-        grads[0] = hidden_grads(0)
-        own_part = input_part(grads[0])
-        hops, near_part, own_part, grads, hidden = stage(hops, near_part, own_part, grads, hidden)
+        near_grads = backward(0)
+        output_far = own_half(far_part, swap(other_half(far_part), "core")).astype(BF16)
+        hops, near_grads, hidden, output_far = stage(hops, near_grads, hidden, output_far)
+        grads = [near_grads, far_grads]
+        own_part, near_part = near_grads[2][: 2 * own_tokens], near_grads[2][2 * own_tokens :]
         near = own_half(near_part, swap(other_half(near_part), "core"))
         own = own_half(own_part, swap(other_half(own_part), "core"))
         sends = near_sends(near, *hops)
-        far_part = output_part(2)
-        sends, own, far_part, normed_all = stage(sends, own, far_part, normed_all)
+        sends, own, normed_all, hidden, grad_all = stage(sends, own, normed_all, hidden, grad_all)
         top_x, bottom_y = swap(sends[0], "tp"), swap(sends[1], "row")
-        output_far = own_half(far_part, swap(other_half(far_part), "core")).astype(BF16)
-        gate_parts = column_part(0, normed_all, grads)
-        top_x, bottom_y, output_far, grads, normed_all, gate_parts = stage(
-            top_x, bottom_y, output_far, grads, normed_all, gate_parts
+        grad_down = weight_grad(grad_all, hidden, plane)
+        top_x, bottom_y, output_far, grads, normed_all, grad_down = stage(
+            top_x, bottom_y, output_far, grads, normed_all, grad_down
         )
         output_hops = far_hops(output_far)
         grad_normed_two = plane_total(own, *hops, top_x, bottom_y)
     else:
-        grads[0] = hidden_grads(0)
-        gate_parts = column_part(0, normed_all, grads)
-        grad_normed_two = plane_sum(input_part(grads[0])).astype(F32)
+        grads = [backward(0)]
+        grad_down = weight_grad(grad_all, hidden, plane)
+        grad_normed_two = plane_sum(grads[0][2]).astype(F32)
         output_hops = grad_normed_two
+    grad_down = scattered(grad_down)
     grad_residual, grad_attn, grad_norm_two = by_tokens(
         back_two_kernel, near_strips, [grad_normed_two, residual, grad_low], norm2_gain, [F32, BF16], True
     )
@@ -650,8 +747,8 @@
     grad_query, grad_kv = attend_back(query_low, grad_out, out_low, keyvalue, totals, tables)
     grad_out_w = dot(out_flat, grad_attn, (1, 0)).astype(BF16)
     grad_out_w = fold(grad_out_w, "core", 1)
-    output_hops, grad_query, grad_kv, grads, grad_out_w, grad_down = stage(
-        output_hops, grad_query, grad_kv, grads, grad_out_w, grad_down
+    output_hops, grad_query, grad_kv, grads, grad_out_w, normed_all, hidden = stage(
+        output_hops, grad_query, grad_kv, grads, grad_out_w, normed_all, hidden
     )
     grad_kv = grad_kv.reshape(ctx, tp, 2 * kv_width, own_tokens)
 
@@ -669,42 +766,47 @@
         return lax.ppermute(value.astype(BF16), "ctx", [(j, j - 1) for j in range(1, ctx)]).astype(F32)
 
     summed = to_owner(grad_kv[ctx - 1])
-    grad_gate_w = column_rest(0, normed_all, grads, gate_parts)
+    grad_gate_w = weight_grad(normed_all, [g[0] for g in grads], plane)
     out_w_low, out_w_high = grad_out_w[: all_slots * 32], grad_out_w[all_slots * 32 :]
     out_w_low = fold(out_w_low, "row", 1)
-    summed, grad_gate_w, grad_kv, grad_query, out_w_low, out_w_high, normed_all, grads = stage(
-        summed, grad_gate_w, grad_kv, grad_query, out_w_low, out_w_high, normed_all, grads
-    )
-    grad_gate_w = lax.psum_scatter(grad_gate_w, "ctx", scatter_dimension=1, tiled=True)
+    summed, grad_kv, grad_query, out_w_low, out_w_high, normed_all, grads, grad_gate_w, grad_down = stage(
+        summed, grad_kv, grad_query, out_w_low, out_w_high, normed_all, grads, grad_gate_w, grad_down
+    )
+    grad_gate_w = scattered(grad_gate_w)
 
     summed = to_owner(grad_kv[2]) + down(summed)
-    up_parts = column_part(1, normed_all, grads)
+    grad_up_w = weight_grad(normed_all, [g[1] for g in grads], plane)
     out_w_high = fold(out_w_high, "row", 1)
-    summed, grad_kv, grad_query, out_w_low, out_w_high, normed_all, grads, up_parts = stage(
-        summed, grad_kv, grad_query, out_w_low, out_w_high, normed_all, grads, up_parts
-    )
+    summed, grad_kv, grad_query, out_w_low, out_w_high, grad_up_w, grad_down, hidden = stage(
+        summed, grad_kv, grad_query, out_w_low, out_w_high, grad_up_w, grad_down, hidden
+    )
+    grad_up_w = scattered(grad_up_w)
 
     summed = to_owner(grad_kv[1]) + down(summed)
-    grad_up_w = column_rest(1, normed_all, grads, up_parts)
     grad_query_proj, grad_q_gain = head_back(query_proj, q_gain, turn, grad_query)
     grad_query_low = grad_query_proj.astype(BF16).reshape(all_slots * HEAD_DIM, own_tokens)
+    near_part = output_part(0)
     grad_down = row_out(grad_down)
-    summed, grad_query_low, grad_q_gain, grad_kv, grad_up_w, grad_gate_w, grad_down, out_w_low, out_w_high = stage(
-        summed, grad_query_low, grad_q_gain, grad_kv, grad_up_w, grad_gate_w, grad_down, out_w_low, out_w_high
-    )
-    grad_up_w = lax.psum_scatter(grad_up_w, "ctx", scatter_dimension=1, tiled=True)
+    summed, grad_query_low, grad_q_gain, grad_kv, grad_down, out_w_low, out_w_high, near_part = stage(
+        summed, grad_query_low, grad_q_gain, grad_kv, grad_down, out_w_low, out_w_high, near_part
+    )
 
     summed = to_owner(grad_kv[0]) + down(summed)
     grad_query_w = dot(normed_near, grad_query_low, (0, 1)).astype(BF16)
     grad_query_w = fold(grad_query_w, "core", 0)
+    grad_normed_near = dot(grad_query_low, query_full, (0, 1))
     grad_down = core_out(grad_down)
-    grad_gate_w = row_out(grad_gate_w)
-    summed, grad_query_w, grad_query_low, grad_down, grad_gate_w, out_w_low, out_w_high = stage(
-        summed, grad_query_w, grad_query_low, grad_down, grad_gate_w, out_w_low, out_w_high
-    )
-
-    grad_normed_near = dot(grad_query_low, query_full, (0, 1))
-    grad_gate_w = core_out(grad_gate_w)
+    if two:
+        own_part, near_part = near_part[: 2 * own_tokens], near_part[2 * own_tokens :]
+        near = own_half(near_part, swap(other_half(near_part), "core"))
+        own = own_half(own_part, swap(other_half(own_part), "core"))
+        sends = near_sends(near, *output_hops)
+    else:
+        own, sends = near_part, summed
+    summed, grad_query_w, grad_normed_near, grad_down, out_w_low, out_w_high, sends, own, grad_gate_w = stage(
+        summed, grad_query_w, grad_normed_near, grad_down, out_w_low, out_w_high, sends, own, grad_gate_w
+    )
+
     grad_key_proj, grad_k_gain = head_back(
         key_proj, k_gain, turn, summed[:kv_width].reshape(KVH, HEAD_DIM, own_tokens)
     )
@@ -724,64 +826,67 @@
         jnp.where(moved[None, :, :, None], small.reshape(3, 1, devices, strip), 0.0), axis=2
     ).reshape(3, width)
     total = lax.dynamic_update_slice(total, small, (2 * kv_width, 0)).astype(BF16)
-    query_w_low, query_w_high = grad_query_w[:, : all_slots * 32], grad_query_w[:, all_slots * 32 :]
-    query_w_low = fold(query_w_low, "row", 0)
+    query_w = fold(grad_query_w[:, : all_slots * 32], "row", 0), grad_query_w[:, all_slots * 32 :]
     grad_out_w = to_tp(jnp.concatenate([out_w_low, out_w_high]), 0)
-    total, query_w_low, query_w_high, grad_out_w, grad_gate_w, hidden = stage(
-        total, query_w_low, query_w_high, grad_out_w, grad_gate_w, hidden
-    )
+    total, query_w, grad_out_w, grad_gate_w, own, sends, grad_up_w = stage(
+        total, query_w, grad_out_w, grad_gate_w, own, sends, grad_up_w
+    )
+
+    def along(value, bit):
+        got = swap(value, "ctx", bit)
+        return sum32(
+            value, jnp.concatenate([got[:, (j ^ bit) * strip : ((j ^ bit) + 1) * strip] for j in range(ctx)], axis=1)
+        )
 
     if not two:
         total = lax.psum(total, ("row", "core", "ctx", "tp"))
-        output = residual + plane_sum(output_part(0)).astype(F32)
-        grad_query_w = jnp.concatenate([query_w_low, fold(query_w_high, "row", 0)], axis=1)
-        grad_query_w = to_tp(grad_query_w, 1)
-        grad_query_w = fold(fold(grad_query_w, "ctx", 0, 2), "ctx", 0)
+        output = residual + plane_sum(own).astype(F32)
+        query_w = jnp.concatenate([query_w[0], fold(query_w[1], "row", 0)], axis=1)
+        grad_query_w = fold(fold(to_tp(query_w, 1), "ctx", 0, 2), "ctx", 0)
         grad_out_w = fold(fold(grad_out_w, "ctx", 1, 2), "ctx", 1)
-        grad_up_w = core_out(row_out(grad_up_w))
+        grad_up_w, grad_gate_w = core_out(row_out(grad_up_w)), core_out(row_out(grad_gate_w))
     else:
         total = fold(total, "core", 1)
-        near_part = output_part(1)
-        query_w_high = fold(query_w_high, "row", 0)
-        total, near_part, query_w_low, query_w_high, grad_out_w = stage(
-            total, near_part, query_w_low, query_w_high, grad_out_w
+        total, query_w, grad_out_w, grad_gate_w, own, sends = stage(
+            total, query_w, grad_out_w, grad_gate_w, own, sends
         )
         size = total.shape[0] // 2
         got = swap(lax.dynamic_slice_in_dim(total, (1 - tp_index) * size, size, 0), "tp")
         total = sum32(lax.dynamic_slice_in_dim(total, tp_index * size, size, 0), got)
-        own_part = output_part(0)
-        near = own_half(near_part, swap(other_half(near_part), "core"))
-        grad_out_w = fold(grad_out_w, "ctx", 1, 2)
-        total, grad_out_w, query_w_low, query_w_high, own_part, near = stage(
-            total, grad_out_w, query_w_low, query_w_high, own_part, near
+        query_w = jnp.concatenate([query_w[0], fold(query_w[1], "row", 0)], axis=1)
+        total, grad_out_w, query_w, grad_gate_w, own, sends = stage(
+            total, grad_out_w, query_w, grad_gate_w, own, sends
         )
         total = fold(total, "row", 1)
-        grad_query_w = fold(jnp.concatenate([query_w_low, query_w_high], axis=1), "tp", 1)
-        own = own_half(own_part, swap(other_half(own_part), "core"))
-        total, grad_query_w, own, grad_out_w = stage(total, grad_query_w, own, grad_out_w)
-        total = fold(total, "ctx", 1, 2)
-        sends = near_sends(near, *output_hops)
+        query_w = fold(query_w, "tp", 1)
+        total, query_w, sends, grad_gate_w, grad_out_w, grad_up_w = stage(
+            total, query_w, sends, grad_gate_w, grad_out_w, grad_up_w
+        )
+        total = along(total, 1)
         top_x, bottom_y = swap(sends[0], "tp"), swap(sends[1], "row")
+        grad_out_w = fold(grad_out_w, "ctx", 1, 2)
+        total, query_w, grad_gate_w, top_x, bottom_y, grad_out_w, grad_up_w = stage(
+            total, query_w, grad_gate_w, top_x, bottom_y, grad_out_w, grad_up_w
+        )
+        total = along(total, 2)
+        output = residual + plane_total(own, *output_hops, top_x, bottom_y)
+        grad_gate_w = row_out(grad_gate_w)
         grad_out_w = fold(grad_out_w, "ctx", 1)
-        total, top_x, bottom_y, grad_query_w, grad_out_w = stage(total, top_x, bottom_y, grad_query_w, grad_out_w)
-        total = fold(total, "ctx", 1)
-        grad_query_w = fold(grad_query_w, "ctx", 0, 2)
-        total, grad_query_w, grad_up_w = stage(total, grad_query_w, grad_up_w)
-        total = join(total, "ctx", 1)
-        output = residual + plane_total(own, *output_hops, top_x, bottom_y)
+        total, query_w, grad_gate_w, grad_up_w, grad_out_w, output = stage(
+            total, query_w, grad_gate_w, grad_up_w, grad_out_w, output
+        )
+        total = join(total, "row", 1)
+        query_w = fold(query_w, "ctx", 0, 2)
+        grad_gate_w = core_out(grad_gate_w)
+        total, grad_up_w, query_w, grad_gate_w = stage(total, grad_up_w, query_w, grad_gate_w)
+        other = swap(total, "tp")
+        grad_query_w = fold(query_w, "ctx", 0)
         grad_up_w = row_out(grad_up_w)
-        total, grad_query_w, grad_up_w, output = stage(total, grad_query_w, grad_up_w, output)
-        total = join(total, "ctx", 1, 2)
-        total, grad_query_w, grad_up_w = stage(total, grad_query_w, grad_up_w)
-        total = join(total, "row", 1)
-        grad_query_w = fold(grad_query_w, "ctx", 0)
-        grad_up_w = core_out(grad_up_w)
-        total, grad_query_w, grad_up_w = stage(total, grad_query_w, grad_up_w)
-        other = swap(total, "tp")
         first = tp_index == 0
         total = jnp.concatenate([jnp.where(first, total, other), jnp.where(first, other, total)])
-        (total,) = stage(total)
+        total, grad_up_w, grad_query_w = stage(total, grad_up_w, grad_query_w)
         total = join(total, "core", 1)
+        grad_up_w = core_out(grad_up_w)
     grad_key_w, grad_value_w, small = unfold(strip_places if two else ranks, total, kv_width)
 
     return (

time: 1010 us -> 986 us (0.976)
  matrix products: 229 us -> 31.3 us
  Pallas kernels: 34.8 us -> 209 us
  other arithmetic: 161 us -> 134 us
  waiting for transfers between devices: 364 us -> 391 us
  local copies, waits for them, and re-layouts: 111 us -> 99.6 us
    dot_general x36 -> x9, matrix products: 229 us -> 31.3 us  [dot(): lax.dot_general(left, right, ((contract[:1], contract[1:]), ((), ())), pr...]
    pallas_call x0 -> x9, Pallas kernels: none -> 174 us  [the longest x2 56.4 us: hidden_back(): pl.pallas_call(hidden_back_kernel, grid=(count // tile,), in_specs=[tall(...]
    convert_element_type x5 -> x1, other arithmetic: 25 us -> 4.34 us  [body(): far = own_half(far_grads[2], swap(far_send, 'core')).astype(BF16)]
    all_gather x2, waiting for transfers between devices: 28.1 us -> 47.3 us  [the longest x1 46.2 us: body(): down_full = lax.all_gather(packed, 'ctx', axis=1, tiled=True)]
    ppermute x3, waiting for transfers between devices: 43 us -> 60 us  [down(): lax.ppermute(value.astype(BF16), 'ctx', [(j, j - 1) for j in range(1, ctx)])]
    dynamic_slice x9 -> x0, local copies, waits for them, and re-layouts: 16.3 us -> none  [the longest x6 11.3 us: row_out(): mine = lax.dynamic_index_in_dim(view, row_index, 0, False)]
    reduce_scatter x3, waiting for transfers between devices: 30.8 us -> 15.2 us  [scattered(): return lax.psum_scatter(gradient, 'ctx', scatter_dimension=1, tiled=True)]
    concatenate x6 -> x3, other arithmetic: 18.3 us -> 6.78 us  [the longest x1 4.42 us: body(): jnp.concatenate([bottom, grad_near[1]])]
  transfers between devices with their start and end apart: 87 -> 85, of which waited for: 39 -> 41; matrix products, arithmetic and copies ran while one was open for 38% -> 21% of each run, Pallas kernels for 3% -> 18%
where the time goes in v2:
time: 986 us; the launch traced here: 977 us
  waiting for transfers between devices  391 us (40%)
  Pallas kernels  209 us (21%)
  other arithmetic  134 us (14%)
  local copies, waits for them, and re-layouts  99.6 us (10%)
  starting transfers between devices  93.8 us (10%)
  matrix products  31.3 us (3%)
  between operations  17.3 us (2%)
    ppermute x74, waiting for transfers between devices, swap(): return lax.ppermute(value, axis, [(i, i ^ bit) for i in range(size)])  265 us
    ppermute x74, starting transfers between devices, swap(): return lax.ppermute(value, axis, [(i, i ^ bit) for i in range(size)])  79.9 us
    ppermute x3, waiting for transfers between devices, down(): lax.ppermute(value.astype(BF16), 'ctx', [(j, j - 1) for j in range(1, ctx)])  60 us
    pallas_call x2, Pallas kernels, hidden_back(): pl.pallas_call(hidden_back_kernel, grid=(count // tile,), in_specs=[tall(...  56.4 us
    pallas_call x3, Pallas kernels, weight_grad(): pl.pallas_call(weight_grad_kernel, grid=(blocks,), in_specs=[pl.BlockSpec...  56.1 us
    all_gather x1, waiting for transfers between devices, body(): down_full = lax.all_gather(packed, 'ctx', axis=1, tiled=True)  46.2 us
    unnamed x255, local copies, waits for them, and re-layouts  42.7 us
    pallas_call x2, Pallas kernels, forward(): pl.pallas_call(forward_kernel, grid=(count // tile,), in_specs=[tall(tile...  38.5 us
  transfers between devices with their start and end apart: 85, of which 41 were waited for; matrix products, arithmetic and copies ran while one was open for 21% of the time, Pallas kernels for 18%

profile of v2, /device:TPU:0, one launch (start us, length us, event | category | flops | bytes accessed | tf_op | source)
XLA Modules:
  0.0 976.8 jit_solution(4244062599246915764)
XLA Ops:
  46.5 12.1 %collective-permute-done.6 = bf16[256,768]{1,0:T(8,128)(2,1)} collective-permute-done((bf16[256,768]{1,0:T(8,128)(2,1)}, bf16[256,768]{1,0:T(8,128)(2,1)}, u32[]{:S(2)}, u32[]{:S(2)}) %collective-permute-start.6) | collective-permute-done | bytes 393248 | tf_op jit(solution)/shard_map/ppermute | solution.py:31
  62.9 10.2 %collective-permute-done.3 = bf16[2,384,1024]{2,1,0:T(8,128)(2,1)} collective-permute-done((bf16[2,384,1024]{2,1,0:T(8,128)(2,1)}, bf16[2,384,1024]{2,1,0:T(8,128)(2,1)}, u32[]{:S(2)}, u32[]{:S(2)}) %collective-permute-start.3) | collective-permute-done | bytes 1572896 | tf_op jit(solution)/shard_map/ppermute | solution.py:31
  100.8 20.4 %collective-permute-start.13 = (bf16[768,256]{1,0:T(8,128)(2,1)S(1)}, bf16[768,256]{1,0:T(8,128)(2,1)S(1)}, u32[]{:S(2)}, u32[]{:S(2)}) collective-permute-start(bf16[768,256]{1,0:T(8,128)(2,1)S(1)} %pad_maximum_fusion.37), channel_id=1, source_target_pairs={{0,4},{2,6},{4,0},{6,2},{1,5},{3,7},{5,1},{7,3},{8,12},{10,14},{12... | collective-permute-start | bytes 1179656 | tf_op jit(solution)/shard_map/ppermute | solution.py:31
  125.1 30.0 %collective-permute-done.13 = bf16[768,256]{1,0:T(8,128)(2,1)S(1)} collective-permute-done((bf16[768,256]{1,0:T(8,128)(2,1)S(1)}, bf16[768,256]{1,0:T(8,128)(2,1)S(1)}, u32[]{:S(2)}, u32[]{:S(2)}) %collective-permute-start.13) | collective-permute-done | bytes 393248 | tf_op jit(solution)/shard_map/ppermute | solution.py:31
  169.8 21.2 %collective-permute-done.14 = bf16[640,384]{1,0:T(8,128)(2,1)S(1)} collective-permute-done((bf16[640,384]{1,0:T(8,128)(2,1)}, bf16[640,384]{1,0:T(8,128)(2,1)S(1)}, u32[]{:S(2)}, u32[]{:S(2)}) %collective-permute-start.14) | collective-permute-done | bytes 491552 | tf_op jit(solution)/shard_map/ppermute | solution.py:31
  225.7 17.6 %collective-permute-done.17 = bf16[768,1024]{1,0:T(8,128)(2,1)S(1)} collective-permute-done((bf16[768,1024]{1,0:T(8,128)(2,1)}, bf16[768,1024]{1,0:T(8,128)(2,1)S(1)}, u32[]{:S(2)}, u32[]{:S(2)}) %collective-permute-start.17) | collective-permute-done | bytes 1572896 | tf_op jit(solution)/shard_map/ppermute | solution.py:31
  270.6 12.6 %collective-permute-done.21 = bf16[192,2048]{1,0:T(8,128)(2,1)S(1)} collective-permute-done((bf16[192,2048]{1,0:T(8,128)(2,1)S(1)}, bf16[192,2048]{1,0:T(8,128)(2,1)S(1)}, u32[]{:S(2)}, u32[]{:S(2)}) %collective-permute-start.21) | collective-permute-done | bytes 786464 | tf_op jit(solution)/shard_map/ppermute | solution.py:31
  296.2 19.2 %forward.2 = (f32[1536,1024]{1,0:T(8,128)}, f32[1536,1024]{1,0:T(8,128)}, bf16[1536,1024]{1,0:T(8,128)(2,1)}) custom-call(bf16[1536,2048]{1,0:T(8,128)(2,1)} %constant_dynamic-update-slice_fusion.8.tokens_ref.refs_0_, bf16[8,512,1024]{2,1,0:T(8,128)(2,1)} %all-gather.3.cloned.1.call-done.gate_w.up_w, ...), custom_call_target="tpu_custom_call" | custom-call | flops 12884901888 | bytes 30408704 | tf_op jit(solution)/shard_map/forward/pallas_call | solution.py:382
  315.4 46.2 %all-gather.5.cloned.1.call-done.down_w = bf16[4,512,1024]{2,1,0:T(8,128)(2,1)} async-done(((bf16[4,128,1024]{2,1,0:T(8,128)(2,1)}), bf16[4,512,1024]{2,1,0:T(8,128)(2,1)}) %all-gather.5.cloned.1.call-update) | async-done | bytes 4194320 | tf_op jit(solution)/shard_map/all_gather | solution.py:670
  374.6 19.3 %forward.3 = (f32[1536,1024]{1,0:T(8,128)}, f32[1536,1024]{1,0:T(8,128)}, bf16[1536,1024]{1,0:T(8,128)(2,1)}) custom-call(bf16[1536,2048]{1,0:T(8,128)(2,1)} %constant_dynamic-update-slice_fusion.18.tokens_ref.refs_1_, bf16[8,512,1024]{2,1,0:T(8,128)(2,1)} %all-gather.3.cloned.1.call-done.gate_w.up_w, ...), custom_call_target="tpu_custom_call" | custom-call | flops 12884901888 | bytes 30408704 | tf_op jit(solution)/shard_map/forward/pallas_call | solution.py:382
  410.4 28.2 %hidden_back.2 = (bf16[1536,1024]{1,0:T(8,128)(2,1)}, bf16[1536,1024]{1,0:T(8,128)(2,1)}, bf16[1536,2048]{1,0:T(8,128)(2,1)}) custom-call(bf16[1536,2048]{1,0:T(8,128)(2,1)} %constant_dynamic-update-slice_fusion.21.grad_ref.refs_1_, f32[1536,1024]{1,0:T(8,128)} %get-tuple-element.291.gate_ref, f32[1536,1024]{1,0:T(8,128)} %get-tuple-element.292.up_ref, ...), custom_call_target="tpu_custom_call" | custom-call | flops 19327352832 | bytes 37748736 | tf_op jit(solution)/shard_map/hidden_back/pallas_call | solution.py:412
  441.1 11.8 %down_product.2 = bf16[1536,2048]{1,0:T(8,128)(2,1)} custom-call(bf16[1536,1024]{1,0:T(8,128)(2,1)} %get-tuple-element.332.hidden_ref.refs_3_, bf16[4,512,1024]{2,1,0:T(8,128)(2,1)} %all-gather.5.cloned.1.call-done.down_w), custom_call_target="tpu_custom_call" | custom-call | flops 6442450944 | bytes 13631488 | tf_op jit(solution)/shard_map/down_product/pallas_call | solution.py:437
  462.1 28.2 %hidden_back.3 = (bf16[1536,1024]{1,0:T(8,128)(2,1)}, bf16[1536,1024]{1,0:T(8,128)(2,1)}, bf16[1536,2048]{1,0:T(8,128)(2,1)}) custom-call(bf16[1536,2048]{1,0:T(8,128)(2,1)} %copy-done.101, f32[1536,1024]{1,0:T(8,128)} %get-tuple-element.305.gate_ref, f32[1536,1024]{1,0:T(8,128)} %get-tuple-element.306.up_ref, ...), custom_call_target="tpu_custom_call" | custom-call | flops 19327352832 | bytes 37748736 | tf_op jit(solution)/shard_map/hidden_back/pallas_call | solution.py:412
  511.6 18.6 %weight_grad.3 = bf16[4,512,1024]{2,1,0:T(8,128)(2,1)} custom-call(bf16[1536,2048]{1,0:T(8,128)(2,1)} %copy-done.101, bf16[1536,2048]{1,0:T(8,128)(2,1)} %constant_dynamic-update-slice_fusion.21.grad_ref.refs_1_, bf16[1536,1024]{1,0:T(8,128)(2,1)} %get-tuple-element.376.refs_2_.hidden_ref, bf16[1536,1024]{1,0:T(8,128)(2,1)} %get-tuple-element.332.hidden_ref.refs_3_), custom_call_target="tpu_custom_call" | custom-call | flops 12884901888 | bytes 18874368 | tf_op jit(solution)/shard_map/weight_grad/pallas_call | solution.py:340
  556.0 12.1 %attend_back.1 = (f32[24,64,384]{2,1,0:T(8,128)S(1)}, bf16[8,2,320,384]{3,2,1,0:T(8,128)(2,1)}) custom-call(s32[2,8]{1,0:T(2,128)S(1)} %copy-done.27, s32[2]{0:T(128)S(1)} %copy-done.29, s32[8]{0:T(128)S(1)} %copy-done.33, s32[20]{0:T(128)S(1)} %copy-done.31, bf16[24,64,384]{2,1,0:T(8,128)(2,1)S(1)} %copy-done.15, bf16[24,64,384]{2,1,0:T(8,128)(2,1)S(1)} %bitcast.227, ...), custom_call_target="tpu_custom_call" | custom-call | flops 30198988800 | bytes 16777216 | tf_op jit(solution)/shard_map/attend_back/pallas_call | solution.py:178
  573.4 18.3 %collective-permute-done.41 = bf16[384,2048]{1,0:T(8,128)(2,1)S(1)} collective-permute-done((bf16[384,2048]{1,0:T(8,128)(2,1)}, bf16[384,2048]{1,0:T(8,128)(2,1)S(1)}, u32[]{:S(2)}, u32[]{:S(2)}) %collective-permute-start.41) | collective-permute-done | bytes 1572896 | tf_op jit(solution)/shard_map/ppermute | solution.py:31
  597.0 18.8 %weight_grad.4 = bf16[4,512,1024]{2,1,0:T(8,128)(2,1)} custom-call(bf16[1536,2048]{1,0:T(8,128)(2,1)} %constant_dynamic-update-slice_fusion.8.tokens_ref.refs_0_, bf16[1536,2048]{1,0:T(8,128)(2,1)} %constant_dynamic-update-slice_fusion.18.tokens_ref.refs_1_, bf16[1536,1024]{1,0:T(8,128)(2,1)} %get-tuple-element.354.refs_2_, ...), custom_call_target="tpu_custom_call" | custom-call | flops 12884901888 | bytes 18874368 | tf_op jit(solution)/shard_map/weight_grad/pallas_call | solution.py:340
  629.6 18.6 %weight_grad.5 = bf16[4,512,1024]{2,1,0:T(8,128)(2,1)} custom-call(bf16[1536,2048]{1,0:T(8,128)(2,1)} %constant_dynamic-update-slice_fusion.8.tokens_ref.refs_0_, bf16[1536,2048]{1,0:T(8,128)(2,1)} %constant_dynamic-update-slice_fusion.18.tokens_ref.refs_1_, bf16[1536,1024]{1,0:T(8,128)(2,1)} %get-tuple-element.366.refs_2_, ...), custom_call_target="tpu_custom_call" | custom-call | flops 12884901888 | bytes 18874368 | tf_op jit(solution)/shard_map/weight_grad/pallas_call | solution.py:340
  660.0 11.6 %down_product.3 = bf16[1536,2048]{1,0:T(8,128)(2,1)} custom-call(bf16[1536,1024]{1,0:T(8,128)(2,1)} %get-tuple-element.376.refs_2_.hidden_ref, bf16[4,512,1024]{2,1,0:T(8,128)(2,1)} %all-gather.5.cloned.1.call-done.down_w), custom_call_target="tpu_custom_call" | custom-call | flops 6442450944 | bytes 13631488 | tf_op jit(solution)/shard_map/down_product/pallas_call | solution.py:437
  674.8 36.8 %collective-permute-done.50 = bf16[640,384]{1,0:T(8,128)(2,1)} collective-permute-done((bf16[640,384]{1,0:T(8,128)(2,1)}, bf16[640,384]{1,0:T(8,128)(2,1)}, u32[]{:S(2)}, u32[]{:S(2)}) %collective-permute-start.50) | collective-permute-done | bytes 491552 | tf_op jit(solution)/shard_map/ppermute | solution.py:766
  741.4 23.1 %collective-permute-done.53 = bf16[640,384]{1,0:T(8,128)(2,1)S(1)} collective-permute-done((bf16[640,384]{1,0:T(8,128)(2,1)S(1)}, bf16[640,384]{1,0:T(8,128)(2,1)S(1)}, u32[]{:S(2)}, u32[]{:S(2)}) %collective-permute-start.53) | collective-permute-done | bytes 491552 | tf_op jit(solution)/shard_map/ppermute | solution.py:766
  807.5 15.2 %reduce-scatter.8.cloned.1.call-done = bf16[4,128,1024]{2,1,0:T(8,128)(2,1)} async-done(((bf16[4,512,1024]{2,1,0:T(8,128)(2,1)}), bf16[4,128,1024]{2,1,0:T(8,128)(2,1)}) %reduce-scatter.8.cloned.1.call-update) | async-done | bytes 1048592 | tf_op jit(solution)/shard_map/reduce_scatter | solution.py:711
  834.9 13.6 %collective-permute-done.61 = bf16[336,1024]{1,0:T(8,128)(2,1)} collective-permute-done((bf16[336,1024]{1,0:T(8,128)(2,1)}, bf16[336,1024]{1,0:T(8,128)(2,1)}, u32[]{:S(2)}, u32[]{:S(2)}) %collective-permute-start.61) | collective-permute-done | bytes 688160 | tf_op jit(solution)/shard_map/ppermute | solution.py:31
  921.0 10.0 %collective-permute-done.73 = bf16[256,768]{1,0:T(8,128)(2,1)S(1)} collective-permute-done((bf16[256,768]{1,0:T(8,128)(2,1)S(1)}, bf16[256,768]{1,0:T(8,128)(2,1)S(1)}, u32[]{:S(2)}, u32[]{:S(2)}) %collective-permute-start.73) | collective-permute-done | bytes 393248 | tf_op jit(solution)/shard_map/ppermute | solution.py:31
  (634 shorter events, 485.6 us)
Async XLA Ops:
  7.2 240.8 %all-gather.3.cloned.1.call-start = ((), (), s32[]{:S(2)}) async-start(), calls=%async_computation.3 | async-start | bytes 10485760 | tf_op jit(solution)/shard_map/all_gather | solution.py:642
  36.3 36.8 %collective-permute-start.3 = (bf16[2,384,1024]{2,1,0:T(8,128)(2,1)}, bf16[2,384,1024]{2,1,0:T(8,128)(2,1)}, u32[]{:S(2)}, u32[]{:S(2)}) collective-permute-start(bf16[2,384,1024]{2,1,0:T(8,128)(2,1)} %pad_maximum_fusion.15), channel_id=1, source_target_pairs={{0,16},{16,0},{1,17},{17,1},{2,18},{18,2},{3,19},{19,3},{4,20},{20... | collective-permute-start | bytes 4718600 | tf_op jit(solution)/shard_map/ppermute | solution.py:31
  77.6 284.0 %all-gather.5.cloned.1.call-start = ((), (), s32[]{:S(2)}) async-start(), calls=%async_computation.4 | async-start | bytes 5242880 | tf_op jit(solution)/shard_map/all_gather | solution.py:670
  100.8 56.3 %collective-permute-start.12 = (bf16[1024,768]{1,0:T(8,128)(2,1)S(1)}, bf16[1024,768]{1,0:T(8,128)(2,1)S(1)}, u32[]{:S(2)}, u32[]{:S(2)}) collective-permute-start(bf16[1024,768]{1,0:T(8,128)(2,1)S(1)} %pad_maximum_fusion.16), channel_id=1, source_target_pairs={{0,1},{1,0},{2,3},{3,2},{4,5},{5,4},{6,7},{7,6},{8,9},{9,8},{10,11... | collective-permute-start | bytes 4718600 | tf_op jit(solution)/shard_map/ppermute | solution.py:31
  100.8 54.3 %collective-permute-start.13 = (bf16[768,256]{1,0:T(8,128)(2,1)S(1)}, bf16[768,256]{1,0:T(8,128)(2,1)S(1)}, u32[]{:S(2)}, u32[]{:S(2)}) collective-permute-start(bf16[768,256]{1,0:T(8,128)(2,1)S(1)} %pad_maximum_fusion.37), channel_id=1, source_target_pairs={{0,4},{2,6},{4,0},{6,2},{1,5},{3,7},{5,1},{7,3},{8,12},{10,14},{12... | collective-permute-start | bytes 1179656 | tf_op jit(solution)/shard_map/ppermute | solution.py:31
  159.0 42.4 %collective-permute-start.15 = (bf16[1024,1536]{1,0:T(8,128)(2,1)}, bf16[1024,1536]{1,0:T(8,128)(2,1)}, u32[]{:S(2)}, u32[]{:S(2)}) collective-permute-start(bf16[1024,1536]{1,0:T(8,128)(2,1)} %pad_maximum_fusion.1), channel_id=1, source_target_pairs={{0,8},{8,0},{1,9},{9,1},{2,10},{10,2},{3,11},{11,3},{4,12},{12,4},... | collective-permute-start | bytes 9437192 | tf_op jit(solution)/shard_map/ppermute | solution.py:31
  160.4 86.5 %collective-permute-start.18 = (bf16[192,2048]{1,0:T(8,128)(2,1)}, bf16[192,2048]{1,0:T(8,128)(2,1)}, u32[]{:S(2)}, u32[]{:S(2)}) collective-permute-start(bf16[192,2048]{1,0:T(8,128)(2,1)} %get-tuple-element.568), channel_id=1, source_target_pairs={{0,1},{1,0},{2,3},{3,2},{4,5},{5,4},{6,7},{7,6},{8,9},{9,8},{10,11... | collective-permute-start | bytes 2359304 | tf_op jit(solution)/shard_map/ppermute | solution.py:31
  161.9 85.0 %collective-permute-start.19 = (bf16[192,2048]{1,0:T(8,128)(2,1)}, bf16[192,2048]{1,0:T(8,128)(2,1)}, u32[]{:S(2)}, u32[]{:S(2)}) collective-permute-start(bf16[192,2048]{1,0:T(8,128)(2,1)} %get-tuple-element.567), channel_id=1, source_target_pairs={{0,16},{16,0},{1,17},{17,1},{2,18},{18,2},{3,19},{19,3},{4,20},{20... | collective-permute-start | bytes 2359304 | tf_op jit(solution)/shard_map/ppermute | solution.py:31
  248.5 373.4 %reduce-scatter.4.cloned.1.call-start = ((), (), s32[]{:S(2)}) async-start(), calls=%async_computation.5 | async-start | bytes 5242880 | tf_op jit(solution)/shard_map/reduce_scatter | solution.py:711
  289.9 71.7 %collective-permute-start.24 = (bf16[384,2048]{1,0:T(8,128)(2,1)}, bf16[384,2048]{1,0:T(8,128)(2,1)}, u32[]{:S(2)}, u32[]{:S(2)}) collective-permute-start(bf16[384,2048]{1,0:T(8,128)(2,1)} %get-tuple-element.593), channel_id=1, source_target_pairs={{0,16},{16,0},{1,17},{17,1},{2,18},{18,2},{3,19},{19,3},{4,20},{20... | collective-permute-start | bytes 4718600 | tf_op jit(solution)/shard_map/ppermute | solution.py:31
  290.3 71.3 %collective-permute-start.25 = (bf16[384,2048]{1,0:T(8,128)(2,1)}, bf16[384,2048]{1,0:T(8,128)(2,1)}, u32[]{:S(2)}, u32[]{:S(2)}) collective-permute-start(bf16[384,2048]{1,0:T(8,128)(2,1)} %get-tuple-element.594), channel_id=1, source_target_pairs={{0,1},{1,0},{2,3},{3,2},{4,5},{5,4},{6,7},{7,6},{8,9},{9,8},{10,11... | collective-permute-start | bytes 4718600 | tf_op jit(solution)/shard_map/ppermute | solution.py:31
  364.1 37.0 %collective-permute-start.30 = (bf16[384,2048]{1,0:T(8,128)(2,1)}, bf16[384,2048]{1,0:T(8,128)(2,1)S(1)}, u32[]{:S(2)}, u32[]{:S(2)}) collective-permute-start(bf16[384,2048]{1,0:T(8,128)(2,1)} %get-tuple-element.591), channel_id=1, source_target_pairs={{0,16},{16,0},{1,17},{17,1},{2,18},{18,2},{3,19},{19,3},{4,20},{20... | collective-permute-start | bytes 4718600 | tf_op jit(solution)/shard_map/ppermute | solution.py:31
  365.6 36.5 %collective-permute-start.31 = (bf16[384,2048]{1,0:T(8,128)(2,1)S(1)}, bf16[384,2048]{1,0:T(8,128)(2,1)S(1)}, u32[]{:S(2)}, u32[]{:S(2)}) collective-permute-start(bf16[384,2048]{1,0:T(8,128)(2,1)S(1)} %copy-done.69), channel_id=1, source_target_pairs={{0,1},{1,0},{2,3},{3,2},{4,5},{5,4},{6,7},{7,6},{8,9},{9,8},{10,11... | collective-permute-start | bytes 4718600 | tf_op jit(solution)/shard_map/ppermute | solution.py:31
  460.1 36.8 %collective-permute-start.34 = (bf16[384,2048]{1,0:T(8,128)(2,1)}, bf16[384,2048]{1,0:T(8,128)(2,1)}, u32[]{:S(2)}, u32[]{:S(2)}) collective-permute-start(bf16[384,2048]{1,0:T(8,128)(2,1)} %get-tuple-element.540), channel_id=1, source_target_pairs={{0,16},{16,0},{1,17},{17,1},{2,18},{18,2},{3,19},{19,3},{4,20},{20... | collective-permute-start | bytes 4718600 | tf_op jit(solution)/shard_map/ppermute | solution.py:31
  533.0 243.5 %reduce-scatter.6.cloned.1.call-start = ((), (), s32[]{:S(2)}) async-start(), calls=%async_computation.6 | async-start | bytes 5242880 | tf_op jit(solution)/shard_map/reduce_scatter | solution.py:711
  554.7 37.0 %collective-permute-start.41 = (bf16[384,2048]{1,0:T(8,128)(2,1)}, bf16[384,2048]{1,0:T(8,128)(2,1)S(1)}, u32[]{:S(2)}, u32[]{:S(2)}) collective-permute-start(bf16[384,2048]{1,0:T(8,128)(2,1)} %get-tuple-element.536), channel_id=1, source_target_pairs={{0,16},{16,0},{1,17},{17,1},{2,18},{18,2},{3,19},{19,3},{4,20},{20... | collective-permute-start | bytes 4718600 | tf_op jit(solution)/shard_map/ppermute | solution.py:31
  555.4 36.7 %collective-permute-start.42 = (bf16[384,2048]{1,0:T(8,128)(2,1)}, bf16[384,2048]{1,0:T(8,128)(2,1)S(1)}, u32[]{:S(2)}, u32[]{:S(2)}) collective-permute-start(bf16[384,2048]{1,0:T(8,128)(2,1)} %get-tuple-element.535), channel_id=1, source_target_pairs={{0,1},{1,0},{2,3},{3,2},{4,5},{5,4},{6,7},{7,6},{8,9},{9,8},{10,11... | collective-permute-start | bytes 4718600 | tf_op jit(solution)/shard_map/ppermute | solution.py:31
  621.9 200.8 %reduce-scatter.8.cloned.1.call-start = ((), (), s32[]{:S(2)}) async-start(), calls=%async_computation.7 | async-start | bytes 5242880 | tf_op jit(solution)/shard_map/reduce_scatter | solution.py:711
  654.4 59.6 %collective-permute-start.51 = (bf16[2,128,1024]{2,1,0:T(8,128)(2,1)}, bf16[2,128,1024]{2,1,0:T(8,128)(2,1)}, u32[]{:S(2)}, u32[]{:S(2)}) collective-permute-start(bf16[2,128,1024]{2,1,0:T(8,128)(2,1)} %dynamic-slice_bitcast_fusion.5), channel_id=1, source_target_pairs={{0,16},{16,0},{1,17},{17,1},{2,18},{18,2},{3,19},{19,3},{4,20},{20... | collective-permute-start | bytes 1572872 | tf_op jit(solution)/shard_map/ppermute | solution.py:31
  657.4 54.3 %collective-permute-start.50 = (bf16[640,384]{1,0:T(8,128)(2,1)}, bf16[640,384]{1,0:T(8,128)(2,1)}, u32[]{:S(2)}, u32[]{:S(2)}) collective-permute-start(bf16[640,384]{1,0:T(8,128)(2,1)} %fusion.13), channel_id=1, source_target_pairs={{2,0},{4,2},{6,4},{3,1},{5,3},{7,5},{10,8},{12,10},{14,12},{11,9},... | collective-permute-start | bytes 1474568 | tf_op jit(solution)/shard_map/ppermute | solution.py:766
  719.5 48.1 %collective-permute-start.56 = (bf16[384,2048]{1,0:T(8,128)(2,1)}, bf16[384,2048]{1,0:T(8,128)(2,1)}, u32[]{:S(2)}, u32[]{:S(2)}) collective-permute-start(bf16[384,2048]{1,0:T(8,128)(2,1)} %get-tuple-element.524), channel_id=1, source_target_pairs={{0,8},{8,0},{1,9},{9,1},{2,10},{10,2},{3,11},{11,3},{4,12},{12,4},... | collective-permute-start | bytes 4718600 | tf_op jit(solution)/shard_map/ppermute | solution.py:31
  719.5 48.1 %collective-permute-start.57 = (bf16[384,2048]{1,0:T(8,128)(2,1)}, bf16[384,2048]{1,0:T(8,128)(2,1)}, u32[]{:S(2)}, u32[]{:S(2)}) collective-permute-start(bf16[384,2048]{1,0:T(8,128)(2,1)} %get-tuple-element.523), channel_id=1, source_target_pairs={{0,8},{8,0},{1,9},{9,1},{2,10},{10,2},{3,11},{11,3},{4,12},{12,4},... | collective-permute-start | bytes 4718600 | tf_op jit(solution)/shard_map/ppermute | solution.py:31
  726.1 47.7 %collective-permute-start.54 = (bf16[1024,1536]{1,0:T(8,128)(2,1)S(1)}, bf16[1024,1536]{1,0:T(8,128)(2,1)S(1)}, u32[]{:S(2)}, u32[]{:S(2)}) collective-permute-start(bf16[1024,1536]{1,0:T(8,128)(2,1)S(1)} %slice.511), channel_id=1, source_target_pairs={{0,8},{8,0},{1,9},{9,1},{2,10},{10,2},{3,11},{11,3},{4,12},{12,4},... | collective-permute-start | bytes 9437192 | tf_op jit(solution)/shard_map/ppermute | solution.py:31
  726.3 39.5 %collective-permute-start.55 = (bf16[2,128,1024]{2,1,0:T(8,128)(2,1)S(1)}, bf16[2,128,1024]{2,1,0:T(8,128)(2,1)S(1)}, u32[]{:S(2)}, u32[]{:S(2)}) collective-permute-start(bf16[2,128,1024]{2,1,0:T(8,128)(2,1)S(1)} %dynamic-slice_bitcast_fusion.4), channel_id=1, source_target_pairs={{0,8},{8,0},{1,9},{9,1},{2,10},{10,2},{3,11},{11,3},{4,12},{12,4},... | collective-permute-start | bytes 1572872 | tf_op jit(solution)/shard_map/ppermute | solution.py:31
  (177 other events, 2085.5 us)
Sparse Core Ops, SparseCore 0:
  77.7 170.2 all-gather.2
  249.6 112.0 all-gather.4
  533.1 75.1 reduce-scatter.3
  622.1 117.7 reduce-scatter.5
  742.0 80.7 reduce-scatter.7

commit v3 on v2

--- a/solution.py
+++ b/solution.py
@@ -772,39 +772,29 @@
     summed, grad_kv, grad_query, out_w_low, out_w_high, normed_all, grads, grad_gate_w, grad_down = stage(
         summed, grad_kv, grad_query, out_w_low, out_w_high, normed_all, grads, grad_gate_w, grad_down
     )
-    grad_gate_w = scattered(grad_gate_w)
 
     summed = to_owner(grad_kv[2]) + down(summed)
-    grad_up_w = weight_grad(normed_all, [g[1] for g in grads], plane)
     out_w_high = fold(out_w_high, "row", 1)
-    summed, grad_kv, grad_query, out_w_low, out_w_high, grad_up_w, grad_down, hidden = stage(
-        summed, grad_kv, grad_query, out_w_low, out_w_high, grad_up_w, grad_down, hidden
-    )
-    grad_up_w = scattered(grad_up_w)
+    summed, grad_kv, grad_query, out_w_low, out_w_high, grad_gate_w, grad_down = stage(
+        summed, grad_kv, grad_query, out_w_low, out_w_high, grad_gate_w, grad_down
+    )
 
     summed = to_owner(grad_kv[1]) + down(summed)
     grad_query_proj, grad_q_gain = head_back(query_proj, q_gain, turn, grad_query)
     grad_query_low = grad_query_proj.astype(BF16).reshape(all_slots * HEAD_DIM, own_tokens)
-    near_part = output_part(0)
     grad_down = row_out(grad_down)
-    summed, grad_query_low, grad_q_gain, grad_kv, grad_down, out_w_low, out_w_high, near_part = stage(
-        summed, grad_query_low, grad_q_gain, grad_kv, grad_down, out_w_low, out_w_high, near_part
-    )
+    summed, grad_query_low, grad_q_gain, grad_kv, grad_down, out_w_low, out_w_high, grad_gate_w = stage(
+        summed, grad_query_low, grad_q_gain, grad_kv, grad_down, out_w_low, out_w_high, grad_gate_w
+    )
+    grad_gate_w = scattered(grad_gate_w)
 
     summed = to_owner(grad_kv[0]) + down(summed)
     grad_query_w = dot(normed_near, grad_query_low, (0, 1)).astype(BF16)
     grad_query_w = fold(grad_query_w, "core", 0)
     grad_normed_near = dot(grad_query_low, query_full, (0, 1))
     grad_down = core_out(grad_down)
-    if two:
-        own_part, near_part = near_part[: 2 * own_tokens], near_part[2 * own_tokens :]
-        near = own_half(near_part, swap(other_half(near_part), "core"))
-        own = own_half(own_part, swap(other_half(own_part), "core"))
-        sends = near_sends(near, *output_hops)
-    else:
-        own, sends = near_part, summed
-    summed, grad_query_w, grad_normed_near, grad_down, out_w_low, out_w_high, sends, own, grad_gate_w = stage(
-        summed, grad_query_w, grad_normed_near, grad_down, out_w_low, out_w_high, sends, own, grad_gate_w
+    summed, grad_query_w, grad_normed_near, grad_down, out_w_low, out_w_high, normed_all, grads, hidden = stage(
+        summed, grad_query_w, grad_normed_near, grad_down, out_w_low, out_w_high, normed_all, grads, hidden
     )
 
     grad_key_proj, grad_k_gain = head_back(
@@ -828,8 +818,8 @@
     total = lax.dynamic_update_slice(total, small, (2 * kv_width, 0)).astype(BF16)
     query_w = fold(grad_query_w[:, : all_slots * 32], "row", 0), grad_query_w[:, all_slots * 32 :]
     grad_out_w = to_tp(jnp.concatenate([out_w_low, out_w_high]), 0)
-    total, query_w, grad_out_w, grad_gate_w, own, sends, grad_up_w = stage(
-        total, query_w, grad_out_w, grad_gate_w, own, sends, grad_up_w
+    total, query_w, grad_out_w, hidden, normed_all, grads = stage(
+        total, query_w, grad_out_w, hidden, normed_all, grads
     )
 
     def along(value, bit):
@@ -840,41 +830,47 @@
 
     if not two:
         total = lax.psum(total, ("row", "core", "ctx", "tp"))
-        output = residual + plane_sum(own).astype(F32)
+        output = residual + plane_sum(output_part(0)).astype(F32)
+        grad_up_w = scattered(weight_grad(normed_all, [g[1] for g in grads], plane))
         query_w = jnp.concatenate([query_w[0], fold(query_w[1], "row", 0)], axis=1)
         grad_query_w = fold(fold(to_tp(query_w, 1), "ctx", 0, 2), "ctx", 0)
         grad_out_w = fold(fold(grad_out_w, "ctx", 1, 2), "ctx", 1)
         grad_up_w, grad_gate_w = core_out(row_out(grad_up_w)), core_out(row_out(grad_gate_w))
     else:
         total = fold(total, "core", 1)
-        total, query_w, grad_out_w, grad_gate_w, own, sends = stage(
-            total, query_w, grad_out_w, grad_gate_w, own, sends
+        total, query_w, grad_out_w, hidden, normed_all, grads = stage(
+            total, query_w, grad_out_w, hidden, normed_all, grads
         )
         size = total.shape[0] // 2
         got = swap(lax.dynamic_slice_in_dim(total, (1 - tp_index) * size, size, 0), "tp")
         total = sum32(lax.dynamic_slice_in_dim(total, tp_index * size, size, 0), got)
         query_w = jnp.concatenate([query_w[0], fold(query_w[1], "row", 0)], axis=1)
-        total, grad_out_w, query_w, grad_gate_w, own, sends = stage(
-            total, grad_out_w, query_w, grad_gate_w, own, sends
+        grad_up_w = weight_grad(normed_all, [g[1] for g in grads], plane)
+        total, grad_out_w, query_w, hidden, grad_up_w, grad_gate_w = stage(
+            total, grad_out_w, query_w, hidden, grad_up_w, grad_gate_w
         )
+        grad_up_w = scattered(grad_up_w)
         total = fold(total, "row", 1)
         query_w = fold(query_w, "tp", 1)
-        total, query_w, sends, grad_gate_w, grad_out_w, grad_up_w = stage(
-            total, query_w, sends, grad_gate_w, grad_out_w, grad_up_w
+        near_part = output_part(0)
+        own_part, near_part = near_part[: 2 * own_tokens], near_part[2 * own_tokens :]
+        near = own_half(near_part, swap(other_half(near_part), "core"))
+        own = own_half(own_part, swap(other_half(own_part), "core"))
+        sends = near_sends(near, *output_hops)
+        total, query_w, sends, own, grad_gate_w, grad_out_w = stage(
+            total, query_w, sends, own, grad_gate_w, grad_out_w
         )
         total = along(total, 1)
         top_x, bottom_y = swap(sends[0], "tp"), swap(sends[1], "row")
         grad_out_w = fold(grad_out_w, "ctx", 1, 2)
-        total, query_w, grad_gate_w, top_x, bottom_y, grad_out_w, grad_up_w = stage(
-            total, query_w, grad_gate_w, top_x, bottom_y, grad_out_w, grad_up_w
+        total, query_w, grad_gate_w, top_x, bottom_y, grad_out_w = stage(
+            total, query_w, grad_gate_w, top_x, bottom_y, grad_out_w
         )
         total = along(total, 2)
         output = residual + plane_total(own, *output_hops, top_x, bottom_y)
         grad_gate_w = row_out(grad_gate_w)
         grad_out_w = fold(grad_out_w, "ctx", 1)
-        total, query_w, grad_gate_w, grad_up_w, grad_out_w, output = stage(
-            total, query_w, grad_gate_w, grad_up_w, grad_out_w, output
-        )
+        total, query_w, grad_gate_w, grad_out_w, output = stage(total, query_w, grad_gate_w, grad_out_w, output)
         total = join(total, "row", 1)
         query_w = fold(query_w, "ctx", 0, 2)
         grad_gate_w = core_out(grad_gate_w)

time: 986 us -> 979 us (level)
    ppermute x74, waiting for transfers between devices: 265 us -> 307 us  [swap(): return lax.ppermute(value, axis, [(i, i ^ bit) for i in range(size)])]
    ppermute x3, waiting for transfers between devices: 60 us -> 32.2 us  [down(): lax.ppermute(value.astype(BF16), 'ctx', [(j, j - 1) for j in range(1, ctx)])]
    reduce_scatter x3, waiting for transfers between devices: 15.2 us -> 0.02 us  [scattered(): return lax.psum_scatter(gradient, 'ctx', scatter_dimension=1, tiled=True)]
    unnamed x255 -> x247, local copies, waits for them, and re-layouts: 42.7 us -> 44 us
  transfers between devices with their start and end apart: 85 -> 85, of which waited for: 41 -> 41; matrix products, arithmetic and copies ran while one was open for 21% -> 21% of each run, Pallas kernels for 18% -> 17%
where the time goes in v3:
time: 979 us; the launch traced here: 973 us
  waiting for transfers between devices  389 us (40%)
  Pallas kernels  210 us (21%)
  other arithmetic  131 us (13%)
  local copies, waits for them, and re-layouts  98.4 us (10%)
  starting transfers between devices  92.9 us (9%)
  matrix products  34.4 us (4%)
  between operations  17.6 us (2%)
    ppermute x74, waiting for transfers between devices, swap(): return lax.ppermute(value, axis, [(i, i ^ bit) for i in range(size)])  307 us
    ppermute x74, starting transfers between devices, swap(): return lax.ppermute(value, axis, [(i, i ^ bit) for i in range(size)])  79.6 us
    pallas_call x2, Pallas kernels, hidden_back(): pl.pallas_call(hidden_back_kernel, grid=(count // tile,), in_specs=[tall(...  56.5 us
    pallas_call x3, Pallas kernels, weight_grad(): pl.pallas_call(weight_grad_kernel, grid=(blocks,), in_specs=[pl.BlockSpec...  56 us
    all_gather x1, waiting for transfers between devices, body(): down_full = lax.all_gather(packed, 'ctx', axis=1, tiled=True)  44.6 us
    unnamed x247, local copies, waits for them, and re-layouts  44 us
    pallas_call x2, Pallas kernels, forward(): pl.pallas_call(forward_kernel, grid=(count // tile,), in_specs=[tall(tile...  38.4 us
    dot_general x9, matrix products, dot(): lax.dot_general(left, right, ((contract[:1], contract[1:]), ((), ())), pr...  34.4 us
  transfers between devices with their start and end apart: 85, of which 41 were waited for; matrix products, arithmetic and copies ran while one was open for 21% of the time, Pallas kernels for 17%

profile of v3, /device:TPU:0, one launch (start us, length us, event | category | flops | bytes accessed | tf_op | source)
XLA Modules:
  0.0 972.9 jit_solution(713912651351955024)
XLA Ops:
  46.5 12.1 %collective-permute-done.6 = bf16[256,768]{1,0:T(8,128)(2,1)} collective-permute-done((bf16[256,768]{1,0:T(8,128)(2,1)}, bf16[256,768]{1,0:T(8,128)(2,1)}, u32[]{:S(2)}, u32[]{:S(2)}) %collective-permute-start.6) | collective-permute-done | bytes 393248 | tf_op jit(solution)/shard_map/ppermute | solution.py:31
  100.8 20.4 %collective-permute-start.13 = (bf16[768,256]{1,0:T(8,128)(2,1)S(1)}, bf16[768,256]{1,0:T(8,128)(2,1)S(1)}, u32[]{:S(2)}, u32[]{:S(2)}) collective-permute-start(bf16[768,256]{1,0:T(8,128)(2,1)S(1)} %pad_maximum_fusion.37), channel_id=1, source_target_pairs={{0,4},{2,6},{4,0},{6,2},{1,5},{3,7},{5,1},{7,3},{8,12},{10,14},{12... | collective-permute-start | bytes 1179656 | tf_op jit(solution)/shard_map/ppermute | solution.py:31
  124.8 30.3 %collective-permute-done.13 = bf16[768,256]{1,0:T(8,128)(2,1)S(1)} collective-permute-done((bf16[768,256]{1,0:T(8,128)(2,1)S(1)}, bf16[768,256]{1,0:T(8,128)(2,1)S(1)}, u32[]{:S(2)}, u32[]{:S(2)}) %collective-permute-start.13) | collective-permute-done | bytes 393248 | tf_op jit(solution)/shard_map/ppermute | solution.py:31
  169.8 21.2 %collective-permute-done.14 = bf16[640,384]{1,0:T(8,128)(2,1)S(1)} collective-permute-done((bf16[640,384]{1,0:T(8,128)(2,1)}, bf16[640,384]{1,0:T(8,128)(2,1)S(1)}, u32[]{:S(2)}, u32[]{:S(2)}) %collective-permute-start.14) | collective-permute-done | bytes 491552 | tf_op jit(solution)/shard_map/ppermute | solution.py:31
  225.6 17.6 %collective-permute-done.17 = bf16[768,1024]{1,0:T(8,128)(2,1)S(1)} collective-permute-done((bf16[768,1024]{1,0:T(8,128)(2,1)}, bf16[768,1024]{1,0:T(8,128)(2,1)S(1)}, u32[]{:S(2)}, u32[]{:S(2)}) %collective-permute-start.17) | collective-permute-done | bytes 1572896 | tf_op jit(solution)/shard_map/ppermute | solution.py:31
  270.8 12.6 %collective-permute-done.21 = bf16[192,2048]{1,0:T(8,128)(2,1)S(1)} collective-permute-done((bf16[192,2048]{1,0:T(8,128)(2,1)S(1)}, bf16[192,2048]{1,0:T(8,128)(2,1)S(1)}, u32[]{:S(2)}, u32[]{:S(2)}) %collective-permute-start.21) | collective-permute-done | bytes 786464 | tf_op jit(solution)/shard_map/ppermute | solution.py:31
  296.5 19.2 %forward.2 = (f32[1536,1024]{1,0:T(8,128)}, f32[1536,1024]{1,0:T(8,128)}, bf16[1536,1024]{1,0:T(8,128)(2,1)}) custom-call(bf16[1536,2048]{1,0:T(8,128)(2,1)} %constant_dynamic-update-slice_fusion.8.tokens_ref.refs_0_, bf16[8,512,1024]{2,1,0:T(8,128)(2,1)} %all-gather.3.cloned.1.call-done.gate_w.up_w, ...), custom_call_target="tpu_custom_call" | custom-call | flops 12884901888 | bytes 30408704 | tf_op jit(solution)/shard_map/forward/pallas_call | solution.py:382
  315.7 44.6 %all-gather.5.cloned.1.call-done.down_w = bf16[4,512,1024]{2,1,0:T(8,128)(2,1)} async-done(((bf16[4,128,1024]{2,1,0:T(8,128)(2,1)}), bf16[4,512,1024]{2,1,0:T(8,128)(2,1)}) %all-gather.5.cloned.1.call-update) | async-done | bytes 4194320 | tf_op jit(solution)/shard_map/all_gather | solution.py:670
  373.3 19.2 %forward.3 = (f32[1536,1024]{1,0:T(8,128)}, f32[1536,1024]{1,0:T(8,128)}, bf16[1536,1024]{1,0:T(8,128)(2,1)}) custom-call(bf16[1536,2048]{1,0:T(8,128)(2,1)} %constant_dynamic-update-slice_fusion.18.tokens_ref.refs_1_, bf16[8,512,1024]{2,1,0:T(8,128)(2,1)} %all-gather.3.cloned.1.call-done.gate_w.up_w, ...), custom_call_target="tpu_custom_call" | custom-call | flops 12884901888 | bytes 30408704 | tf_op jit(solution)/shard_map/forward/pallas_call | solution.py:382
  409.1 28.2 %hidden_back.2 = (bf16[1536,1024]{1,0:T(8,128)(2,1)}, bf16[1536,1024]{1,0:T(8,128)(2,1)}, bf16[1536,2048]{1,0:T(8,128)(2,1)}) custom-call(bf16[1536,2048]{1,0:T(8,128)(2,1)} %constant_dynamic-update-slice_fusion.21.grad_ref.refs_1_, f32[1536,1024]{1,0:T(8,128)} %get-tuple-element.289.gate_ref, f32[1536,1024]{1,0:T(8,128)} %get-tuple-element.290.up_ref, ...), custom_call_target="tpu_custom_call" | custom-call | flops 19327352832 | bytes 37748736 | tf_op jit(solution)/shard_map/hidden_back/pallas_call | solution.py:412
  439.8 11.6 %down_product.2 = bf16[1536,2048]{1,0:T(8,128)(2,1)} custom-call(bf16[1536,1024]{1,0:T(8,128)(2,1)} %get-tuple-element.330.hidden_ref.refs_3_, bf16[4,512,1024]{2,1,0:T(8,128)(2,1)} %all-gather.5.cloned.1.call-done.down_w), custom_call_target="tpu_custom_call" | custom-call | flops 6442450944 | bytes 13631488 | tf_op jit(solution)/shard_map/down_product/pallas_call | solution.py:437
  460.5 28.3 %hidden_back.3 = (bf16[1536,1024]{1,0:T(8,128)(2,1)}, bf16[1536,1024]{1,0:T(8,128)(2,1)}, bf16[1536,2048]{1,0:T(8,128)(2,1)}) custom-call(bf16[1536,2048]{1,0:T(8,128)(2,1)} %copy-done.101, f32[1536,1024]{1,0:T(8,128)} %get-tuple-element.303.gate_ref, f32[1536,1024]{1,0:T(8,128)} %get-tuple-element.304.up_ref, ...), custom_call_target="tpu_custom_call" | custom-call | flops 19327352832 | bytes 37748736 | tf_op jit(solution)/shard_map/hidden_back/pallas_call | solution.py:412
  510.0 18.6 %weight_grad.3 = bf16[4,512,1024]{2,1,0:T(8,128)(2,1)} custom-call(bf16[1536,2048]{1,0:T(8,128)(2,1)} %copy-done.101, bf16[1536,2048]{1,0:T(8,128)(2,1)} %constant_dynamic-update-slice_fusion.21.grad_ref.refs_1_, bf16[1536,1024]{1,0:T(8,128)(2,1)} %get-tuple-element.417.refs_2_.hidden_ref, bf16[1536,1024]{1,0:T(8,128)(2,1)} %get-tuple-element.330.hidden_ref.refs_3_), custom_call_target="tpu_custom_call" | custom-call | flops 12884901888 | bytes 18874368 | tf_op jit(solution)/shard_map/weight_grad/pallas_call | solution.py:340
  554.6 12.2 %attend_back.1 = (f32[24,64,384]{2,1,0:T(8,128)S(1)}, bf16[8,2,320,384]{3,2,1,0:T(8,128)(2,1)}) custom-call(s32[2,8]{1,0:T(2,128)S(1)} %copy-done.27, s32[2]{0:T(128)S(1)} %copy-done.29, s32[8]{0:T(128)S(1)} %copy-done.33, s32[20]{0:T(128)S(1)} %copy-done.31, bf16[24,64,384]{2,1,0:T(8,128)(2,1)S(1)} %copy-done.15, bf16[24,64,384]{2,1,0:T(8,128)(2,1)S(1)} %bitcast.227, ...), custom_call_target="tpu_custom_call" | custom-call | flops 30198988800 | bytes 16777216 | tf_op jit(solution)/shard_map/attend_back/pallas_call | solution.py:178
  572.0 18.4 %collective-permute-done.41 = bf16[384,2048]{1,0:T(8,128)(2,1)S(1)} collective-permute-done((bf16[384,2048]{1,0:T(8,128)(2,1)}, bf16[384,2048]{1,0:T(8,128)(2,1)S(1)}, u32[]{:S(2)}, u32[]{:S(2)}) %collective-permute-start.41) | collective-permute-done | bytes 1572896 | tf_op jit(solution)/shard_map/ppermute | solution.py:31
  595.8 18.8 %weight_grad.4 = bf16[4,512,1024]{2,1,0:T(8,128)(2,1)} custom-call(bf16[1536,2048]{1,0:T(8,128)(2,1)} %constant_dynamic-update-slice_fusion.8.tokens_ref.refs_0_, bf16[1536,2048]{1,0:T(8,128)(2,1)} %constant_dynamic-update-slice_fusion.18.tokens_ref.refs_1_, bf16[1536,1024]{1,0:T(8,128)(2,1)} %get-tuple-element.352.refs_2_, ...), custom_call_target="tpu_custom_call" | custom-call | flops 12884901888 | bytes 18874368 | tf_op jit(solution)/shard_map/weight_grad/pallas_call | solution.py:340
  658.5 16.2 %collective-permute-done.50 = bf16[640,384]{1,0:T(8,128)(2,1)} collective-permute-done((bf16[640,384]{1,0:T(8,128)(2,1)}, bf16[640,384]{1,0:T(8,128)(2,1)}, u32[]{:S(2)}, u32[]{:S(2)}) %collective-permute-start.50) | collective-permute-done | bytes 491552 | tf_op jit(solution)/shard_map/ppermute | solution.py:766
  702.7 12.8 %collective-permute-done.53 = bf16[640,384]{1,0:T(8,128)(2,1)} collective-permute-done((bf16[640,384]{1,0:T(8,128)(2,1)}, bf16[640,384]{1,0:T(8,128)(2,1)}, u32[]{:S(2)}, u32[]{:S(2)}) %collective-permute-start.53) | collective-permute-done | bytes 491552 | tf_op jit(solution)/shard_map/ppermute | solution.py:766
  763.5 18.6 %weight_grad.5 = bf16[4,512,1024]{2,1,0:T(8,128)(2,1)} custom-call(bf16[1536,2048]{1,0:T(8,128)(2,1)} %constant_dynamic-update-slice_fusion.8.tokens_ref.refs_0_, bf16[1536,2048]{1,0:T(8,128)(2,1)} %constant_dynamic-update-slice_fusion.18.tokens_ref.refs_1_, bf16[1536,1024]{1,0:T(8,128)(2,1)} %get-tuple-element.412.refs_2_, ...), custom_call_target="tpu_custom_call" | custom-call | flops 12884901888 | bytes 18874368 | tf_op jit(solution)/shard_map/weight_grad/pallas_call | solution.py:340
  785.8 11.7 %down_product.3 = bf16[1536,2048]{1,0:T(8,128)(2,1)} custom-call(bf16[1536,1024]{1,0:T(8,128)(2,1)} %get-tuple-element.417.refs_2_.hidden_ref, bf16[4,512,1024]{2,1,0:T(8,128)(2,1)} %all-gather.5.cloned.1.call-done.down_w), custom_call_target="tpu_custom_call" | custom-call | flops 6442450944 | bytes 13631488 | tf_op jit(solution)/shard_map/down_product/pallas_call | solution.py:437
  829.1 26.3 %collective-permute-done.65 = bf16[336,512]{1,0:T(8,128)(2,1)S(1)} collective-permute-done((bf16[336,512]{1,0:T(8,128)(2,1)S(1)}, bf16[336,512]{1,0:T(8,128)(2,1)S(1)}, u32[]{:S(2)}, u32[]{:S(2)}) %collective-permute-start.65) | collective-permute-done | bytes 344096 | tf_op jit(solution)/shard_map/ppermute | solution.py:31
  855.6 13.9 %collective-permute-done.68 = bf16[768,256]{1,0:T(8,128)(2,1)S(1)} collective-permute-done((bf16[768,256]{1,0:T(8,128)(2,1)S(1)}, bf16[768,256]{1,0:T(8,128)(2,1)S(1)}, u32[]{:S(2)}, u32[]{:S(2)}) %collective-permute-start.68) | collective-permute-done | bytes 393248 | tf_op jit(solution)/shard_map/ppermute | solution.py:31
  873.9 14.2 %collective-permute-done.71 = bf16[768,128]{1,0:T(8,128)(2,1)S(1)} collective-permute-done((bf16[768,128]{1,0:T(8,128)(2,1)S(1)}, bf16[768,128]{1,0:T(8,128)(2,1)S(1)}, u32[]{:S(2)}, u32[]{:S(2)}) %collective-permute-start.71) | collective-permute-done | bytes 196640 | tf_op jit(solution)/shard_map/ppermute | solution.py:31
  888.8 17.0 %collective-permute-done.69 = bf16[336,512]{1,0:T(8,128)(2,1)S(1)} collective-permute-done((bf16[336,512]{1,0:T(8,128)(2,1)S(1)}, bf16[336,512]{1,0:T(8,128)(2,1)S(1)}, u32[]{:S(2)}, u32[]{:S(2)}) %collective-permute-start.69) | collective-permute-done | bytes 344096 | tf_op jit(solution)/shard_map/ppermute | solution.py:31
  (624 shorter events, 491.4 us)
Async XLA Ops:
  7.2 240.8 %all-gather.3.cloned.1.call-start = ((), (), s32[]{:S(2)}) async-start(), calls=%async_computation.3 | async-start | bytes 10485760 | tf_op jit(solution)/shard_map/all_gather | solution.py:642
  36.3 36.8 %collective-permute-start.3 = (bf16[2,384,1024]{2,1,0:T(8,128)(2,1)}, bf16[2,384,1024]{2,1,0:T(8,128)(2,1)}, u32[]{:S(2)}, u32[]{:S(2)}) collective-permute-start(bf16[2,384,1024]{2,1,0:T(8,128)(2,1)} %pad_maximum_fusion.15), channel_id=1, source_target_pairs={{0,16},{16,0},{1,17},{17,1},{2,18},{18,2},{3,19},{19,3},{4,20},{20... | collective-permute-start | bytes 4718600 | tf_op jit(solution)/shard_map/ppermute | solution.py:31
  77.6 282.7 %all-gather.5.cloned.1.call-start = ((), (), s32[]{:S(2)}) async-start(), calls=%async_computation.4 | async-start | bytes 5242880 | tf_op jit(solution)/shard_map/all_gather | solution.py:670
  100.8 56.3 %collective-permute-start.12 = (bf16[1024,768]{1,0:T(8,128)(2,1)S(1)}, bf16[1024,768]{1,0:T(8,128)(2,1)S(1)}, u32[]{:S(2)}, u32[]{:S(2)}) collective-permute-start(bf16[1024,768]{1,0:T(8,128)(2,1)S(1)} %pad_maximum_fusion.16), channel_id=1, source_target_pairs={{0,1},{1,0},{2,3},{3,2},{4,5},{5,4},{6,7},{7,6},{8,9},{9,8},{10,11... | collective-permute-start | bytes 4718600 | tf_op jit(solution)/shard_map/ppermute | solution.py:31
  100.8 54.2 %collective-permute-start.13 = (bf16[768,256]{1,0:T(8,128)(2,1)S(1)}, bf16[768,256]{1,0:T(8,128)(2,1)S(1)}, u32[]{:S(2)}, u32[]{:S(2)}) collective-permute-start(bf16[768,256]{1,0:T(8,128)(2,1)S(1)} %pad_maximum_fusion.37), channel_id=1, source_target_pairs={{0,4},{2,6},{4,0},{6,2},{1,5},{3,7},{5,1},{7,3},{8,12},{10,14},{12... | collective-permute-start | bytes 1179656 | tf_op jit(solution)/shard_map/ppermute | solution.py:31
  159.0 42.3 %collective-permute-start.15 = (bf16[1024,1536]{1,0:T(8,128)(2,1)}, bf16[1024,1536]{1,0:T(8,128)(2,1)}, u32[]{:S(2)}, u32[]{:S(2)}) collective-permute-start(bf16[1024,1536]{1,0:T(8,128)(2,1)} %pad_maximum_fusion.1), channel_id=1, source_target_pairs={{0,8},{8,0},{1,9},{9,1},{2,10},{10,2},{3,11},{11,3},{4,12},{12,4},... | collective-permute-start | bytes 9437192 | tf_op jit(solution)/shard_map/ppermute | solution.py:31
  160.3 86.5 %collective-permute-start.18 = (bf16[192,2048]{1,0:T(8,128)(2,1)}, bf16[192,2048]{1,0:T(8,128)(2,1)}, u32[]{:S(2)}, u32[]{:S(2)}) collective-permute-start(bf16[192,2048]{1,0:T(8,128)(2,1)} %get-tuple-element.564), channel_id=1, source_target_pairs={{0,1},{1,0},{2,3},{3,2},{4,5},{5,4},{6,7},{7,6},{8,9},{9,8},{10,11... | collective-permute-start | bytes 2359304 | tf_op jit(solution)/shard_map/ppermute | solution.py:31
  161.8 85.0 %collective-permute-start.19 = (bf16[192,2048]{1,0:T(8,128)(2,1)}, bf16[192,2048]{1,0:T(8,128)(2,1)}, u32[]{:S(2)}, u32[]{:S(2)}) collective-permute-start(bf16[192,2048]{1,0:T(8,128)(2,1)} %get-tuple-element.563), channel_id=1, source_target_pairs={{0,16},{16,0},{1,17},{17,1},{2,18},{18,2},{3,19},{19,3},{4,20},{20... | collective-permute-start | bytes 2359304 | tf_op jit(solution)/shard_map/ppermute | solution.py:31
  207.4 35.8 %collective-permute-start.17 = (bf16[768,1024]{1,0:T(8,128)(2,1)}, bf16[768,1024]{1,0:T(8,128)(2,1)S(1)}, u32[]{:S(2)}, u32[]{:S(2)}) collective-permute-start(bf16[768,1024]{1,0:T(8,128)(2,1)} %pad_maximum_fusion.17), channel_id=1, source_target_pairs={{0,1},{1,0},{2,3},{3,2},{4,5},{5,4},{6,7},{7,6},{8,9},{9,8},{10,11... | collective-permute-start | bytes 4718600 | tf_op jit(solution)/shard_map/ppermute | solution.py:31
  248.5 372.1 %reduce-scatter.4.cloned.1.call-start = ((), (), s32[]{:S(2)}) async-start(), calls=%async_computation.5 | async-start | bytes 5242880 | tf_op jit(solution)/shard_map/reduce_scatter | solution.py:711
  290.1 70.2 %collective-permute-start.24 = (bf16[384,2048]{1,0:T(8,128)(2,1)}, bf16[384,2048]{1,0:T(8,128)(2,1)}, u32[]{:S(2)}, u32[]{:S(2)}) collective-permute-start(bf16[384,2048]{1,0:T(8,128)(2,1)} %get-tuple-element.589), channel_id=1, source_target_pairs={{0,16},{16,0},{1,17},{17,1},{2,18},{18,2},{3,19},{19,3},{4,20},{20... | collective-permute-start | bytes 4718600 | tf_op jit(solution)/shard_map/ppermute | solution.py:31
  290.5 69.7 %collective-permute-start.25 = (bf16[384,2048]{1,0:T(8,128)(2,1)}, bf16[384,2048]{1,0:T(8,128)(2,1)}, u32[]{:S(2)}, u32[]{:S(2)}) collective-permute-start(bf16[384,2048]{1,0:T(8,128)(2,1)} %get-tuple-element.590), channel_id=1, source_target_pairs={{0,1},{1,0},{2,3},{3,2},{4,5},{5,4},{6,7},{7,6},{8,9},{9,8},{10,11... | collective-permute-start | bytes 4718600 | tf_op jit(solution)/shard_map/ppermute | solution.py:31
  362.7 37.0 %collective-permute-start.30 = (bf16[384,2048]{1,0:T(8,128)(2,1)}, bf16[384,2048]{1,0:T(8,128)(2,1)S(1)}, u32[]{:S(2)}, u32[]{:S(2)}) collective-permute-start(bf16[384,2048]{1,0:T(8,128)(2,1)} %get-tuple-element.587), channel_id=1, source_target_pairs={{0,16},{16,0},{1,17},{17,1},{2,18},{18,2},{3,19},{19,3},{4,20},{20... | collective-permute-start | bytes 4718600 | tf_op jit(solution)/shard_map/ppermute | solution.py:31
  364.3 36.5 %collective-permute-start.31 = (bf16[384,2048]{1,0:T(8,128)(2,1)S(1)}, bf16[384,2048]{1,0:T(8,128)(2,1)S(1)}, u32[]{:S(2)}, u32[]{:S(2)}) collective-permute-start(bf16[384,2048]{1,0:T(8,128)(2,1)S(1)} %copy-done.71), channel_id=1, source_target_pairs={{0,1},{1,0},{2,3},{3,2},{4,5},{5,4},{6,7},{7,6},{8,9},{9,8},{10,11... | collective-permute-start | bytes 4718600 | tf_op jit(solution)/shard_map/ppermute | solution.py:31
  458.5 36.8 %collective-permute-start.34 = (bf16[384,2048]{1,0:T(8,128)(2,1)}, bf16[384,2048]{1,0:T(8,128)(2,1)}, u32[]{:S(2)}, u32[]{:S(2)}) collective-permute-start(bf16[384,2048]{1,0:T(8,128)(2,1)} %get-tuple-element.536), channel_id=1, source_target_pairs={{0,16},{16,0},{1,17},{17,1},{2,18},{18,2},{3,19},{19,3},{4,20},{20... | collective-permute-start | bytes 4718600 | tf_op jit(solution)/shard_map/ppermute | solution.py:31
  459.1 36.4 %collective-permute-start.35 = (bf16[384,2048]{1,0:T(8,128)(2,1)}, bf16[384,2048]{1,0:T(8,128)(2,1)S(1)}, u32[]{:S(2)}, u32[]{:S(2)}) collective-permute-start(bf16[384,2048]{1,0:T(8,128)(2,1)} %get-tuple-element.535), channel_id=1, source_target_pairs={{0,1},{1,0},{2,3},{3,2},{4,5},{5,4},{6,7},{7,6},{8,9},{9,8},{10,11... | collective-permute-start | bytes 4718600 | tf_op jit(solution)/shard_map/ppermute | solution.py:31
  531.4 254.4 %reduce-scatter.6.cloned.1.call-start = ((), (), s32[]{:S(2)}) async-start(), calls=%async_computation.6 | async-start | bytes 5242880 | tf_op jit(solution)/shard_map/reduce_scatter | solution.py:711
  553.4 37.0 %collective-permute-start.41 = (bf16[384,2048]{1,0:T(8,128)(2,1)}, bf16[384,2048]{1,0:T(8,128)(2,1)S(1)}, u32[]{:S(2)}, u32[]{:S(2)}) collective-permute-start(bf16[384,2048]{1,0:T(8,128)(2,1)} %get-tuple-element.532), channel_id=1, source_target_pairs={{0,16},{16,0},{1,17},{17,1},{2,18},{18,2},{3,19},{19,3},{4,20},{20... | collective-permute-start | bytes 4718600 | tf_op jit(solution)/shard_map/ppermute | solution.py:31
  553.9 36.7 %collective-permute-start.42 = (bf16[384,2048]{1,0:T(8,128)(2,1)}, bf16[384,2048]{1,0:T(8,128)(2,1)S(1)}, u32[]{:S(2)}, u32[]{:S(2)}) collective-permute-start(bf16[384,2048]{1,0:T(8,128)(2,1)} %get-tuple-element.531), channel_id=1, source_target_pairs={{0,1},{1,0},{2,3},{3,2},{4,5},{5,4},{6,7},{7,6},{8,9},{9,8},{10,11... | collective-permute-start | bytes 4718600 | tf_op jit(solution)/shard_map/ppermute | solution.py:31
  690.2 237.3 %reduce-scatter.8.cloned.1.call-start = ((), (), s32[]{:S(2)}) async-start(), calls=%async_computation.7 | async-start | bytes 5242880 | tf_op jit(solution)/shard_map/reduce_scatter | solution.py:711
  828.0 41.7 %collective-permute-start.66 = (bf16[192,2048]{1,0:T(8,128)(2,1)S(1)}, bf16[192,2048]{1,0:T(8,128)(2,1)S(1)}, u32[]{:S(2)}, u32[]{:S(2)}) collective-permute-start(bf16[192,2048]{1,0:T(8,128)(2,1)S(1)} %get-tuple-element.425), channel_id=1, source_target_pairs={{0,1},{1,0},{2,3},{3,2},{4,5},{5,4},{6,7},{7,6},{8,9},{9,8},{10,11... | collective-permute-start | bytes 2359304 | tf_op jit(solution)/shard_map/ppermute | solution.py:31
  828.6 41.1 %collective-permute-start.67 = (bf16[192,2048]{1,0:T(8,128)(2,1)S(1)}, bf16[192,2048]{1,0:T(8,128)(2,1)S(1)}, u32[]{:S(2)}, u32[]{:S(2)}) collective-permute-start(bf16[192,2048]{1,0:T(8,128)(2,1)S(1)} %get-tuple-element.426), channel_id=1, source_target_pairs={{0,16},{16,0},{1,17},{17,1},{2,18},{18,2},{3,19},{19,3},{4,20},{20... | collective-permute-start | bytes 2359304 | tf_op jit(solution)/shard_map/ppermute | solution.py:31
  829.1 40.5 %collective-permute-start.68 = (bf16[768,256]{1,0:T(8,128)(2,1)S(1)}, bf16[768,256]{1,0:T(8,128)(2,1)S(1)}, u32[]{:S(2)}, u32[]{:S(2)}) collective-permute-start(bf16[768,256]{1,0:T(8,128)(2,1)S(1)} %slice.472), channel_id=1, source_target_pairs={{0,4},{2,6},{4,0},{6,2},{1,5},{3,7},{5,1},{7,3},{8,12},{10,14},{12... | collective-permute-start | bytes 1179656 | tf_op jit(solution)/shard_map/ppermute | solution.py:31
  869.9 36.1 %collective-permute-start.70 = (bf16[2,128,1024]{2,1,0:T(8,128)(2,1)S(1)}, bf16[2,128,1024]{2,1,0:T(8,128)(2,1)S(1)}, u32[]{:S(2)}, u32[]{:S(2)}) collective-permute-start(bf16[2,128,1024]{2,1,0:T(8,128)(2,1)S(1)} %dynamic-slice_bitcast_fusion.3), channel_id=1, source_target_pairs={{0,16},{16,0},{1,17},{17,1},{2,18},{18,2},{3,19},{19,3},{4,20},{20... | collective-permute-start | bytes 1572872 | tf_op jit(solution)/shard_map/ppermute | solution.py:31
  (173 other events, 2032.3 us)
Sparse Core Ops, SparseCore 0:
  77.7 170.2 all-gather.2
  249.5 110.7 all-gather.4
  531.5 75.0 reduce-scatter.3
  690.3 88.5 reduce-scatter.5
  797.7 104.7 reduce-scatter.7

commit v4 on v3

--- a/solution.py
+++ b/solution.py
@@ -786,16 +786,16 @@
     summed, grad_query_low, grad_q_gain, grad_kv, grad_down, out_w_low, out_w_high, grad_gate_w = stage(
         summed, grad_query_low, grad_q_gain, grad_kv, grad_down, out_w_low, out_w_high, grad_gate_w
     )
-    grad_gate_w = scattered(grad_gate_w)
 
     summed = to_owner(grad_kv[0]) + down(summed)
     grad_query_w = dot(normed_near, grad_query_low, (0, 1)).astype(BF16)
     grad_query_w = fold(grad_query_w, "core", 0)
     grad_normed_near = dot(grad_query_low, query_full, (0, 1))
     grad_down = core_out(grad_down)
-    summed, grad_query_w, grad_normed_near, grad_down, out_w_low, out_w_high, normed_all, grads, hidden = stage(
-        summed, grad_query_w, grad_normed_near, grad_down, out_w_low, out_w_high, normed_all, grads, hidden
-    )
+    summed, grad_query_w, grad_normed_near, grad_down, out_w_low, out_w_high, grad_gate_w, normed_all, grads, hidden = stage(
+        summed, grad_query_w, grad_normed_near, grad_down, out_w_low, out_w_high, grad_gate_w, normed_all, grads, hidden
+    )
+    grad_gate_w = scattered(grad_gate_w)
 
     grad_key_proj, grad_k_gain = head_back(
         key_proj, k_gain, turn, summed[:kv_width].reshape(KVH, HEAD_DIM, own_tokens)
@@ -846,9 +846,7 @@
         total = sum32(lax.dynamic_slice_in_dim(total, tp_index * size, size, 0), got)
         query_w = jnp.concatenate([query_w[0], fold(query_w[1], "row", 0)], axis=1)
         grad_up_w = weight_grad(normed_all, [g[1] for g in grads], plane)
-        total, grad_out_w, query_w, hidden, grad_up_w, grad_gate_w = stage(
-            total, grad_out_w, query_w, hidden, grad_up_w, grad_gate_w
-        )
+        total, grad_out_w, query_w, hidden, grad_up_w = stage(total, grad_out_w, query_w, hidden, grad_up_w)
         grad_up_w = scattered(grad_up_w)
         total = fold(total, "row", 1)
         query_w = fold(query_w, "tp", 1)

time: 979 us -> 980 us (level)
    unnamed x247 -> x259, local copies, waits for them, and re-layouts: 44 us -> 45 us
  transfers between devices with their start and end apart: 85 -> 85, of which waited for: 41 -> 41; matrix products, arithmetic and copies ran while one was open for 21% -> 21% of each run, Pallas kernels for 17% -> 18%
where the time goes in v4:
time: 980 us; the launch traced here: 974 us
  waiting for transfers between devices  383 us (39%)
  Pallas kernels  209 us (21%)
  other arithmetic  134 us (14%)
  local copies, waits for them, and re-layouts  100 us (10%)
  starting transfers between devices  96.8 us (10%)
  matrix products  34.4 us (4%)
  between operations  17.3 us (2%)
    ppermute x74, waiting for transfers between devices, swap(): return lax.ppermute(value, axis, [(i, i ^ bit) for i in range(size)])  301 us
    ppermute x74, starting transfers between devices, swap(): return lax.ppermute(value, axis, [(i, i ^ bit) for i in range(size)])  82.8 us
    pallas_call x2, Pallas kernels, hidden_back(): pl.pallas_call(hidden_back_kernel, grid=(count // tile,), in_specs=[tall(...  56.4 us
    pallas_call x3, Pallas kernels, weight_grad(): pl.pallas_call(weight_grad_kernel, grid=(blocks,), in_specs=[pl.BlockSpec...  56 us
    unnamed x259, local copies, waits for them, and re-layouts  45 us
    all_gather x1, waiting for transfers between devices, body(): down_full = lax.all_gather(packed, 'ctx', axis=1, tiled=True)  44.8 us
    pallas_call x2, Pallas kernels, forward(): pl.pallas_call(forward_kernel, grid=(count // tile,), in_specs=[tall(tile...  38.4 us
    dot_general x9, matrix products, dot(): lax.dot_general(left, right, ((contract[:1], contract[1:]), ((), ())), pr...  34.4 us
  transfers between devices with their start and end apart: 85, of which 41 were waited for; matrix products, arithmetic and copies ran while one was open for 21% of the time, Pallas kernels for 18%

profile of v4, /device:TPU:0, one launch (start us, length us, event | category | flops | bytes accessed | tf_op | source)
XLA Modules:
  0.0 974.3 jit_solution(16626535228963201180)
XLA Ops:
  46.5 12.1 %collective-permute-done.6 = bf16[256,768]{1,0:T(8,128)(2,1)} collective-permute-done((bf16[256,768]{1,0:T(8,128)(2,1)}, bf16[256,768]{1,0:T(8,128)(2,1)}, u32[]{:S(2)}, u32[]{:S(2)}) %collective-permute-start.6) | collective-permute-done | bytes 393248 | tf_op jit(solution)/shard_map/ppermute | solution.py:31
  100.8 20.4 %collective-permute-start.13 = (bf16[768,256]{1,0:T(8,128)(2,1)S(1)}, bf16[768,256]{1,0:T(8,128)(2,1)S(1)}, u32[]{:S(2)}, u32[]{:S(2)}) collective-permute-start(bf16[768,256]{1,0:T(8,128)(2,1)S(1)} %pad_maximum_fusion.37), channel_id=1, source_target_pairs={{0,4},{2,6},{4,0},{6,2},{1,5},{3,7},{5,1},{7,3},{8,12},{10,14},{12... | collective-permute-start | bytes 1179656 | tf_op jit(solution)/shard_map/ppermute | solution.py:31
  125.1 30.0 %collective-permute-done.13 = bf16[768,256]{1,0:T(8,128)(2,1)S(1)} collective-permute-done((bf16[768,256]{1,0:T(8,128)(2,1)S(1)}, bf16[768,256]{1,0:T(8,128)(2,1)S(1)}, u32[]{:S(2)}, u32[]{:S(2)}) %collective-permute-start.13) | collective-permute-done | bytes 393248 | tf_op jit(solution)/shard_map/ppermute | solution.py:31
  169.8 21.2 %collective-permute-done.14 = bf16[640,384]{1,0:T(8,128)(2,1)S(1)} collective-permute-done((bf16[640,384]{1,0:T(8,128)(2,1)}, bf16[640,384]{1,0:T(8,128)(2,1)S(1)}, u32[]{:S(2)}, u32[]{:S(2)}) %collective-permute-start.14) | collective-permute-done | bytes 491552 | tf_op jit(solution)/shard_map/ppermute | solution.py:31
  225.7 17.6 %collective-permute-done.17 = bf16[768,1024]{1,0:T(8,128)(2,1)S(1)} collective-permute-done((bf16[768,1024]{1,0:T(8,128)(2,1)}, bf16[768,1024]{1,0:T(8,128)(2,1)S(1)}, u32[]{:S(2)}, u32[]{:S(2)}) %collective-permute-start.17) | collective-permute-done | bytes 1572896 | tf_op jit(solution)/shard_map/ppermute | solution.py:31
  270.6 12.6 %collective-permute-done.21 = bf16[192,2048]{1,0:T(8,128)(2,1)S(1)} collective-permute-done((bf16[192,2048]{1,0:T(8,128)(2,1)S(1)}, bf16[192,2048]{1,0:T(8,128)(2,1)S(1)}, u32[]{:S(2)}, u32[]{:S(2)}) %collective-permute-start.21) | collective-permute-done | bytes 786464 | tf_op jit(solution)/shard_map/ppermute | solution.py:31
  296.3 19.2 %forward.2 = (f32[1536,1024]{1,0:T(8,128)}, f32[1536,1024]{1,0:T(8,128)}, bf16[1536,1024]{1,0:T(8,128)(2,1)}) custom-call(bf16[1536,2048]{1,0:T(8,128)(2,1)} %constant_dynamic-update-slice_fusion.8.tokens_ref.refs_0_, bf16[8,512,1024]{2,1,0:T(8,128)(2,1)} %all-gather.3.cloned.1.call-done.gate_w.up_w, ...), custom_call_target="tpu_custom_call" | custom-call | flops 12884901888 | bytes 30408704 | tf_op jit(solution)/shard_map/forward/pallas_call | solution.py:382
  315.5 44.8 %all-gather.5.cloned.1.call-done.down_w = bf16[4,512,1024]{2,1,0:T(8,128)(2,1)} async-done(((bf16[4,128,1024]{2,1,0:T(8,128)(2,1)}), bf16[4,512,1024]{2,1,0:T(8,128)(2,1)}) %all-gather.5.cloned.1.call-update) | async-done | bytes 4194320 | tf_op jit(solution)/shard_map/all_gather | solution.py:670
  373.3 19.2 %forward.3 = (f32[1536,1024]{1,0:T(8,128)}, f32[1536,1024]{1,0:T(8,128)}, bf16[1536,1024]{1,0:T(8,128)(2,1)}) custom-call(bf16[1536,2048]{1,0:T(8,128)(2,1)} %constant_dynamic-update-slice_fusion.18.tokens_ref.refs_1_, bf16[8,512,1024]{2,1,0:T(8,128)(2,1)} %all-gather.3.cloned.1.call-done.gate_w.up_w, ...), custom_call_target="tpu_custom_call" | custom-call | flops 12884901888 | bytes 30408704 | tf_op jit(solution)/shard_map/forward/pallas_call | solution.py:382
  409.1 28.2 %hidden_back.2 = (bf16[1536,1024]{1,0:T(8,128)(2,1)}, bf16[1536,1024]{1,0:T(8,128)(2,1)}, bf16[1536,2048]{1,0:T(8,128)(2,1)}) custom-call(bf16[1536,2048]{1,0:T(8,128)(2,1)} %constant_dynamic-update-slice_fusion.21.grad_ref.refs_1_, f32[1536,1024]{1,0:T(8,128)} %get-tuple-element.289.gate_ref, f32[1536,1024]{1,0:T(8,128)} %get-tuple-element.290.up_ref, ...), custom_call_target="tpu_custom_call" | custom-call | flops 19327352832 | bytes 37748736 | tf_op jit(solution)/shard_map/hidden_back/pallas_call | solution.py:412
  439.8 11.8 %down_product.2 = bf16[1536,2048]{1,0:T(8,128)(2,1)} custom-call(bf16[1536,1024]{1,0:T(8,128)(2,1)} %get-tuple-element.330.hidden_ref.refs_3_, bf16[4,512,1024]{2,1,0:T(8,128)(2,1)} %all-gather.5.cloned.1.call-done.down_w), custom_call_target="tpu_custom_call" | custom-call | flops 6442450944 | bytes 13631488 | tf_op jit(solution)/shard_map/down_product/pallas_call | solution.py:437
  460.8 28.2 %hidden_back.3 = (bf16[1536,1024]{1,0:T(8,128)(2,1)}, bf16[1536,1024]{1,0:T(8,128)(2,1)}, bf16[1536,2048]{1,0:T(8,128)(2,1)}) custom-call(bf16[1536,2048]{1,0:T(8,128)(2,1)} %copy-done.105, f32[1536,1024]{1,0:T(8,128)} %get-tuple-element.303.gate_ref, f32[1536,1024]{1,0:T(8,128)} %get-tuple-element.304.up_ref, ...), custom_call_target="tpu_custom_call" | custom-call | flops 19327352832 | bytes 37748736 | tf_op jit(solution)/shard_map/hidden_back/pallas_call | solution.py:412
  510.3 18.6 %weight_grad.3 = bf16[4,512,1024]{2,1,0:T(8,128)(2,1)} custom-call(bf16[1536,2048]{1,0:T(8,128)(2,1)} %copy-done.105, bf16[1536,2048]{1,0:T(8,128)(2,1)} %constant_dynamic-update-slice_fusion.21.grad_ref.refs_1_, bf16[1536,1024]{1,0:T(8,128)(2,1)} %get-tuple-element.417.refs_2_.hidden_ref, bf16[1536,1024]{1,0:T(8,128)(2,1)} %get-tuple-element.330.hidden_ref.refs_3_), custom_call_target="tpu_custom_call" | custom-call | flops 12884901888 | bytes 18874368 | tf_op jit(solution)/shard_map/weight_grad/pallas_call | solution.py:340
  554.5 12.2 %attend_back.1 = (f32[24,64,384]{2,1,0:T(8,128)S(1)}, bf16[8,2,320,384]{3,2,1,0:T(8,128)(2,1)}) custom-call(s32[2,8]{1,0:T(2,128)S(1)} %copy-done.27, s32[2]{0:T(128)S(1)} %copy-done.29, s32[8]{0:T(128)S(1)} %copy-done.33, s32[20]{0:T(128)S(1)} %copy-done.31, bf16[24,64,384]{2,1,0:T(8,128)(2,1)S(1)} %copy-done.15, bf16[24,64,384]{2,1,0:T(8,128)(2,1)S(1)} %bitcast.227, ...), custom_call_target="tpu_custom_call" | custom-call | flops 30198988800 | bytes 16777216 | tf_op jit(solution)/shard_map/attend_back/pallas_call | solution.py:178
  571.9 18.3 %collective-permute-done.41 = bf16[384,2048]{1,0:T(8,128)(2,1)S(1)} collective-permute-done((bf16[384,2048]{1,0:T(8,128)(2,1)}, bf16[384,2048]{1,0:T(8,128)(2,1)S(1)}, u32[]{:S(2)}, u32[]{:S(2)}) %collective-permute-start.41) | collective-permute-done | bytes 1572896 | tf_op jit(solution)/shard_map/ppermute | solution.py:31
  595.6 18.8 %weight_grad.4 = bf16[4,512,1024]{2,1,0:T(8,128)(2,1)} custom-call(bf16[1536,2048]{1,0:T(8,128)(2,1)} %constant_dynamic-update-slice_fusion.8.tokens_ref.refs_0_, bf16[1536,2048]{1,0:T(8,128)(2,1)} %constant_dynamic-update-slice_fusion.18.tokens_ref.refs_1_, bf16[1536,1024]{1,0:T(8,128)(2,1)} %get-tuple-element.352.refs_2_, ...), custom_call_target="tpu_custom_call" | custom-call | flops 12884901888 | bytes 18874368 | tf_op jit(solution)/shard_map/weight_grad/pallas_call | solution.py:340
  658.5 17.5 %collective-permute-done.50 = bf16[640,384]{1,0:T(8,128)(2,1)} collective-permute-done((bf16[640,384]{1,0:T(8,128)(2,1)}, bf16[640,384]{1,0:T(8,128)(2,1)}, u32[]{:S(2)}, u32[]{:S(2)}) %collective-permute-start.50) | collective-permute-done | bytes 491552 | tf_op jit(solution)/shard_map/ppermute | solution.py:766
  702.7 11.2 %collective-permute-done.53 = bf16[640,384]{1,0:T(8,128)(2,1)S(1)} collective-permute-done((bf16[640,384]{1,0:T(8,128)(2,1)}, bf16[640,384]{1,0:T(8,128)(2,1)S(1)}, u32[]{:S(2)}, u32[]{:S(2)}) %collective-permute-start.53) | collective-permute-done | bytes 491552 | tf_op jit(solution)/shard_map/ppermute | solution.py:766
  762.4 18.6 %weight_grad.5 = bf16[4,512,1024]{2,1,0:T(8,128)(2,1)} custom-call(bf16[1536,2048]{1,0:T(8,128)(2,1)} %constant_dynamic-update-slice_fusion.8.tokens_ref.refs_0_, bf16[1536,2048]{1,0:T(8,128)(2,1)} %constant_dynamic-update-slice_fusion.18.tokens_ref.refs_1_, bf16[1536,1024]{1,0:T(8,128)(2,1)} %get-tuple-element.413.refs_2_, ...), custom_call_target="tpu_custom_call" | custom-call | flops 12884901888 | bytes 18874368 | tf_op jit(solution)/shard_map/weight_grad/pallas_call | solution.py:340
  784.7 11.6 %down_product.3 = bf16[1536,2048]{1,0:T(8,128)(2,1)} custom-call(bf16[1536,1024]{1,0:T(8,128)(2,1)} %get-tuple-element.417.refs_2_.hidden_ref, bf16[4,512,1024]{2,1,0:T(8,128)(2,1)} %all-gather.5.cloned.1.call-done.down_w), custom_call_target="tpu_custom_call" | custom-call | flops 6442450944 | bytes 13631488 | tf_op jit(solution)/shard_map/down_product/pallas_call | solution.py:437
  829.1 23.9 %collective-permute-done.65 = bf16[336,512]{1,0:T(8,128)(2,1)S(1)} collective-permute-done((bf16[336,512]{1,0:T(8,128)(2,1)S(1)}, bf16[336,512]{1,0:T(8,128)(2,1)S(1)}, u32[]{:S(2)}, u32[]{:S(2)}) %collective-permute-start.65) | collective-permute-done | bytes 344096 | tf_op jit(solution)/shard_map/ppermute | solution.py:31
  853.2 16.2 %collective-permute-done.68 = bf16[768,256]{1,0:T(8,128)(2,1)S(1)} collective-permute-done((bf16[768,256]{1,0:T(8,128)(2,1)S(1)}, bf16[768,256]{1,0:T(8,128)(2,1)S(1)}, u32[]{:S(2)}, u32[]{:S(2)}) %collective-permute-start.68) | collective-permute-done | bytes 393248 | tf_op jit(solution)/shard_map/ppermute | solution.py:31
  876.3 12.6 %collective-permute-done.71 = bf16[768,128]{1,0:T(8,128)(2,1)S(1)} collective-permute-done((bf16[768,128]{1,0:T(8,128)(2,1)S(1)}, bf16[768,128]{1,0:T(8,128)(2,1)S(1)}, u32[]{:S(2)}, u32[]{:S(2)}) %collective-permute-start.71) | collective-permute-done | bytes 196640 | tf_op jit(solution)/shard_map/ppermute | solution.py:31
  889.7 21.2 %collective-permute-done.69 = bf16[336,512]{1,0:T(8,128)(2,1)S(1)} collective-permute-done((bf16[336,512]{1,0:T(8,128)(2,1)S(1)}, bf16[336,512]{1,0:T(8,128)(2,1)S(1)}, u32[]{:S(2)}, u32[]{:S(2)}) %collective-permute-start.69) | collective-permute-done | bytes 344096 | tf_op jit(solution)/shard_map/ppermute | solution.py:31
  (637 shorter events, 490.8 us)
Async XLA Ops:
  7.2 240.8 %all-gather.3.cloned.1.call-start = ((), (), s32[]{:S(2)}) async-start(), calls=%async_computation.3 | async-start | bytes 10485760 | tf_op jit(solution)/shard_map/all_gather | solution.py:642
  36.3 36.8 %collective-permute-start.3 = (bf16[2,384,1024]{2,1,0:T(8,128)(2,1)}, bf16[2,384,1024]{2,1,0:T(8,128)(2,1)}, u32[]{:S(2)}, u32[]{:S(2)}) collective-permute-start(bf16[2,384,1024]{2,1,0:T(8,128)(2,1)} %pad_maximum_fusion.15), channel_id=1, source_target_pairs={{0,16},{16,0},{1,17},{17,1},{2,18},{18,2},{3,19},{19,3},{4,20},{20... | collective-permute-start | bytes 4718600 | tf_op jit(solution)/shard_map/ppermute | solution.py:31
  77.6 282.7 %all-gather.5.cloned.1.call-start = ((), (), s32[]{:S(2)}) async-start(), calls=%async_computation.4 | async-start | bytes 5242880 | tf_op jit(solution)/shard_map/all_gather | solution.py:670
  100.8 56.3 %collective-permute-start.12 = (bf16[1024,768]{1,0:T(8,128)(2,1)S(1)}, bf16[1024,768]{1,0:T(8,128)(2,1)S(1)}, u32[]{:S(2)}, u32[]{:S(2)}) collective-permute-start(bf16[1024,768]{1,0:T(8,128)(2,1)S(1)} %pad_maximum_fusion.16), channel_id=1, source_target_pairs={{0,1},{1,0},{2,3},{3,2},{4,5},{5,4},{6,7},{7,6},{8,9},{9,8},{10,11... | collective-permute-start | bytes 4718600 | tf_op jit(solution)/shard_map/ppermute | solution.py:31
  100.8 54.3 %collective-permute-start.13 = (bf16[768,256]{1,0:T(8,128)(2,1)S(1)}, bf16[768,256]{1,0:T(8,128)(2,1)S(1)}, u32[]{:S(2)}, u32[]{:S(2)}) collective-permute-start(bf16[768,256]{1,0:T(8,128)(2,1)S(1)} %pad_maximum_fusion.37), channel_id=1, source_target_pairs={{0,4},{2,6},{4,0},{6,2},{1,5},{3,7},{5,1},{7,3},{8,12},{10,14},{12... | collective-permute-start | bytes 1179656 | tf_op jit(solution)/shard_map/ppermute | solution.py:31
  159.0 42.4 %collective-permute-start.15 = (bf16[1024,1536]{1,0:T(8,128)(2,1)}, bf16[1024,1536]{1,0:T(8,128)(2,1)}, u32[]{:S(2)}, u32[]{:S(2)}) collective-permute-start(bf16[1024,1536]{1,0:T(8,128)(2,1)} %pad_maximum_fusion.1), channel_id=1, source_target_pairs={{0,8},{8,0},{1,9},{9,1},{2,10},{10,2},{3,11},{11,3},{4,12},{12,4},... | collective-permute-start | bytes 9437192 | tf_op jit(solution)/shard_map/ppermute | solution.py:31
  160.4 86.5 %collective-permute-start.18 = (bf16[192,2048]{1,0:T(8,128)(2,1)}, bf16[192,2048]{1,0:T(8,128)(2,1)}, u32[]{:S(2)}, u32[]{:S(2)}) collective-permute-start(bf16[192,2048]{1,0:T(8,128)(2,1)} %get-tuple-element.564), channel_id=1, source_target_pairs={{0,1},{1,0},{2,3},{3,2},{4,5},{5,4},{6,7},{7,6},{8,9},{9,8},{10,11... | collective-permute-start | bytes 2359304 | tf_op jit(solution)/shard_map/ppermute | solution.py:31
  161.9 85.0 %collective-permute-start.19 = (bf16[192,2048]{1,0:T(8,128)(2,1)}, bf16[192,2048]{1,0:T(8,128)(2,1)}, u32[]{:S(2)}, u32[]{:S(2)}) collective-permute-start(bf16[192,2048]{1,0:T(8,128)(2,1)} %get-tuple-element.563), channel_id=1, source_target_pairs={{0,16},{16,0},{1,17},{17,1},{2,18},{18,2},{3,19},{19,3},{4,20},{20... | collective-permute-start | bytes 2359304 | tf_op jit(solution)/shard_map/ppermute | solution.py:31
  248.5 372.0 %reduce-scatter.4.cloned.1.call-start = ((), (), s32[]{:S(2)}) async-start(), calls=%async_computation.5 | async-start | bytes 5242880 | tf_op jit(solution)/shard_map/reduce_scatter | solution.py:711
  290.0 70.3 %collective-permute-start.24 = (bf16[384,2048]{1,0:T(8,128)(2,1)}, bf16[384,2048]{1,0:T(8,128)(2,1)}, u32[]{:S(2)}, u32[]{:S(2)}) collective-permute-start(bf16[384,2048]{1,0:T(8,128)(2,1)} %get-tuple-element.589), channel_id=1, source_target_pairs={{0,16},{16,0},{1,17},{17,1},{2,18},{18,2},{3,19},{19,3},{4,20},{20... | collective-permute-start | bytes 4718600 | tf_op jit(solution)/shard_map/ppermute | solution.py:31
  290.4 70.0 %collective-permute-start.25 = (bf16[384,2048]{1,0:T(8,128)(2,1)}, bf16[384,2048]{1,0:T(8,128)(2,1)}, u32[]{:S(2)}, u32[]{:S(2)}) collective-permute-start(bf16[384,2048]{1,0:T(8,128)(2,1)} %get-tuple-element.590), channel_id=1, source_target_pairs={{0,1},{1,0},{2,3},{3,2},{4,5},{5,4},{6,7},{7,6},{8,9},{9,8},{10,11... | collective-permute-start | bytes 4718600 | tf_op jit(solution)/shard_map/ppermute | solution.py:31
  362.8 37.0 %collective-permute-start.30 = (bf16[384,2048]{1,0:T(8,128)(2,1)}, bf16[384,2048]{1,0:T(8,128)(2,1)S(1)}, u32[]{:S(2)}, u32[]{:S(2)}) collective-permute-start(bf16[384,2048]{1,0:T(8,128)(2,1)} %get-tuple-element.587), channel_id=1, source_target_pairs={{0,16},{16,0},{1,17},{17,1},{2,18},{18,2},{3,19},{19,3},{4,20},{20... | collective-permute-start | bytes 4718600 | tf_op jit(solution)/shard_map/ppermute | solution.py:31
  364.3 36.5 %collective-permute-start.31 = (bf16[384,2048]{1,0:T(8,128)(2,1)S(1)}, bf16[384,2048]{1,0:T(8,128)(2,1)S(1)}, u32[]{:S(2)}, u32[]{:S(2)}) collective-permute-start(bf16[384,2048]{1,0:T(8,128)(2,1)S(1)} %copy-done.75), channel_id=1, source_target_pairs={{0,1},{1,0},{2,3},{3,2},{4,5},{5,4},{6,7},{7,6},{8,9},{9,8},{10,11... | collective-permute-start | bytes 4718600 | tf_op jit(solution)/shard_map/ppermute | solution.py:31
  458.8 36.8 %collective-permute-start.34 = (bf16[384,2048]{1,0:T(8,128)(2,1)}, bf16[384,2048]{1,0:T(8,128)(2,1)}, u32[]{:S(2)}, u32[]{:S(2)}) collective-permute-start(bf16[384,2048]{1,0:T(8,128)(2,1)} %get-tuple-element.536), channel_id=1, source_target_pairs={{0,16},{16,0},{1,17},{17,1},{2,18},{18,2},{3,19},{19,3},{4,20},{20... | collective-permute-start | bytes 4718600 | tf_op jit(solution)/shard_map/ppermute | solution.py:31
  459.3 36.4 %collective-permute-start.35 = (bf16[384,2048]{1,0:T(8,128)(2,1)}, bf16[384,2048]{1,0:T(8,128)(2,1)S(1)}, u32[]{:S(2)}, u32[]{:S(2)}) collective-permute-start(bf16[384,2048]{1,0:T(8,128)(2,1)} %get-tuple-element.535), channel_id=1, source_target_pairs={{0,1},{1,0},{2,3},{3,2},{4,5},{5,4},{6,7},{7,6},{8,9},{9,8},{10,11... | collective-permute-start | bytes 4718600 | tf_op jit(solution)/shard_map/ppermute | solution.py:31
  531.6 291.1 %reduce-scatter.6.cloned.1.call-start = ((), (), s32[]{:S(2)}) async-start(), calls=%async_computation.6 | async-start | bytes 5242880 | tf_op jit(solution)/shard_map/reduce_scatter | solution.py:711
  553.2 37.0 %collective-permute-start.41 = (bf16[384,2048]{1,0:T(8,128)(2,1)}, bf16[384,2048]{1,0:T(8,128)(2,1)S(1)}, u32[]{:S(2)}, u32[]{:S(2)}) collective-permute-start(bf16[384,2048]{1,0:T(8,128)(2,1)} %get-tuple-element.532), channel_id=1, source_target_pairs={{0,16},{16,0},{1,17},{17,1},{2,18},{18,2},{3,19},{19,3},{4,20},{20... | collective-permute-start | bytes 4718600 | tf_op jit(solution)/shard_map/ppermute | solution.py:31
  553.9 36.7 %collective-permute-start.42 = (bf16[384,2048]{1,0:T(8,128)(2,1)}, bf16[384,2048]{1,0:T(8,128)(2,1)S(1)}, u32[]{:S(2)}, u32[]{:S(2)}) collective-permute-start(bf16[384,2048]{1,0:T(8,128)(2,1)} %get-tuple-element.531), channel_id=1, source_target_pairs={{0,1},{1,0},{2,3},{3,2},{4,5},{5,4},{6,7},{7,6},{8,9},{9,8},{10,11... | collective-permute-start | bytes 4718600 | tf_op jit(solution)/shard_map/ppermute | solution.py:31
  722.4 207.4 %reduce-scatter.8.cloned.1.call-start = ((), (), s32[]{:S(2)}) async-start(), calls=%async_computation.7 | async-start | bytes 5242880 | tf_op jit(solution)/shard_map/reduce_scatter | solution.py:711
  824.6 44.9 %collective-permute-start.66 = (bf16[192,2048]{1,0:T(8,128)(2,1)S(1)}, bf16[192,2048]{1,0:T(8,128)(2,1)S(1)}, u32[]{:S(2)}, u32[]{:S(2)}) collective-permute-start(bf16[192,2048]{1,0:T(8,128)(2,1)S(1)} %get-tuple-element.425), channel_id=1, source_target_pairs={{0,1},{1,0},{2,3},{3,2},{4,5},{5,4},{6,7},{7,6},{8,9},{9,8},{10,11... | collective-permute-start | bytes 2359304 | tf_op jit(solution)/shard_map/ppermute | solution.py:31
  826.0 43.5 %collective-permute-start.67 = (bf16[192,2048]{1,0:T(8,128)(2,1)S(1)}, bf16[192,2048]{1,0:T(8,128)(2,1)S(1)}, u32[]{:S(2)}, u32[]{:S(2)}) collective-permute-start(bf16[192,2048]{1,0:T(8,128)(2,1)S(1)} %get-tuple-element.426), channel_id=1, source_target_pairs={{0,16},{16,0},{1,17},{17,1},{2,18},{18,2},{3,19},{19,3},{4,20},{20... | collective-permute-start | bytes 2359304 | tf_op jit(solution)/shard_map/ppermute | solution.py:31
  827.9 41.5 %collective-permute-start.68 = (bf16[768,256]{1,0:T(8,128)(2,1)S(1)}, bf16[768,256]{1,0:T(8,128)(2,1)S(1)}, u32[]{:S(2)}, u32[]{:S(2)}) collective-permute-start(bf16[768,256]{1,0:T(8,128)(2,1)S(1)} %slice.472), channel_id=1, source_target_pairs={{0,4},{2,6},{4,0},{6,2},{1,5},{3,7},{5,1},{7,3},{8,12},{10,14},{12... | collective-permute-start | bytes 1179656 | tf_op jit(solution)/shard_map/ppermute | solution.py:31
  869.7 41.3 %collective-permute-start.70 = (bf16[2,128,1024]{2,1,0:T(8,128)(2,1)S(1)}, bf16[2,128,1024]{2,1,0:T(8,128)(2,1)S(1)}, u32[]{:S(2)}, u32[]{:S(2)}) collective-permute-start(bf16[2,128,1024]{2,1,0:T(8,128)(2,1)S(1)} %dynamic-slice_bitcast_fusion.3), channel_id=1, source_target_pairs={{0,16},{16,0},{1,17},{17,1},{2,18},{18,2},{3,19},{19,3},{4,20},{20... | collective-permute-start | bytes 1572872 | tf_op jit(solution)/shard_map/ppermute | solution.py:31
  869.8 41.1 %collective-permute-start.69 = (bf16[336,512]{1,0:T(8,128)(2,1)S(1)}, bf16[336,512]{1,0:T(8,128)(2,1)S(1)}, u32[]{:S(2)}, u32[]{:S(2)}) collective-permute-start(bf16[336,512]{1,0:T(8,128)(2,1)S(1)} %add_convert_fusion.16), channel_id=1, source_target_pairs={{0,4},{2,6},{4,0},{6,2},{1,5},{3,7},{5,1},{7,3},{8,12},{10,14},{12... | collective-permute-start | bytes 1032200 | tf_op jit(solution)/shard_map/ppermute | solution.py:31
  (179 other events, 2128.2 us)
Sparse Core Ops, SparseCore 0:
  77.7 170.2 all-gather.2
  249.6 110.7 all-gather.4
  531.7 75.1 reduce-scatter.3
  722.5 76.1 reduce-scatter.5
  800.9 104.1 reduce-scatter.7

commit v5 on v4

--- a/solution.py
+++ b/solution.py
@@ -664,10 +664,9 @@
     out_part = from_tp(out_part, 0)
     top, bottom = grad_low[:half], grad_low[half:]
     grad_near = (swap(top, "tp"), swap(bottom, "row")) if two else (top, bottom)
-    out_low, totals, out_part, grad_near, packed, gate_up = stage(
-        out_low, totals, out_part, grad_near, packed, gate_up
-    )
+    out_low, totals, packed, gate_up = stage(out_low, totals, packed, gate_up)
     down_full = lax.all_gather(packed, "ctx", axis=1, tiled=True)
+    out_low, totals, out_part, grad_near = stage(out_low, totals, out_part, grad_near)
     out_full = join(out_part, "core", 1)
     out_flat = out_low.reshape(all_slots * HEAD_DIM, own_tokens)
     attended = dot(out_flat, out_full, (0, 0))

time: 980 us -> 986 us (level)
  transfers between devices with their start and end apart: 85 -> 85, of which waited for: 41 -> 41; matrix products, arithmetic and copies ran while one was open for 21% -> 20% of each run, Pallas kernels for 18% -> 18%
where the time goes in v5:
time: 986 us; the launch traced here: 977 us
  waiting for transfers between devices  384 us (39%)
  Pallas kernels  209 us (21%)
  other arithmetic  134 us (14%)
  local copies, waits for them, and re-layouts  100 us (10%)
  starting transfers between devices  97.3 us (10%)
  matrix products  34.4 us (3%)
  between operations  17.3 us (2%)
    ppermute x74, waiting for transfers between devices, swap(): return lax.ppermute(value, axis, [(i, i ^ bit) for i in range(size)])  300 us
    ppermute x74, starting transfers between devices, swap(): return lax.ppermute(value, axis, [(i, i ^ bit) for i in range(size)])  83.2 us
    pallas_call x2, Pallas kernels, hidden_back(): pl.pallas_call(hidden_back_kernel, grid=(count // tile,), in_specs=[tall(...  56.4 us
    pallas_call x3, Pallas kernels, weight_grad(): pl.pallas_call(weight_grad_kernel, grid=(blocks,), in_specs=[pl.BlockSpec...  56 us
    all_gather x1, waiting for transfers between devices, body(): down_full = lax.all_gather(packed, 'ctx', axis=1, tiled=True)  46.7 us
    unnamed x259, local copies, waits for them, and re-layouts  45.3 us
    pallas_call x2, Pallas kernels, forward(): pl.pallas_call(forward_kernel, grid=(count // tile,), in_specs=[tall(tile...  38.4 us
    dot_general x9, matrix products, dot(): lax.dot_general(left, right, ((contract[:1], contract[1:]), ((), ())), pr...  34.4 us
  transfers between devices with their start and end apart: 85, of which 41 were waited for; matrix products, arithmetic and copies ran while one was open for 20% of the time, Pallas kernels for 18%

profile of v5, /device:TPU:0, one launch (start us, length us, event | category | flops | bytes accessed | tf_op | source)
XLA Modules:
  0.0 976.6 jit_solution(461720713470759534)
XLA Ops:
  46.5 12.1 %collective-permute-done.6 = bf16[256,768]{1,0:T(8,128)(2,1)} collective-permute-done((bf16[256,768]{1,0:T(8,128)(2,1)}, bf16[256,768]{1,0:T(8,128)(2,1)}, u32[]{:S(2)}, u32[]{:S(2)}) %collective-permute-start.6) | collective-permute-done | bytes 393248 | tf_op jit(solution)/shard_map/ppermute | solution.py:31
  100.8 20.4 %collective-permute-start.13 = (bf16[768,256]{1,0:T(8,128)(2,1)S(1)}, bf16[768,256]{1,0:T(8,128)(2,1)S(1)}, u32[]{:S(2)}, u32[]{:S(2)}) collective-permute-start(bf16[768,256]{1,0:T(8,128)(2,1)S(1)} %pad_maximum_fusion.37), channel_id=1, source_target_pairs={{0,4},{2,6},{4,0},{6,2},{1,5},{3,7},{5,1},{7,3},{8,12},{10,14},{12... | collective-permute-start | bytes 1179656 | tf_op jit(solution)/shard_map/ppermute | solution.py:31
  125.1 30.0 %collective-permute-done.13 = bf16[768,256]{1,0:T(8,128)(2,1)S(1)} collective-permute-done((bf16[768,256]{1,0:T(8,128)(2,1)S(1)}, bf16[768,256]{1,0:T(8,128)(2,1)S(1)}, u32[]{:S(2)}, u32[]{:S(2)}) %collective-permute-start.13) | collective-permute-done | bytes 393248 | tf_op jit(solution)/shard_map/ppermute | solution.py:31
  169.8 21.2 %collective-permute-done.14 = bf16[640,384]{1,0:T(8,128)(2,1)S(1)} collective-permute-done((bf16[640,384]{1,0:T(8,128)(2,1)}, bf16[640,384]{1,0:T(8,128)(2,1)S(1)}, u32[]{:S(2)}, u32[]{:S(2)}) %collective-permute-start.14) | collective-permute-done | bytes 491552 | tf_op jit(solution)/shard_map/ppermute | solution.py:31
  226.8 16.6 %collective-permute-done.17 = bf16[768,1024]{1,0:T(8,128)(2,1)S(1)} collective-permute-done((bf16[768,1024]{1,0:T(8,128)(2,1)}, bf16[768,1024]{1,0:T(8,128)(2,1)S(1)}, u32[]{:S(2)}, u32[]{:S(2)}) %collective-permute-start.17) | collective-permute-done | bytes 1572896 | tf_op jit(solution)/shard_map/ppermute | solution.py:31
  270.6 12.6 %collective-permute-done.21 = bf16[192,2048]{1,0:T(8,128)(2,1)S(1)} collective-permute-done((bf16[192,2048]{1,0:T(8,128)(2,1)S(1)}, bf16[192,2048]{1,0:T(8,128)(2,1)S(1)}, u32[]{:S(2)}, u32[]{:S(2)}) %collective-permute-start.21) | collective-permute-done | bytes 786464 | tf_op jit(solution)/shard_map/ppermute | solution.py:31
  296.2 19.2 %forward.2 = (f32[1536,1024]{1,0:T(8,128)}, f32[1536,1024]{1,0:T(8,128)}, bf16[1536,1024]{1,0:T(8,128)(2,1)}) custom-call(bf16[1536,2048]{1,0:T(8,128)(2,1)} %constant_dynamic-update-slice_fusion.8.tokens_ref.refs_0_, bf16[8,512,1024]{2,1,0:T(8,128)(2,1)} %all-gather.3.cloned.1.call-done.gate_w.up_w, ...), custom_call_target="tpu_custom_call" | custom-call | flops 12884901888 | bytes 30408704 | tf_op jit(solution)/shard_map/forward/pallas_call | solution.py:382
  315.5 46.7 %all-gather.5.cloned.1.call-done.down_w = bf16[4,512,1024]{2,1,0:T(8,128)(2,1)} async-done(((bf16[4,128,1024]{2,1,0:T(8,128)(2,1)}), bf16[4,512,1024]{2,1,0:T(8,128)(2,1)}) %all-gather.5.cloned.1.call-update) | async-done | bytes 4194320 | tf_op jit(solution)/shard_map/all_gather | solution.py:668
  375.2 19.2 %forward.3 = (f32[1536,1024]{1,0:T(8,128)}, f32[1536,1024]{1,0:T(8,128)}, bf16[1536,1024]{1,0:T(8,128)(2,1)}) custom-call(bf16[1536,2048]{1,0:T(8,128)(2,1)} %constant_dynamic-update-slice_fusion.18.tokens_ref.refs_1_, bf16[8,512,1024]{2,1,0:T(8,128)(2,1)} %all-gather.3.cloned.1.call-done.gate_w.up_w, ...), custom_call_target="tpu_custom_call" | custom-call | flops 12884901888 | bytes 30408704 | tf_op jit(solution)/shard_map/forward/pallas_call | solution.py:382
  411.0 28.2 %hidden_back.2 = (bf16[1536,1024]{1,0:T(8,128)(2,1)}, bf16[1536,1024]{1,0:T(8,128)(2,1)}, bf16[1536,2048]{1,0:T(8,128)(2,1)}) custom-call(bf16[1536,2048]{1,0:T(8,128)(2,1)} %constant_dynamic-update-slice_fusion.21.grad_ref.refs_1_, f32[1536,1024]{1,0:T(8,128)} %get-tuple-element.293.gate_ref, f32[1536,1024]{1,0:T(8,128)} %get-tuple-element.294.up_ref, ...), custom_call_target="tpu_custom_call" | custom-call | flops 19327352832 | bytes 37748736 | tf_op jit(solution)/shard_map/hidden_back/pallas_call | solution.py:412
  441.7 11.8 %down_product.2 = bf16[1536,2048]{1,0:T(8,128)(2,1)} custom-call(bf16[1536,1024]{1,0:T(8,128)(2,1)} %get-tuple-element.334.hidden_ref.refs_3_, bf16[4,512,1024]{2,1,0:T(8,128)(2,1)} %all-gather.5.cloned.1.call-done.down_w), custom_call_target="tpu_custom_call" | custom-call | flops 6442450944 | bytes 13631488 | tf_op jit(solution)/shard_map/down_product/pallas_call | solution.py:437
  462.7 28.2 %hidden_back.3 = (bf16[1536,1024]{1,0:T(8,128)(2,1)}, bf16[1536,1024]{1,0:T(8,128)(2,1)}, bf16[1536,2048]{1,0:T(8,128)(2,1)}) custom-call(bf16[1536,2048]{1,0:T(8,128)(2,1)} %copy-done.105, f32[1536,1024]{1,0:T(8,128)} %get-tuple-element.307.gate_ref, f32[1536,1024]{1,0:T(8,128)} %get-tuple-element.308.up_ref, ...), custom_call_target="tpu_custom_call" | custom-call | flops 19327352832 | bytes 37748736 | tf_op jit(solution)/shard_map/hidden_back/pallas_call | solution.py:412
  512.1 18.6 %weight_grad.3 = bf16[4,512,1024]{2,1,0:T(8,128)(2,1)} custom-call(bf16[1536,2048]{1,0:T(8,128)(2,1)} %copy-done.105, bf16[1536,2048]{1,0:T(8,128)(2,1)} %constant_dynamic-update-slice_fusion.21.grad_ref.refs_1_, bf16[1536,1024]{1,0:T(8,128)(2,1)} %get-tuple-element.421.refs_2_.hidden_ref, bf16[1536,1024]{1,0:T(8,128)(2,1)} %get-tuple-element.334.hidden_ref.refs_3_), custom_call_target="tpu_custom_call" | custom-call | flops 12884901888 | bytes 18874368 | tf_op jit(solution)/shard_map/weight_grad/pallas_call | solution.py:340
  556.4 12.2 %attend_back.1 = (f32[24,64,384]{2,1,0:T(8,128)S(1)}, bf16[8,2,320,384]{3,2,1,0:T(8,128)(2,1)}) custom-call(s32[2,8]{1,0:T(2,128)S(1)} %copy-done.27, s32[2]{0:T(128)S(1)} %copy-done.29, s32[8]{0:T(128)S(1)} %copy-done.33, s32[20]{0:T(128)S(1)} %copy-done.31, bf16[24,64,384]{2,1,0:T(8,128)(2,1)S(1)} %copy-done.15, bf16[24,64,384]{2,1,0:T(8,128)(2,1)S(1)} %bitcast.227, ...), custom_call_target="tpu_custom_call" | custom-call | flops 30198988800 | bytes 16777216 | tf_op jit(solution)/shard_map/attend_back/pallas_call | solution.py:178
  573.8 18.2 %collective-permute-done.41 = bf16[384,2048]{1,0:T(8,128)(2,1)S(1)} collective-permute-done((bf16[384,2048]{1,0:T(8,128)(2,1)}, bf16[384,2048]{1,0:T(8,128)(2,1)S(1)}, u32[]{:S(2)}, u32[]{:S(2)}) %collective-permute-start.41) | collective-permute-done | bytes 1572896 | tf_op jit(solution)/shard_map/ppermute | solution.py:31
  597.4 18.8 %weight_grad.4 = bf16[4,512,1024]{2,1,0:T(8,128)(2,1)} custom-call(bf16[1536,2048]{1,0:T(8,128)(2,1)} %constant_dynamic-update-slice_fusion.8.tokens_ref.refs_0_, bf16[1536,2048]{1,0:T(8,128)(2,1)} %constant_dynamic-update-slice_fusion.18.tokens_ref.refs_1_, bf16[1536,1024]{1,0:T(8,128)(2,1)} %get-tuple-element.356.refs_2_, ...), custom_call_target="tpu_custom_call" | custom-call | flops 12884901888 | bytes 18874368 | tf_op jit(solution)/shard_map/weight_grad/pallas_call | solution.py:340
  660.3 16.3 %collective-permute-done.50 = bf16[640,384]{1,0:T(8,128)(2,1)} collective-permute-done((bf16[640,384]{1,0:T(8,128)(2,1)}, bf16[640,384]{1,0:T(8,128)(2,1)}, u32[]{:S(2)}, u32[]{:S(2)}) %collective-permute-start.50) | collective-permute-done | bytes 491552 | tf_op jit(solution)/shard_map/ppermute | solution.py:765
  703.3 12.7 %collective-permute-done.53 = bf16[640,384]{1,0:T(8,128)(2,1)S(1)} collective-permute-done((bf16[640,384]{1,0:T(8,128)(2,1)}, bf16[640,384]{1,0:T(8,128)(2,1)S(1)}, u32[]{:S(2)}, u32[]{:S(2)}) %collective-permute-start.53) | collective-permute-done | bytes 491552 | tf_op jit(solution)/shard_map/ppermute | solution.py:765
  764.8 18.6 %weight_grad.5 = bf16[4,512,1024]{2,1,0:T(8,128)(2,1)} custom-call(bf16[1536,2048]{1,0:T(8,128)(2,1)} %constant_dynamic-update-slice_fusion.8.tokens_ref.refs_0_, bf16[1536,2048]{1,0:T(8,128)(2,1)} %constant_dynamic-update-slice_fusion.18.tokens_ref.refs_1_, bf16[1536,1024]{1,0:T(8,128)(2,1)} %get-tuple-element.417.refs_2_, ...), custom_call_target="tpu_custom_call" | custom-call | flops 12884901888 | bytes 18874368 | tf_op jit(solution)/shard_map/weight_grad/pallas_call | solution.py:340
  787.1 11.6 %down_product.3 = bf16[1536,2048]{1,0:T(8,128)(2,1)} custom-call(bf16[1536,1024]{1,0:T(8,128)(2,1)} %get-tuple-element.421.refs_2_.hidden_ref, bf16[4,512,1024]{2,1,0:T(8,128)(2,1)} %all-gather.5.cloned.1.call-done.down_w), custom_call_target="tpu_custom_call" | custom-call | flops 6442450944 | bytes 13631488 | tf_op jit(solution)/shard_map/down_product/pallas_call | solution.py:437
  830.4 26.9 %collective-permute-done.65 = bf16[336,512]{1,0:T(8,128)(2,1)S(1)} collective-permute-done((bf16[336,512]{1,0:T(8,128)(2,1)S(1)}, bf16[336,512]{1,0:T(8,128)(2,1)S(1)}, u32[]{:S(2)}, u32[]{:S(2)}) %collective-permute-start.65) | collective-permute-done | bytes 344096 | tf_op jit(solution)/shard_map/ppermute | solution.py:31
  875.9 10.9 %collective-permute-done.71 = bf16[768,128]{1,0:T(8,128)(2,1)S(1)} collective-permute-done((bf16[768,128]{1,0:T(8,128)(2,1)S(1)}, bf16[768,128]{1,0:T(8,128)(2,1)S(1)}, u32[]{:S(2)}, u32[]{:S(2)}) %collective-permute-start.71) | collective-permute-done | bytes 196640 | tf_op jit(solution)/shard_map/ppermute | solution.py:31
  887.5 19.9 %collective-permute-done.69 = bf16[336,512]{1,0:T(8,128)(2,1)S(1)} collective-permute-done((bf16[336,512]{1,0:T(8,128)(2,1)S(1)}, bf16[336,512]{1,0:T(8,128)(2,1)S(1)}, u32[]{:S(2)}, u32[]{:S(2)}) %collective-permute-start.69) | collective-permute-done | bytes 344096 | tf_op jit(solution)/shard_map/ppermute | solution.py:31
  915.8 12.2 %collective-permute-done.73 = bf16[256,768]{1,0:T(8,128)(2,1)S(1)} collective-permute-done((bf16[256,768]{1,0:T(8,128)(2,1)S(1)}, bf16[256,768]{1,0:T(8,128)(2,1)S(1)}, u32[]{:S(2)}, u32[]{:S(2)}) %collective-permute-start.73) | collective-permute-done | bytes 393248 | tf_op jit(solution)/shard_map/ppermute | solution.py:31
  (637 shorter events, 496.0 us)
Async XLA Ops:
  7.2 240.8 %all-gather.3.cloned.1.call-start = ((), (), s32[]{:S(2)}) async-start(), calls=%async_computation.3 | async-start | bytes 10485760 | tf_op jit(solution)/shard_map/all_gather | solution.py:642
  36.3 36.8 %collective-permute-start.3 = (bf16[2,384,1024]{2,1,0:T(8,128)(2,1)}, bf16[2,384,1024]{2,1,0:T(8,128)(2,1)}, u32[]{:S(2)}, u32[]{:S(2)}) collective-permute-start(bf16[2,384,1024]{2,1,0:T(8,128)(2,1)} %pad_maximum_fusion.15), channel_id=1, source_target_pairs={{0,16},{16,0},{1,17},{17,1},{2,18},{18,2},{3,19},{19,3},{4,20},{20... | collective-permute-start | bytes 4718600 | tf_op jit(solution)/shard_map/ppermute | solution.py:31
  77.6 284.6 %all-gather.5.cloned.1.call-start = ((), (), s32[]{:S(2)}) async-start(), calls=%async_computation.4 | async-start | bytes 5242880 | tf_op jit(solution)/shard_map/all_gather | solution.py:668
  100.8 56.3 %collective-permute-start.12 = (bf16[1024,768]{1,0:T(8,128)(2,1)S(1)}, bf16[1024,768]{1,0:T(8,128)(2,1)S(1)}, u32[]{:S(2)}, u32[]{:S(2)}) collective-permute-start(bf16[1024,768]{1,0:T(8,128)(2,1)S(1)} %pad_maximum_fusion.16), channel_id=1, source_target_pairs={{0,1},{1,0},{2,3},{3,2},{4,5},{5,4},{6,7},{7,6},{8,9},{9,8},{10,11... | collective-permute-start | bytes 4718600 | tf_op jit(solution)/shard_map/ppermute | solution.py:31
  100.8 54.3 %collective-permute-start.13 = (bf16[768,256]{1,0:T(8,128)(2,1)S(1)}, bf16[768,256]{1,0:T(8,128)(2,1)S(1)}, u32[]{:S(2)}, u32[]{:S(2)}) collective-permute-start(bf16[768,256]{1,0:T(8,128)(2,1)S(1)} %pad_maximum_fusion.37), channel_id=1, source_target_pairs={{0,4},{2,6},{4,0},{6,2},{1,5},{3,7},{5,1},{7,3},{8,12},{10,14},{12... | collective-permute-start | bytes 1179656 | tf_op jit(solution)/shard_map/ppermute | solution.py:31
  159.0 42.4 %collective-permute-start.15 = (bf16[1024,1536]{1,0:T(8,128)(2,1)}, bf16[1024,1536]{1,0:T(8,128)(2,1)}, u32[]{:S(2)}, u32[]{:S(2)}) collective-permute-start(bf16[1024,1536]{1,0:T(8,128)(2,1)} %pad_maximum_fusion.1), channel_id=1, source_target_pairs={{0,8},{8,0},{1,9},{9,1},{2,10},{10,2},{3,11},{11,3},{4,12},{12,4},... | collective-permute-start | bytes 9437192 | tf_op jit(solution)/shard_map/ppermute | solution.py:31
  160.4 87.6 %collective-permute-start.18 = (bf16[192,2048]{1,0:T(8,128)(2,1)}, bf16[192,2048]{1,0:T(8,128)(2,1)}, u32[]{:S(2)}, u32[]{:S(2)}) collective-permute-start(bf16[192,2048]{1,0:T(8,128)(2,1)} %get-tuple-element.568), channel_id=1, source_target_pairs={{0,1},{1,0},{2,3},{3,2},{4,5},{5,4},{6,7},{7,6},{8,9},{9,8},{10,11... | collective-permute-start | bytes 2359304 | tf_op jit(solution)/shard_map/ppermute | solution.py:31
  161.9 86.1 %collective-permute-start.19 = (bf16[192,2048]{1,0:T(8,128)(2,1)}, bf16[192,2048]{1,0:T(8,128)(2,1)}, u32[]{:S(2)}, u32[]{:S(2)}) collective-permute-start(bf16[192,2048]{1,0:T(8,128)(2,1)} %get-tuple-element.567), channel_id=1, source_target_pairs={{0,16},{16,0},{1,17},{17,1},{2,18},{18,2},{3,19},{19,3},{4,20},{20... | collective-permute-start | bytes 2359304 | tf_op jit(solution)/shard_map/ppermute | solution.py:31
  248.5 373.9 %reduce-scatter.4.cloned.1.call-start = ((), (), s32[]{:S(2)}) async-start(), calls=%async_computation.5 | async-start | bytes 5242880 | tf_op jit(solution)/shard_map/reduce_scatter | solution.py:710
  289.9 72.3 %collective-permute-start.24 = (bf16[384,2048]{1,0:T(8,128)(2,1)}, bf16[384,2048]{1,0:T(8,128)(2,1)}, u32[]{:S(2)}, u32[]{:S(2)}) collective-permute-start(bf16[384,2048]{1,0:T(8,128)(2,1)} %get-tuple-element.593), channel_id=1, source_target_pairs={{0,16},{16,0},{1,17},{17,1},{2,18},{18,2},{3,19},{19,3},{4,20},{20... | collective-permute-start | bytes 4718600 | tf_op jit(solution)/shard_map/ppermute | solution.py:31
  290.3 71.9 %collective-permute-start.25 = (bf16[384,2048]{1,0:T(8,128)(2,1)}, bf16[384,2048]{1,0:T(8,128)(2,1)}, u32[]{:S(2)}, u32[]{:S(2)}) collective-permute-start(bf16[384,2048]{1,0:T(8,128)(2,1)} %get-tuple-element.594), channel_id=1, source_target_pairs={{0,1},{1,0},{2,3},{3,2},{4,5},{5,4},{6,7},{7,6},{8,9},{9,8},{10,11... | collective-permute-start | bytes 4718600 | tf_op jit(solution)/shard_map/ppermute | solution.py:31
  364.7 37.0 %collective-permute-start.30 = (bf16[384,2048]{1,0:T(8,128)(2,1)}, bf16[384,2048]{1,0:T(8,128)(2,1)S(1)}, u32[]{:S(2)}, u32[]{:S(2)}) collective-permute-start(bf16[384,2048]{1,0:T(8,128)(2,1)} %get-tuple-element.591), channel_id=1, source_target_pairs={{0,16},{16,0},{1,17},{17,1},{2,18},{18,2},{3,19},{19,3},{4,20},{20... | collective-permute-start | bytes 4718600 | tf_op jit(solution)/shard_map/ppermute | solution.py:31
  366.2 36.5 %collective-permute-start.31 = (bf16[384,2048]{1,0:T(8,128)(2,1)S(1)}, bf16[384,2048]{1,0:T(8,128)(2,1)S(1)}, u32[]{:S(2)}, u32[]{:S(2)}) collective-permute-start(bf16[384,2048]{1,0:T(8,128)(2,1)S(1)} %copy-done.75), channel_id=1, source_target_pairs={{0,1},{1,0},{2,3},{3,2},{4,5},{5,4},{6,7},{7,6},{8,9},{9,8},{10,11... | collective-permute-start | bytes 4718600 | tf_op jit(solution)/shard_map/ppermute | solution.py:31
  460.7 36.8 %collective-permute-start.34 = (bf16[384,2048]{1,0:T(8,128)(2,1)}, bf16[384,2048]{1,0:T(8,128)(2,1)}, u32[]{:S(2)}, u32[]{:S(2)}) collective-permute-start(bf16[384,2048]{1,0:T(8,128)(2,1)} %get-tuple-element.540), channel_id=1, source_target_pairs={{0,16},{16,0},{1,17},{17,1},{2,18},{18,2},{3,19},{19,3},{4,20},{20... | collective-permute-start | bytes 4718600 | tf_op jit(solution)/shard_map/ppermute | solution.py:31
  461.2 36.4 %collective-permute-start.35 = (bf16[384,2048]{1,0:T(8,128)(2,1)}, bf16[384,2048]{1,0:T(8,128)(2,1)S(1)}, u32[]{:S(2)}, u32[]{:S(2)}) collective-permute-start(bf16[384,2048]{1,0:T(8,128)(2,1)} %get-tuple-element.539), channel_id=1, source_target_pairs={{0,1},{1,0},{2,3},{3,2},{4,5},{5,4},{6,7},{7,6},{8,9},{9,8},{10,11... | collective-permute-start | bytes 4718600 | tf_op jit(solution)/shard_map/ppermute | solution.py:31
  533.5 291.7 %reduce-scatter.6.cloned.1.call-start = ((), (), s32[]{:S(2)}) async-start(), calls=%async_computation.6 | async-start | bytes 5242880 | tf_op jit(solution)/shard_map/reduce_scatter | solution.py:710
  555.0 37.0 %collective-permute-start.41 = (bf16[384,2048]{1,0:T(8,128)(2,1)}, bf16[384,2048]{1,0:T(8,128)(2,1)S(1)}, u32[]{:S(2)}, u32[]{:S(2)}) collective-permute-start(bf16[384,2048]{1,0:T(8,128)(2,1)} %get-tuple-element.536), channel_id=1, source_target_pairs={{0,16},{16,0},{1,17},{17,1},{2,18},{18,2},{3,19},{19,3},{4,20},{20... | collective-permute-start | bytes 4718600 | tf_op jit(solution)/shard_map/ppermute | solution.py:31
  555.8 36.7 %collective-permute-start.42 = (bf16[384,2048]{1,0:T(8,128)(2,1)}, bf16[384,2048]{1,0:T(8,128)(2,1)S(1)}, u32[]{:S(2)}, u32[]{:S(2)}) collective-permute-start(bf16[384,2048]{1,0:T(8,128)(2,1)} %get-tuple-element.535), channel_id=1, source_target_pairs={{0,1},{1,0},{2,3},{3,2},{4,5},{5,4},{6,7},{7,6},{8,9},{9,8},{10,11... | collective-permute-start | bytes 4718600 | tf_op jit(solution)/shard_map/ppermute | solution.py:31
  724.6 206.0 %reduce-scatter.8.cloned.1.call-start = ((), (), s32[]{:S(2)}) async-start(), calls=%async_computation.7 | async-start | bytes 5242880 | tf_op jit(solution)/shard_map/reduce_scatter | solution.py:710
  827.2 40.7 %collective-permute-start.66 = (bf16[192,2048]{1,0:T(8,128)(2,1)S(1)}, bf16[192,2048]{1,0:T(8,128)(2,1)S(1)}, u32[]{:S(2)}, u32[]{:S(2)}) collective-permute-start(bf16[192,2048]{1,0:T(8,128)(2,1)S(1)} %get-tuple-element.429), channel_id=1, source_target_pairs={{0,1},{1,0},{2,3},{3,2},{4,5},{5,4},{6,7},{7,6},{8,9},{9,8},{10,11... | collective-permute-start | bytes 2359304 | tf_op jit(solution)/shard_map/ppermute | solution.py:31
  827.5 40.4 %collective-permute-start.67 = (bf16[192,2048]{1,0:T(8,128)(2,1)S(1)}, bf16[192,2048]{1,0:T(8,128)(2,1)S(1)}, u32[]{:S(2)}, u32[]{:S(2)}) collective-permute-start(bf16[192,2048]{1,0:T(8,128)(2,1)S(1)} %get-tuple-element.430), channel_id=1, source_target_pairs={{0,16},{16,0},{1,17},{17,1},{2,18},{18,2},{3,19},{19,3},{4,20},{20... | collective-permute-start | bytes 2359304 | tf_op jit(solution)/shard_map/ppermute | solution.py:31
  828.9 38.8 %collective-permute-start.68 = (bf16[768,256]{1,0:T(8,128)(2,1)S(1)}, bf16[768,256]{1,0:T(8,128)(2,1)S(1)}, u32[]{:S(2)}, u32[]{:S(2)}) collective-permute-start(bf16[768,256]{1,0:T(8,128)(2,1)S(1)} %slice.472), channel_id=1, source_target_pairs={{0,4},{2,6},{4,0},{6,2},{1,5},{3,7},{5,1},{7,3},{8,12},{10,14},{12... | collective-permute-start | bytes 1179656 | tf_op jit(solution)/shard_map/ppermute | solution.py:31
  869.1 38.4 %collective-permute-start.70 = (bf16[2,128,1024]{2,1,0:T(8,128)(2,1)S(1)}, bf16[2,128,1024]{2,1,0:T(8,128)(2,1)S(1)}, u32[]{:S(2)}, u32[]{:S(2)}) collective-permute-start(bf16[2,128,1024]{2,1,0:T(8,128)(2,1)S(1)} %dynamic-slice_bitcast_fusion.3), channel_id=1, source_target_pairs={{0,16},{16,0},{1,17},{17,1},{2,18},{18,2},{3,19},{19,3},{4,20},{20... | collective-permute-start | bytes 1572872 | tf_op jit(solution)/shard_map/ppermute | solution.py:31
  870.1 37.3 %collective-permute-start.69 = (bf16[336,512]{1,0:T(8,128)(2,1)S(1)}, bf16[336,512]{1,0:T(8,128)(2,1)S(1)}, u32[]{:S(2)}, u32[]{:S(2)}) collective-permute-start(bf16[336,512]{1,0:T(8,128)(2,1)S(1)} %add_convert_fusion.16), channel_id=1, source_target_pairs={{0,4},{2,6},{4,0},{6,2},{1,5},{3,7},{5,1},{7,3},{8,12},{10,14},{12... | collective-permute-start | bytes 1032200 | tf_op jit(solution)/shard_map/ppermute | solution.py:31
  (179 other events, 2123.2 us)
Sparse Core Ops, SparseCore 0:
  77.7 170.2 all-gather.2
  249.6 112.6 all-gather.4
  533.6 75.1 reduce-scatter.3
  724.7 75.8 reduce-scatter.5
  802.7 104.1 reduce-scatter.7
